TPU v7x, 256 devices: a whole 4x4x8 slice. The times are simulated.
256 devices in a mesh: seq: 64 (over y, x_hi, z), head: 4 (over x_lo, core).
Axes of the slice: x: 4 (x_hi: 2, x_lo: 2; x = x_hi * 2 + x_lo), y: 4, z: 8, core: 2. Of those that a mesh axis runs over, the one named last changes fastest.
Arguments:
- video_query: bfloat16 [8192, 2560], P('seq', 'head'), may hold values from -1800 to 1800
- video_key: bfloat16 [8192, 2560], P('seq', 'head'), may hold values from -1800 to 1800
- video_value: bfloat16 [8192, 2560], P('seq', 'head'), may hold values from -6 to 6
- cross_query: bfloat16 [8192, 2560], P('seq', 'head'), may hold values from -1800 to 1800
- text_key: bfloat16 [512, 2560], P('seq', 'head'), may hold values from -1800 to 1800
- text_value: bfloat16 [512, 2560], P('seq', 'head'), may hold values from -6 to 6
- text_mask: int32 [512], P('seq'), may hold values from 0 to 1, as said below
- norm_gains: float32 [4, 2560], P(None, 'head'), may hold values from 0.8 to 2.5
- gate_table: float32 [1000, 2560], P(None, 'head'), may hold values from -4 to 4
- timestep: int32 [1], replicated, may hold values from 0 to 999
Outputs:
- block_update: bfloat16 [8192, 2560], P('seq', 'head')
Inputs may be any that keep to these rules, and one draw needn't show every extreme that they name: `text_mask`: the ones form a prefix of at least 64 positions, zeros follow.
All inputs are finite; a program needn't handle non-finite values.
Results may differ from a plain program's by a relative error of at most 0.0055.
The roundings to bfloat16 on the way count: a program that leaves them out, or rounds other values in their place, can miss the bound.
Values may be sent and summed in bfloat16 or wider, within the bound.
No kernel may reach another device: no remote copies, remote signals or barrier semaphores. Data moves between devices by JAX's collectives and lax.ppermute only.
A program may use at most 128 MiB of HBM per device.

v0:
```python
import jax
import jax.numpy as jnp
from jax import lax
from jax.sharding import PartitionSpec as P

HEADS = 20
HD = 128


NEG_FILL = -1e30


def squares(matrix):
    values = matrix.astype(jnp.float32)
    return jnp.sum(values * values, axis=1)


def rescale(matrix, totals, gains_row):
    values = matrix.astype(jnp.float32)
    factor = lax.rsqrt(totals / (HEADS * HD) + 1e-06)
    return (values * factor[:, None] * gains_row).astype(jnp.bfloat16)


def empty_running(heads_dev, row_count):
    return (
        jnp.full((heads_dev, row_count), NEG_FILL, jnp.float32),
        jnp.zeros((heads_dev, row_count), jnp.float32),
        jnp.zeros((heads_dev, row_count, HD), jnp.float32),
    )


def absorb(running, query_heads, key_block, value_block, usable):
    maxima, totals, accumulated = running
    heads_dev = query_heads.shape[1]
    key_count = key_block.shape[0]
    key_heads = key_block.reshape(key_count, heads_dev, HD)
    value_heads = value_block.reshape(key_count, heads_dev, HD)
    scores = jnp.einsum(
        "qhd,khd->hqk", query_heads, key_heads, preferred_element_type=jnp.float32
    ) * HD ** (-0.5)
    if usable is not None:
        scores = jnp.where(usable[None, None, :], scores, NEG_FILL)
    new_max = jnp.maximum(maxima, jnp.max(scores, axis=2))
    weights = jnp.exp(scores - new_max[:, :, None])
    if usable is not None:
        weights = jnp.where(usable[None, None, :], weights, 0.0)
    totals = jnp.sum(weights, axis=2)
    accumulated = jnp.einsum(
        "hqk,khd->hqd",
        weights.astype(jnp.bfloat16),
        value_heads,
        preferred_element_type=jnp.float32,
    )
    return (new_max, totals, accumulated)


def finish(running):
    maxima, totals, accumulated = running
    result = accumulated / totals[:, :, None]
    return result.transpose(1, 0, 2).reshape(result.shape[1], -1)


def local(
    video_query,
    video_key,
    video_value,
    cross_query,
    text_key,
    text_value,
    text_mask,
    norm_gains,
    gate_table,
    timestep,
):
    row_count = video_query.shape[0]
    columns = video_query.shape[1]
    heads_dev = columns // HD
    norm_sums = lax.psum(
        (squares(video_query), squares(video_key), squares(cross_query), squares(text_key)), "head"
    )
    query_norm = rescale(video_query, norm_sums[0], norm_gains[0])
    key_norm = rescale(video_key, norm_sums[1], norm_gains[1])
    cross_norm = rescale(cross_query, norm_sums[2], norm_gains[2])
    text_norm = rescale(text_key, norm_sums[3], norm_gains[3])
    query_heads = query_norm.reshape(row_count, heads_dev, HD)
    cross_heads = cross_norm.reshape(row_count, heads_dev, HD)
    self_running = absorb(
        empty_running(heads_dev, row_count),
        query_heads,
        lax.all_gather(key_norm, "seq", axis=0, tiled=True),
        lax.all_gather(video_value, "seq", axis=0, tiled=True),
        None,
    )
    text_flags = text_mask.astype(jnp.bfloat16)
    text_whole, tvalue_whole, flags_whole = (
        lax.all_gather(text_norm, "seq", axis=0, tiled=True),
        lax.all_gather(text_value, "seq", axis=0, tiled=True),
        lax.all_gather(text_flags, "seq", axis=0, tiled=True),
    )
    cross_running = absorb(
        empty_running(heads_dev, row_count), cross_heads, text_whole, tvalue_whole, flags_whole > 0
    )
    gating = lax.dynamic_slice_in_dim(gate_table, timestep[0], 1, 0)[0]
    combined = gating * finish(self_running) + finish(cross_running)
    return combined.astype(jnp.bfloat16)


def solution(mesh):
    placed = (
        P("seq", "head"),
        P("seq", "head"),
        P("seq", "head"),
        P("seq", "head"),
        P("seq", "head"),
        P("seq", "head"),
        P("seq"),
        P(None, "head"),
        P(None, "head"),
        P(),
    )
    return jax.shard_map(
        local, mesh=mesh, in_specs=placed, out_specs=P("seq", "head"), check_vma=False
    )
```

profile of v0, /device:TPU:2, one launch (start us, length us, event | category | flops | bytes accessed | tf_op | source)
XLA Modules:
  0.0 659.2 jit_solution(11061498055427171203)
XLA Ops:
  6.5 0.0 copy-start
  6.5 0.0 all-gather.3.cloned.1.call-start
  6.5 1.2 copy.32
  7.8 0.1 fusion.20
  7.9 1.1 copy.33
  8.9 0.1 fusion.23
  9.1 1.1 copy.38
  10.1 0.1 fusion.26
  10.2 0.8 fusion.29
  11.1 0.9 slice_reduce_fusion.2
  11.9 6.4 all-reduce.1
  18.3 0.8 fusion.25
  19.1 0.0 all-gather.3.cloned.1.call-update
  19.2 0.0 all-gather.5.cloned.1.call-start
  19.2 0.7 all-gather.5.cloned.1.call-update
  19.9 0.8 fusion.31
  20.7 199.9 %all_gather.18 = bf16[512,640]{1,0:T(8,128)(2,1)} all-gather(bf16[8,640]{1,0:T(8,128)(2,1)S(1)} %fusion.31), channel_id=1, replica_groups=mesh['seq'=64,'head'=4] {'seq'}, dimensions={0}, use_global_device_ids=true | all-gather | bytes 665600 | tf_op jit(solution)/shard_map/all_gather | solution.py:96
  220.6 1.3 copy.39
  221.9 1.2 convert_element_type.45
  223.2 189.4 %all_gather.19 = bf16[512,640]{1,0:T(8,128)(2,1)} all-gather(bf16[8,640]{1,0:T(8,128)(2,1)} %param.15), channel_id=1, replica_groups=mesh['seq'=64,'head'=4] {'seq'}, dimensions={0}, use_global_device_ids=true | all-gather | bytes 665600 | tf_op jit(solution)/shard_map/all_gather | solution.py:97
  412.6 2.2 copy.42
  414.7 1.3 dynamic-slice
  416.6 0.9 dynamic-update-slice
  417.5 179.0 %all-reduce = bf16[512]{0:T(512)(128)(2,1)} all-reduce(bf16[512]{0:T(512)(128)(2,1)S(1)} %dynamic-update-slice), channel_id=1, replica_groups=mesh['seq'=64,'head'=4] {'seq'}, use_global_device_ids=true, to_apply=%add | all-reduce | flops 512 | bytes 2048
  596.5 0.6 broadcast_compare_fusion
  597.2 0.6 add_rsqrt_fusion.1
  597.8 0.2 fusion.28
  598.0 0.5 fusion.34
  598.4 0.4 fusion.11
  598.9 1.6 fusion.7
  600.4 0.2 copy.43
  601.3 0.0 copy-done
  601.3 0.2 fusion.22
  601.5 0.0 all-gather.3.cloned.1.call-done
  601.5 13.9 %multiply_reduce_fusion = (f32[5,128]{1,0:T(8,128)S(1)}, f32[5,128,8192]{2,1,0:T(8,128)}) fusion(bf16[128,5,128]{0,2,1:T(8,128)(2,1)S(1)} %bitcast.33, bf16[8192,5,128]{0,2,1:T(8,128)(2,1)} %bitcast.30), kind=kOutput, calls=%fused_computation.1 | convolution fusion | flops 1352662400 | bytes 31623680 | tf_op jit(solution)/shard_map/qhd,khd->hqk/dot_general | solution.py:38
  615.4 9.3 %fusion = f32[5,128]{1,0:T(8,128)S(1)} fusion(f32[5,128,8192]{2,1,0:T(8,128)} %get-tuple-element.16, f32[5,128]{1,0:T(8,128)S(1)} %broadcast_maximum_fusion.1), kind=kLoop, calls=%fused_computation.2 | loop fusion | flops 15728000 | bytes 20976640 | tf_op jit(solution)/shard_map/reduce_sum | solution.py:47
  624.7 0.0 all-gather.5.cloned.1.call-done
  624.7 14.5 %copy.36 = bf16[8192,640]{0,1:T(8,128)(2,1)} copy(bf16[8192,640]{1,0:T(8,128)(2,1)} %all-gather.5.cloned.1.call-done) | data formatting | bytes 20971520 | tf_op jit(solution)/shard_map/all_gather | solution.py:91
  639.3 12.3 %fusion.13 = f32[128,5,128]{0,2,1:T(8,128)S(1)} fusion(bf16[8192,5,128]{0,2,1:T(8,128)(2,1)} %bitcast.29, f32[5,128,8192]{2,1,0:T(8,128)} %get-tuple-element.16, f32[5,128]{1,0:T(8,128)S(1)} %broadcast_maximum_fusion.1, f32[128,5]{0,1:T(8,128)S(1)} %bitcast.37), kind=kOutput, calls=%fused_computation.15 | convolution fusion | flops 1357987840 | bytes 31790080 | tf_op jit(solution)/shard_map/hqk,khd->hqd/dot_general | solution.py:48
  651.5 0.2 copy.37
  651.7 0.7 add_convert_fusion
  (6 shorter events, 0.0 us)
Async XLA Ops:
  6.5 594.7 %copy-start = (f32[1000,640]{1,0:T(8,128)S(1)}, f32[1000,640]{1,0:T(8,128)}, u32[]{:S(2)}) copy-start(f32[1000,640]{1,0:T(8,128)} %param.18) | copy-start | bytes 7680004
  6.5 594.9 %all-gather.3.cloned.1.call-start = ((), (), s32[]{:S(2)}) async-start(), calls=%async_computation | async-start | bytes 10649600 | tf_op jit(solution)/shard_map/all_gather | solution.py:90
  19.2 605.6 %all-gather.5.cloned.1.call-start = ((), (), s32[]{:S(2)}) async-start(), calls=%async_computation.1 | async-start | bytes 10649600 | tf_op jit(solution)/shard_map/all_gather | solution.py:91
Sparse Core Ops, SparseCore 0:
  19.3 199.6 all-gather.2
  222.5 165.2 all-gather.4
where the time goes:
time: 660 us; the launch traced here: 659 us
  blocking collectives  575 us (87%)
  matrix products  28.2 us (4%)
  local copies, waits for them, and re-layouts  24.8 us (4%)
  other arithmetic  16 us (2%)
  between operations  14.8 us (2%)
    all_gather x1, blocking collectives, local(): lax.all_gather(text_norm, 'seq', axis=0, tiled=True)  200 us
    all_gather x1, blocking collectives, local(): lax.all_gather(text_value, 'seq', axis=0, tiled=True)  189 us
    unnamed x1, blocking collectives  179 us
    all_gather x1, local copies, waits for them, and re-layouts, local(): lax.all_gather(video_value, 'seq', axis=0, tiled=True)  14.5 us
    dot_general x2, matrix products, absorb(): jnp.einsum('qhd,khd->hqk', query_heads, key_heads, preferred_element_type...  14.4 us
    dot_general x2, matrix products, absorb(): jnp.einsum('hqk,khd->hqd', weights.astype(jnp.bfloat16), value_heads, pre...  13.8 us
  transfers between devices with their start and end apart: 2, of which 0 were waited for; matrix products, arithmetic and copies ran while one was open for 5% of the time, Pallas kernels for 0%

commit v1 on v0

v1 whole, which is shorter than its diff:
```python
import jax
import jax.numpy as jnp
import numpy as np
from jax import lax
from jax.experimental import pallas as pl
from jax.experimental.pallas import tpu as pltpu
from jax.sharding import Mesh, PartitionSpec as P

HEADS = 20
HD = 128
LOG2E = 1.4426950408889634
SCALE2 = HD ** (-0.5) * LOG2E
PAD_MARK = 1e30
PAD_TEST = 1e20
NEG_FILL = -1e30
ROWS = 128
COLS = 640
HPD = 5
GROUP = 8
TEXT_ROWS = 16
OUT_ROWS = COLS + 16 + COLS


def squares(matrix):
    values = matrix.astype(jnp.float32)
    return jnp.sum(values * values, axis=1)


def rescale(matrix, totals, gains_row):
    values = matrix.astype(jnp.float32)
    factor = lax.rsqrt(totals / (HEADS * HD) + 1e-06)
    return (values * factor[:, None] * gains_row).astype(jnp.bfloat16)


def shift(array, step):
    return lax.ppermute(array, "z", [(i, (i + step) % 8) for i in range(8)])


def spread(array, dy, dx):
    pairs = []
    for y in range(4):
        for x in range(2):
            pairs.append((y * 2 + x, ((y + dy) % 4) * 2 + (x + dx) % 2))
    return lax.ppermute(array, ("y", "xh"), pairs)


def dot(a, b, ca, cb):
    return lax.dot_general(a, b, (((ca,), (cb,)), ((), ())), preferred_element_type=jnp.float32)


def flash_kernel(slot_ref, *refs):
    q_refs = refs[:8]
    c_refs = refs[8:15]
    k4_ref, v4_ref = refs[15:17]
    out_ref = refs[17]
    k_s, vt_s, tk_s, tv_s = refs[18:]
    for h in range(HPD):
        cols = slice(h * HD, (h + 1) * HD)
        for n, ref in enumerate(c_refs):
            k_s[n * ROWS:(n + 1) * ROWS, :] = ref[0:ROWS, cols]
            vt_s[:, n * ROWS:(n + 1) * ROWS] = ref[ROWS:2 * ROWS, cols].T
            text = ref[2 * ROWS:2 * ROWS + TEXT_ROWS, cols].astype(jnp.float32)
            tk_s[n * 8:(n + 1) * 8, :] = text[0:8]
            tv_s[n * 8:(n + 1) * 8, :] = text[8:16]
        k_s[7 * ROWS:8 * ROWS, :] = k4_ref[:, cols]
        vt_s[:, 7 * ROWS:8 * ROWS] = v4_ref[0:ROWS, cols].T
        text = v4_ref[ROWS:ROWS + TEXT_ROWS, cols].astype(jnp.float32)
        tk_s[56:64, :] = text[0:8]
        tv_s[56:64, :] = text[8:16]
        text_k = tk_s[...].astype(jnp.bfloat16)
        text_v = tv_s[...].astype(jnp.bfloat16)
        for pair in range(4):
            q = jnp.concatenate([q_refs[2 * pair][:, cols], q_refs[2 * pair + 1][:, cols]], axis=0)
            s = dot(k_s[...], q, 1, 1)
            top = jnp.max(s, axis=0, keepdims=True)
            p = jnp.exp2((s - top) * SCALE2)
            total = jnp.sum(p, axis=0, keepdims=True)
            o = dot(vt_s[...], p.astype(jnp.bfloat16), 1, 0)
            o = (o * (1.0 / total)).astype(jnp.bfloat16)
            level = top * SCALE2 + jnp.log2(total)
            hi = level.astype(jnp.bfloat16).astype(jnp.float32)
            rest = level - hi
            mid = rest.astype(jnp.bfloat16).astype(jnp.float32)
            low = rest - mid
            for half in range(2):
                slot = slot_ref[2 * pair + half]
                lanes = slice(half * ROWS, (half + 1) * ROWS)
                out_ref[slot, h * HD:(h + 1) * HD, :] = o[:, lanes]
                stats = jnp.concatenate([hi[:, lanes], mid[:, lanes], low[:, lanes]], axis=0)
                if h == 0:
                    out_ref[slot, COLS:COLS + 16, :] = jnp.zeros((16, ROWS), jnp.bfloat16)
                out_ref[slot, COLS + 3 * h:COLS + 3 * h + 3, :] = stats.astype(jnp.bfloat16)
                base = COLS + 16 + h * HD
                out_ref[slot, base:base + 64, :] = text_k
                out_ref[slot, base + 64:base + 128, :] = text_v


def final_kernel(in_ref, qc_ref, gate_ref, out_ref):
    for h in range(HPD):
        cols = slice(h * HD, (h + 1) * HD)
        levels = []
        for j in range(GROUP):
            stats = in_ref[j, COLS:COLS + 16, :].astype(jnp.float32)[3 * h:3 * h + 3]
            levels.append(stats[0:1] + stats[1:2] + stats[2:3])
        top = levels[0]
        for level in levels[1:]:
            top = jnp.maximum(top, level)
        shares = [jnp.exp2(level - top) for level in levels]
        total = shares[0]
        for share in shares[1:]:
            total = total + share
        inverse = 1.0 / total
        own = jnp.zeros((HD, ROWS), jnp.float32)
        for j in range(GROUP):
            own = own + in_ref[j, h * HD:(h + 1) * HD, :].astype(jnp.float32) * (shares[j] * inverse)
        base = COLS + 16 + h * HD
        keys = jnp.concatenate([in_ref[j, base:base + 64, :] for j in range(GROUP)], axis=0)
        values = jnp.concatenate([in_ref[j, base + 64:base + 128, :] for j in range(GROUP)], axis=0)
        s = dot(keys, qc_ref[:, cols], 1, 1)
        real = keys[:, 0:1].astype(jnp.float32) < PAD_TEST
        s = jnp.where(real, s, NEG_FILL)
        top = jnp.max(s, axis=0, keepdims=True)
        p = jnp.where(real, jnp.exp2((s - top) * SCALE2), 0.0)
        total = jnp.sum(p, axis=0, keepdims=True)
        cross = dot(values, p.astype(jnp.bfloat16), 0, 0) * (1.0 / total)
        out_ref[:, cols] = (gate_ref[:, cols] * own.T + cross.T).astype(jnp.bfloat16)


VM = pl.BlockSpec(memory_space=pltpu.VMEM)


def local(
    video_query,
    video_key,
    video_value,
    cross_query,
    text_key,
    text_value,
    text_mask,
    norm_gains,
    gate_table,
    timestep,
):
    norm_sums = lax.psum(
        jnp.concatenate([squares(video_query), squares(video_key), squares(cross_query), squares(text_key)]),
        "head",
    )
    key_norm = rescale(video_key, norm_sums[128:256], norm_gains[1])
    text_norm = rescale(text_key, norm_sums[384:392], norm_gains[3])
    text_norm = jnp.where(text_mask[:, None] > 0, text_norm, jnp.bfloat16(PAD_MARK))
    own = jnp.concatenate([key_norm, video_value, text_norm, text_value], axis=0)
    query_norm = rescale(video_query, norm_sums[0:128], norm_gains[0])
    cross_norm = rescale(cross_query, norm_sums[256:384], norm_gains[2])

    up1, down1 = shift(own, 1), shift(own, -1)
    up2, down2 = shift(up1, 1), shift(down1, -1)
    up3, down3 = shift(up2, 1), shift(down2, -1)
    key4 = shift(up3[:ROWS], 1)
    value4 = shift(down3[ROWS:], -1)

    moves = [(0, 0), (0, 1), (1, 0), (1, 1), (2, 0), (2, 1), (3, 0), (3, 1)]
    queries = [query_norm] + [spread(query_norm, dy, dx) for dy, dx in moves[1:]]
    y, x = lax.axis_index("y"), lax.axis_index("xh")
    slots = jnp.stack([((y - dy) % 4) * 2 + (x - dx) % 2 for dy, dx in moves]).astype(jnp.int32)

    partial = pl.pallas_call(
        flash_kernel,
        out_shape=jax.ShapeDtypeStruct((GROUP, OUT_ROWS, ROWS), jnp.bfloat16),
        in_specs=[pl.BlockSpec(memory_space=pltpu.SMEM)] + [VM] * 17,
        out_specs=VM,
        scratch_shapes=[
            pltpu.VMEM((1024, HD), jnp.bfloat16),
            pltpu.VMEM((HD, 1024), jnp.bfloat16),
            pltpu.VMEM((64, HD), jnp.float32),
            pltpu.VMEM((64, HD), jnp.float32),
        ],
        compiler_params=pltpu.CompilerParams(vmem_limit_bytes=48 * 1024 * 1024),
        cost_estimate=pl.CostEstimate(flops=2700000000, bytes_accessed=8000000, transcendentals=5242880),
    )(slots, *queries, own, up1, up2, up3, down1, down2, down3, key4, value4)

    received = lax.all_to_all(partial, ("y", "xh"), 0, 0)
    gating = lax.dynamic_slice_in_dim(gate_table, timestep[0], 1, 0)
    return pl.pallas_call(
        final_kernel,
        out_shape=jax.ShapeDtypeStruct((ROWS, COLS), jnp.bfloat16),
        in_specs=[VM] * 3,
        out_specs=VM,
        compiler_params=pltpu.CompilerParams(vmem_limit_bytes=32 * 1024 * 1024),
    )(received, cross_norm, gating)


def solution(mesh):
    grid = Mesh(mesh.devices.reshape(4, 2, 8, 4), ("y", "xh", "z", "head"))
    tokens = ("y", "xh", "z")
    placed = (
        P(tokens, "head"),
        P(tokens, "head"),
        P(tokens, "head"),
        P(tokens, "head"),
        P(tokens, "head"),
        P(tokens, "head"),
        P(tokens),
        P(None, "head"),
        P(None, "head"),
        P(),
    )
    return jax.shard_map(
        local, mesh=grid, in_specs=placed, out_specs=P(tokens, "head"), check_vma=False
    )
```

time: 660 us -> 134 us (0.20)
  blocking collectives: 575 us -> 5.82 us
  waiting for transfers between devices: 0.75 us -> 47.9 us
  starting transfers between devices: 0.04 us -> 35.4 us
  matrix products: 28.2 us -> 0 us
  Pallas kernels: 0 us -> 19.9 us
  between operations: 14.8 us -> 0.77 us
  local copies, waits for them, and re-layouts: 24.8 us -> 15.8 us
  other arithmetic: 16 us -> 7.84 us
    all_gather x2 -> x0, blocking collectives: 389 us -> none  [the longest x1 200 us: local(): lax.all_gather(text_norm, 'seq', axis=0, tiled=True)]
    unnamed x1 -> x0, blocking collectives: 179 us -> none
    ppermute x0 -> x15, starting transfers between devices: none -> 30.8 us  [the longest x8 16.5 us: shift(): return lax.ppermute(array, 'z', [(i, (i + step) % 8) for i in range(8)])]
    all_to_all x0 -> x1, waiting for transfers between devices: none -> 28.6 us  [local(): received = lax.all_to_all(partial, ('y', 'xh'), 0, 0)]
    dot_general x4 -> x0, matrix products: 28.2 us -> none  [the longest x2 14.4 us: absorb(): jnp.einsum('qhd,khd->hqk', query_heads, key_heads, preferred_element_type...]
    pallas_call x0 -> x2, Pallas kernels: none -> 19.9 us  [the longest x1 16.1 us: local(): pl.pallas_call(flash_kernel, out_shape=jax.ShapeDtypeStruct((GROUP, OUT_R...]
    ppermute x0 -> x15, waiting for transfers between devices: none -> 19.3 us  [the longest x8 13.9 us: shift(): return lax.ppermute(array, 'z', [(i, (i + step) % 8) for i in range(8)])]
    all_gather x3 -> x0, local copies, waits for them, and re-layouts: 18 us -> none  [the longest x1 14.5 us: local(): lax.all_gather(video_value, 'seq', axis=0, tiled=True)]
  transfers between devices with their start and end apart: 2 -> 16, of which waited for: 0 -> 8; matrix products, arithmetic and copies ran while one was open for 5% -> 2% of each run, Pallas kernels for 0% -> 0%
where the time goes in v1:
time: 134 us; the launch traced here: 133 us
  waiting for transfers between devices  47.9 us (36%)
  starting transfers between devices  35.4 us (26%)
  Pallas kernels  19.9 us (15%)
  local copies, waits for them, and re-layouts  15.8 us (12%)
  other arithmetic  7.84 us (6%)
  blocking collectives  5.82 us (4%)
    all_to_all x1, waiting for transfers between devices, local(): received = lax.all_to_all(partial, ('y', 'xh'), 0, 0)  28.6 us
    ppermute x8, starting transfers between devices, shift(): return lax.ppermute(array, 'z', [(i, (i + step) % 8) for i in range(8)])  16.5 us
    pallas_call x1, Pallas kernels, local(): pl.pallas_call(flash_kernel, out_shape=jax.ShapeDtypeStruct((GROUP, OUT_R...  16.1 us
    ppermute x7, starting transfers between devices, spread(): return lax.ppermute(array, ('y', 'xh'), pairs)  14.2 us
    ppermute x8, waiting for transfers between devices, shift(): return lax.ppermute(array, 'z', [(i, (i + step) % 8) for i in range(8)])  13.9 us
    unnamed x40, local copies, waits for them, and re-layouts  13.4 us
    psum x1, blocking collectives, local(): lax.psum(jnp.concatenate([squares(video_query), squares(video_key), squar...  5.82 us
    ppermute x7, waiting for transfers between devices, spread(): return lax.ppermute(array, ('y', 'xh'), pairs)  5.46 us
  transfers between devices with their start and end apart: 16, of which 8 were waited for; matrix products, arithmetic and copies ran while one was open for 2% of the time, Pallas kernels for 0%

profile of v1, /device:TPU:2, one launch (start us, length us, event | category | flops | bytes accessed | tf_op | source)
XLA Modules:
  0.0 133.3 jit_solution(9523964926662102742)
XLA Ops:
  0.0 1.2 fusion.6
  1.2 0.8 fusion.9
  2.0 1.1 fusion
  3.2 5.8 %psum.7 = f32[392]{0:T(512)S(1)} all-reduce(f32[392]{0:T(512)S(1)} %pad_maximum_fusion.1), channel_id=1, replica_groups=mesh['y'=4,'xh'=2,'z'=8,'head'=4] {'head'}, use_global_device_ids=true, to_apply=%region_4.0 | all-reduce | flops 392 | bytes 3136 | tf_op jit(solution)/shard_map/psum | solution.py:144
  9.0 0.9 slice_reduce_fusion
  9.9 0.7 broadcast_compare_fusion
  10.6 1.0 fusion.5
  11.6 0.8 fusion.12
  12.4 1.0 pad_maximum_fusion.refs_8_
  13.3 6.0 %collective-permute-start.10 = (bf16[272,640]{1,0:T(8,128)(2,1)S(1)}, bf16[272,640]{1,0:T(8,128)(2,1)S(1)}, u32[]{:S(2)}, u32[]{:S(2)}) collective-permute-start(bf16[272,640]{1,0:T(8,128)(2,1)S(1)} %pad_maximum_fusion.refs_8_), channel_id=1, source_target_pairs={{0,28},{4,0},{8,4},{12,8},{16,12},{20,16},{24,20},{28,24},{1,29},{... | collective-permute-start | bytes 1044488 | tf_op jit(solution)/shard_map/ppermute | solution.py:36
  19.4 0.0 collective-permute-start.7
  19.4 7.2 %collective-permute-done.10.refs_12_ = bf16[272,640]{1,0:T(8,128)(2,1)S(1)} collective-permute-done((bf16[272,640]{1,0:T(8,128)(2,1)S(1)}, bf16[272,640]{1,0:T(8,128)(2,1)S(1)}, u32[]{:S(2)}, u32[]{:S(2)}) %collective-permute-start.10) | collective-permute-done | bytes 348192 | tf_op jit(solution)/shard_map/ppermute | solution.py:36
  26.6 3.7 %collective-permute-start.11 = (bf16[272,640]{1,0:T(8,128)(2,1)S(1)}, bf16[272,640]{1,0:T(8,128)(2,1)S(1)}, u32[]{:S(2)}, u32[]{:S(2)}) collective-permute-start(bf16[272,640]{1,0:T(8,128)(2,1)S(1)} %collective-permute-done.10.refs_12_), channel_id=1, source_target_pairs={{0,28},{4,0},{8,4},{12,8},{16,12},{20,16},{24,20},{28,24},{1,29},{... | collective-permute-start | bytes 1044488 | tf_op jit(solution)/shard_map/ppermute | solution.py:36
  30.3 0.7 copy-done.3
  31.0 0.0 collective-permute-done.7.refs_9_
  31.0 0.0 collective-permute-start.8
  31.0 0.7 copy-done.5
  31.8 4.8 %collective-permute-done.11.refs_13_ = bf16[272,640]{1,0:T(8,128)(2,1)S(1)} collective-permute-done((bf16[272,640]{1,0:T(8,128)(2,1)S(1)}, bf16[272,640]{1,0:T(8,128)(2,1)S(1)}, u32[]{:S(2)}, u32[]{:S(2)}) %collective-permute-start.11) | collective-permute-done | bytes 348192 | tf_op jit(solution)/shard_map/ppermute | solution.py:36
  36.6 3.7 %collective-permute-start.12 = (bf16[272,640]{1,0:T(8,128)(2,1)S(1)}, bf16[272,640]{1,0:T(8,128)(2,1)S(1)}, u32[]{:S(2)}, u32[]{:S(2)}) collective-permute-start(bf16[272,640]{1,0:T(8,128)(2,1)S(1)} %collective-permute-done.11.refs_13_), channel_id=1, source_target_pairs={{0,28},{4,0},{8,4},{12,8},{16,12},{20,16},{24,20},{28,24},{1,29},{... | collective-permute-start | bytes 1044488 | tf_op jit(solution)/shard_map/ppermute | solution.py:36
  40.3 0.5 collective-permute-done.8.refs_10_
  40.8 0.0 collective-permute-start.9
  40.8 1.1 fusion.2.refs_0_
  41.9 1.9 %collective-permute-start = (bf16[128,640]{1,0:T(8,128)(2,1)S(1)}, bf16[128,640]{1,0:T(8,128)(2,1)S(1)}, u32[]{:S(2)}, u32[]{:S(2)}) collective-permute-start(bf16[128,640]{1,0:T(8,128)(2,1)S(1)} %fusion.2.refs_0_), channel_id=1, source_target_pairs={{0,32},{32,0},{64,96},{96,64},{128,160},{160,128},{192,224},{224,1... | collective-permute-start | bytes 491528 | tf_op jit(solution)/shard_map/ppermute | solution.py:44
  43.8 1.6 %collective-permute-start.1 = (bf16[128,640]{1,0:T(8,128)(2,1)S(1)}, bf16[128,640]{1,0:T(8,128)(2,1)S(1)}, u32[]{:S(2)}, u32[]{:S(2)}) collective-permute-start(bf16[128,640]{1,0:T(8,128)(2,1)S(1)} %fusion.2.refs_0_), channel_id=1, source_target_pairs={{0,64},{32,96},{64,128},{96,160},{128,192},{160,224},{192,0},{224,... | collective-permute-start | bytes 491528 | tf_op jit(solution)/shard_map/ppermute | solution.py:44
  45.4 2.8 %collective-permute-start.2 = (bf16[128,640]{1,0:T(8,128)(2,1)S(1)}, bf16[128,640]{1,0:T(8,128)(2,1)S(1)}, u32[]{:S(2)}, u32[]{:S(2)}) collective-permute-start(bf16[128,640]{1,0:T(8,128)(2,1)S(1)} %fusion.2.refs_0_), channel_id=1, source_target_pairs={{0,96},{32,64},{64,160},{96,128},{128,224},{160,192},{192,32},{224... | collective-permute-start | bytes 491528 | tf_op jit(solution)/shard_map/ppermute | solution.py:44
  48.1 0.0 collective-permute-done.12.refs_14_
  48.1 1.5 %collective-permute-start.3 = (bf16[128,640]{1,0:T(8,128)(2,1)S(1)}, bf16[128,640]{1,0:T(8,128)(2,1)S(1)}, u32[]{:S(2)}, u32[]{:S(2)}) collective-permute-start(bf16[128,640]{1,0:T(8,128)(2,1)S(1)} %fusion.2.refs_0_), channel_id=1, source_target_pairs={{0,128},{32,160},{64,192},{96,224},{128,0},{160,32},{192,64},{224,... | collective-permute-start | bytes 491528 | tf_op jit(solution)/shard_map/ppermute | solution.py:44
  49.7 0.7 slice.41
  50.4 0.0 collective-permute-done.9.refs_11_
  50.4 3.1 %collective-permute-start.14 = (bf16[144,640]{1,0:T(8,128)(2,1)}, bf16[144,640]{1,0:T(8,128)(2,1)}, u32[]{:S(2)}, u32[]{:S(2)}) collective-permute-start(bf16[144,640]{1,0:T(8,128)(2,1)} %slice.41), channel_id=1, source_target_pairs={{0,28},{4,0},{8,4},{12,8},{16,12},{20,16},{24,20},{28,24},{1,29},{... | collective-permute-start | bytes 552968 | tf_op jit(solution)/shard_map/ppermute | solution.py:36
  53.5 0.7 slice.40
  54.2 0.7 copy-done.1
  54.9 0.0 collective-permute-done.refs_1_
  54.9 0.7 copy-done.11
  55.6 3.2 %collective-permute-start.4 = (bf16[128,640]{1,0:T(8,128)(2,1)S(1)}, bf16[128,640]{1,0:T(8,128)(2,1)}, u32[]{:S(2)}, u32[]{:S(2)}) collective-permute-start(bf16[128,640]{1,0:T(8,128)(2,1)S(1)} %fusion.2.refs_0_), channel_id=1, source_target_pairs={{0,160},{32,128},{64,224},{96,192},{128,32},{160,0},{192,96},{224,... | collective-permute-start | bytes 491528 | tf_op jit(solution)/shard_map/ppermute | solution.py:44
  58.8 0.0 collective-permute-done.1.refs_2_
  58.8 0.7 copy-done.13
  59.4 1.7 %collective-permute-start.5 = (bf16[128,640]{1,0:T(8,128)(2,1)S(1)}, bf16[128,640]{1,0:T(8,128)(2,1)}, u32[]{:S(2)}, u32[]{:S(2)}) collective-permute-start(bf16[128,640]{1,0:T(8,128)(2,1)S(1)} %fusion.2.refs_0_), channel_id=1, source_target_pairs={{0,192},{32,224},{64,0},{96,32},{128,64},{160,96},{192,128},{224,1... | collective-permute-start | bytes 491528 | tf_op jit(solution)/shard_map/ppermute | solution.py:44
  61.1 0.0 collective-permute-done.2.refs_3_
  61.1 0.7 copy-done.15
  61.8 1.6 %collective-permute-start.6 = (bf16[128,640]{1,0:T(8,128)(2,1)S(1)}, bf16[128,640]{1,0:T(8,128)(2,1)}, u32[]{:S(2)}, u32[]{:S(2)}) collective-permute-start(bf16[128,640]{1,0:T(8,128)(2,1)S(1)} %fusion.2.refs_0_), channel_id=1, source_target_pairs={{0,224},{32,192},{64,32},{96,0},{128,96},{160,64},{192,160},{224,1... | collective-permute-start | bytes 491528 | tf_op jit(solution)/shard_map/ppermute | solution.py:44
  63.4 0.0 collective-permute-done.3.refs_4_
  63.4 0.7 copy-done.17
  64.1 0.0 collective-permute-start.13
  64.1 0.1 stack.35.slot_ref
  64.1 1.6 %collective-permute-done.4.refs_5_ = bf16[128,640]{1,0:T(8,128)(2,1)} collective-permute-done((bf16[128,640]{1,0:T(8,128)(2,1)S(1)}, bf16[128,640]{1,0:T(8,128)(2,1)}, u32[]{:S(2)}, u32[]{:S(2)}) %collective-permute-start.4) | collective-permute-done | bytes 163872 | tf_op jit(solution)/shard_map/ppermute | solution.py:44
  65.8 1.3 %collective-permute-done.5.refs_6_ = bf16[128,640]{1,0:T(8,128)(2,1)} collective-permute-done((bf16[128,640]{1,0:T(8,128)(2,1)S(1)}, bf16[128,640]{1,0:T(8,128)(2,1)}, u32[]{:S(2)}, u32[]{:S(2)}) %collective-permute-start.5) | collective-permute-done | bytes 163872 | tf_op jit(solution)/shard_map/ppermute | solution.py:44
  67.1 2.5 %collective-permute-done.6.refs_7_ = bf16[128,640]{1,0:T(8,128)(2,1)} collective-permute-done((bf16[128,640]{1,0:T(8,128)(2,1)S(1)}, bf16[128,640]{1,0:T(8,128)(2,1)}, u32[]{:S(2)}, u32[]{:S(2)}) %collective-permute-start.6) | collective-permute-done | bytes 163872 | tf_op jit(solution)/shard_map/ppermute | solution.py:44
  69.6 1.3 collective-permute-done.13.refs_15_
  70.9 0.0 collective-permute-done.14.refs_16_
  70.9 1.0 copy-done.2
  71.9 1.0 copy-done.4
  72.9 1.0 copy-done.6
  73.8 1.0 copy-done.8
  74.8 1.0 copy-done.10
  75.8 0.9 copy-done.12
  76.7 0.9 copy-done.14
  77.6 0.9 copy-done.16
  78.6 0.9 copy-done.18
  79.5 16.1 %shard_map.100 = bf16[8,1296,128]{2,1,0:T(8,128)(2,1)} custom-call(s32[8]{0:T(128)S(1)} %stack.35.slot_ref, bf16[128,640]{1,0:T(8,128)(2,1)S(1)} %fusion.2.refs_0_, bf16[128,640]{1,0:T(8,128)(2,1)S(1)} %copy-done.12, bf16[128,640]{1,0:T(8,128)(2,1)S(1)} %copy-done.14, bf16[128,640]{1,0:T(8,128)(2,1)S(1)} %copy-done.16, bf16[128,640]{1,0:T(8,128)(2,1)S(1)} %copy-done.18, ...), custom_call_target="tpu_custom_call" | custom-call | flops 2700000000 | bytes 8000000 | tf_op jit(solution)/shard_map/pallas_call | solution.py:166
  95.6 4.6 %all-to-all-start = ((bf16[8,1296,128]{2,1,0:T(8,128)(2,1)}), bf16[8,1296,128]{2,1,0:T(8,128)(2,1)}, u32[]{:S(2)}, u32[]{:S(2)}) async-start(bf16[8,1296,128]{2,1,0:T(8,128)(2,1)} %shard_map.100), calls=%async_computation | async-start | bytes 5308416 | tf_op jit(solution)/shard_map/all_to_all | solution.py:181
  100.9 0.1 fusion.8.qc_ref
  101.0 28.6 %all-to-all-done.in_ref = bf16[8,1296,128]{2,1,0:T(8,128)(2,1)} async-done(((bf16[8,1296,128]{2,1,0:T(8,128)(2,1)}), bf16[8,1296,128]{2,1,0:T(8,128)(2,1)}, u32[]{:S(2)}, u32[]{:S(2)}) %all-to-all-start) | async-done | bytes 2654240 | tf_op jit(solution)/shard_map/all_to_all | solution.py:181
  129.6 3.7 %shard_map.101 = bf16[128,640]{1,0:T(8,128)(2,1)} custom-call(bf16[8,1296,128]{2,1,0:T(8,128)(2,1)} %all-to-all-done.in_ref, bf16[128,640]{1,0:T(8,128)(2,1)S(1)} %fusion.8.qc_ref, f32[1,640]{1,0:T(1,128)S(1)} %constant_dynamic-slice_fusion.gate_ref), custom_call_target="tpu_custom_call" | custom-call | tf_op jit(solution)/shard_map/pallas_call | solution.py:183
  (28 shorter events, 0.1 us)
Async XLA Ops:
  0.0 100.9 %copy-start = (f32[1000,640]{1,0:T(8,128)S(1)}, f32[1000,640]{1,0:T(8,128)}, u32[]{:S(2)}) copy-start(f32[1000,640]{1,0:T(8,128)} %param.18) | copy-start | bytes 7680004
  13.3 13.2 %collective-permute-start.10 = (bf16[272,640]{1,0:T(8,128)(2,1)S(1)}, bf16[272,640]{1,0:T(8,128)(2,1)S(1)}, u32[]{:S(2)}, u32[]{:S(2)}) collective-permute-start(bf16[272,640]{1,0:T(8,128)(2,1)S(1)} %pad_maximum_fusion.refs_8_), channel_id=1, source_target_pairs={{0,28},{4,0},{8,4},{12,8},{16,12},{20,16},{24,20},{28,24},{1,29},{... | collective-permute-start | bytes 1044488 | tf_op jit(solution)/shard_map/ppermute | solution.py:36
  19.4 11.7 %collective-permute-start.7 = (bf16[272,640]{1,0:T(8,128)(2,1)S(1)}, bf16[272,640]{1,0:T(8,128)(2,1)S(1)}, u32[]{:S(2)}, u32[]{:S(2)}) collective-permute-start(bf16[272,640]{1,0:T(8,128)(2,1)S(1)} %pad_maximum_fusion.refs_8_), channel_id=1, source_target_pairs={{0,4},{4,8},{8,12},{12,16},{16,20},{20,24},{24,28},{28,0},{1,5},{5... | collective-permute-start | bytes 1044488 | tf_op jit(solution)/shard_map/ppermute | solution.py:36
  26.6 10.0 %collective-permute-start.11 = (bf16[272,640]{1,0:T(8,128)(2,1)S(1)}, bf16[272,640]{1,0:T(8,128)(2,1)S(1)}, u32[]{:S(2)}, u32[]{:S(2)}) collective-permute-start(bf16[272,640]{1,0:T(8,128)(2,1)S(1)} %collective-permute-done.10.refs_12_), channel_id=1, source_target_pairs={{0,28},{4,0},{8,4},{12,8},{16,12},{20,16},{24,20},{28,24},{1,29},{... | collective-permute-start | bytes 1044488 | tf_op jit(solution)/shard_map/ppermute | solution.py:36
  30.3 0.7 copy-start.3
  31.0 9.7 %collective-permute-start.8 = (bf16[272,640]{1,0:T(8,128)(2,1)S(1)}, bf16[272,640]{1,0:T(8,128)(2,1)S(1)}, u32[]{:S(2)}, u32[]{:S(2)}) collective-permute-start(bf16[272,640]{1,0:T(8,128)(2,1)S(1)} %collective-permute-done.7.refs_9_), channel_id=1, source_target_pairs={{0,4},{4,8},{8,12},{12,16},{16,20},{20,24},{24,28},{28,0},{1,5},{5... | collective-permute-start | bytes 1044488 | tf_op jit(solution)/shard_map/ppermute | solution.py:36
  31.0 0.7 copy-start.5
  36.6 26.8 %copy-start.7 = (bf16[272,640]{1,0:T(8,128)(2,1)}, bf16[272,640]{1,0:T(8,128)(2,1)S(1)}, u32[]{:S(2)}) copy-start(bf16[272,640]{1,0:T(8,128)(2,1)S(1)} %collective-permute-done.11.refs_13_) | copy-start | bytes 1044484
  36.6 11.5 %collective-permute-start.12 = (bf16[272,640]{1,0:T(8,128)(2,1)S(1)}, bf16[272,640]{1,0:T(8,128)(2,1)S(1)}, u32[]{:S(2)}, u32[]{:S(2)}) collective-permute-start(bf16[272,640]{1,0:T(8,128)(2,1)S(1)} %collective-permute-done.11.refs_13_), channel_id=1, source_target_pairs={{0,28},{4,0},{8,4},{12,8},{16,12},{20,16},{24,20},{28,24},{1,29},{... | collective-permute-start | bytes 1044488 | tf_op jit(solution)/shard_map/ppermute | solution.py:36
  40.8 23.3 %copy-start.9 = (bf16[272,640]{1,0:T(8,128)(2,1)}, bf16[272,640]{1,0:T(8,128)(2,1)S(1)}, u32[]{:S(2)}) copy-start(bf16[272,640]{1,0:T(8,128)(2,1)S(1)} %collective-permute-done.8.refs_10_) | copy-start | bytes 1044484
  40.8 9.6 %collective-permute-start.9 = (bf16[272,640]{1,0:T(8,128)(2,1)S(1)}, bf16[272,640]{1,0:T(8,128)(2,1)S(1)}, u32[]{:S(2)}, u32[]{:S(2)}) collective-permute-start(bf16[272,640]{1,0:T(8,128)(2,1)S(1)} %collective-permute-done.8.refs_10_), channel_id=1, source_target_pairs={{0,4},{4,8},{8,12},{12,16},{16,20},{20,24},{24,28},{28,0},{1,5},{5... | collective-permute-start | bytes 1044488 | tf_op jit(solution)/shard_map/ppermute | solution.py:36
  41.9 13.0 %collective-permute-start = (bf16[128,640]{1,0:T(8,128)(2,1)S(1)}, bf16[128,640]{1,0:T(8,128)(2,1)S(1)}, u32[]{:S(2)}, u32[]{:S(2)}) collective-permute-start(bf16[128,640]{1,0:T(8,128)(2,1)S(1)} %fusion.2.refs_0_), channel_id=1, source_target_pairs={{0,32},{32,0},{64,96},{96,64},{128,160},{160,128},{192,224},{224,1... | collective-permute-start | bytes 491528 | tf_op jit(solution)/shard_map/ppermute | solution.py:44
  43.8 15.0 %collective-permute-start.1 = (bf16[128,640]{1,0:T(8,128)(2,1)S(1)}, bf16[128,640]{1,0:T(8,128)(2,1)S(1)}, u32[]{:S(2)}, u32[]{:S(2)}) collective-permute-start(bf16[128,640]{1,0:T(8,128)(2,1)S(1)} %fusion.2.refs_0_), channel_id=1, source_target_pairs={{0,64},{32,96},{64,128},{96,160},{128,192},{160,224},{192,0},{224,... | collective-permute-start | bytes 491528 | tf_op jit(solution)/shard_map/ppermute | solution.py:44
  45.4 15.7 %collective-permute-start.2 = (bf16[128,640]{1,0:T(8,128)(2,1)S(1)}, bf16[128,640]{1,0:T(8,128)(2,1)S(1)}, u32[]{:S(2)}, u32[]{:S(2)}) collective-permute-start(bf16[128,640]{1,0:T(8,128)(2,1)S(1)} %fusion.2.refs_0_), channel_id=1, source_target_pairs={{0,96},{32,64},{64,160},{96,128},{128,224},{160,192},{192,32},{224... | collective-permute-start | bytes 491528 | tf_op jit(solution)/shard_map/ppermute | solution.py:44
  48.1 15.3 %collective-permute-start.3 = (bf16[128,640]{1,0:T(8,128)(2,1)S(1)}, bf16[128,640]{1,0:T(8,128)(2,1)S(1)}, u32[]{:S(2)}, u32[]{:S(2)}) collective-permute-start(bf16[128,640]{1,0:T(8,128)(2,1)S(1)} %fusion.2.refs_0_), channel_id=1, source_target_pairs={{0,128},{32,160},{64,192},{96,224},{128,0},{160,32},{192,64},{224,... | collective-permute-start | bytes 491528 | tf_op jit(solution)/shard_map/ppermute | solution.py:44
  50.4 20.5 %collective-permute-start.14 = (bf16[144,640]{1,0:T(8,128)(2,1)}, bf16[144,640]{1,0:T(8,128)(2,1)}, u32[]{:S(2)}, u32[]{:S(2)}) collective-permute-start(bf16[144,640]{1,0:T(8,128)(2,1)} %slice.41), channel_id=1, source_target_pairs={{0,28},{4,0},{8,4},{12,8},{16,12},{20,16},{24,20},{28,24},{1,29},{... | collective-permute-start | bytes 552968 | tf_op jit(solution)/shard_map/ppermute | solution.py:36
  54.2 0.7 copy-start.1
  54.9 0.7 copy-start.11
  55.6 10.2 %collective-permute-start.4 = (bf16[128,640]{1,0:T(8,128)(2,1)S(1)}, bf16[128,640]{1,0:T(8,128)(2,1)}, u32[]{:S(2)}, u32[]{:S(2)}) collective-permute-start(bf16[128,640]{1,0:T(8,128)(2,1)S(1)} %fusion.2.refs_0_), channel_id=1, source_target_pairs={{0,160},{32,128},{64,224},{96,192},{128,32},{160,0},{192,96},{224,... | collective-permute-start | bytes 491528 | tf_op jit(solution)/shard_map/ppermute | solution.py:44
  58.8 0.7 copy-start.13
  59.4 7.7 %collective-permute-start.5 = (bf16[128,640]{1,0:T(8,128)(2,1)S(1)}, bf16[128,640]{1,0:T(8,128)(2,1)}, u32[]{:S(2)}, u32[]{:S(2)}) collective-permute-start(bf16[128,640]{1,0:T(8,128)(2,1)S(1)} %fusion.2.refs_0_), channel_id=1, source_target_pairs={{0,192},{32,224},{64,0},{96,32},{128,64},{160,96},{192,128},{224,1... | collective-permute-start | bytes 491528 | tf_op jit(solution)/shard_map/ppermute | solution.py:44
  61.1 0.7 copy-start.15
  61.8 7.8 %collective-permute-start.6 = (bf16[128,640]{1,0:T(8,128)(2,1)S(1)}, bf16[128,640]{1,0:T(8,128)(2,1)}, u32[]{:S(2)}, u32[]{:S(2)}) collective-permute-start(bf16[128,640]{1,0:T(8,128)(2,1)S(1)} %fusion.2.refs_0_), channel_id=1, source_target_pairs={{0,224},{32,192},{64,32},{96,0},{128,96},{160,64},{192,160},{224,1... | collective-permute-start | bytes 491528 | tf_op jit(solution)/shard_map/ppermute | solution.py:44
  63.4 0.7 copy-start.17
  64.1 6.8 %collective-permute-start.13 = (bf16[128,640]{1,0:T(8,128)(2,1)}, bf16[128,640]{1,0:T(8,128)(2,1)}, u32[]{:S(2)}, u32[]{:S(2)}) collective-permute-start(bf16[128,640]{1,0:T(8,128)(2,1)} %slice.40), channel_id=1, source_target_pairs={{0,4},{4,8},{8,12},{12,16},{16,20},{20,24},{24,28},{28,0},{1,5},{5... | collective-permute-start | bytes 491528 | tf_op jit(solution)/shard_map/ppermute | solution.py:36
  70.9 1.0 copy-start.2
  71.9 1.0 copy-start.4
  72.9 1.0 copy-start.6
  73.8 1.0 copy-start.8
  74.8 1.0 copy-start.10
  75.8 0.9 copy-start.12
  76.7 0.9 copy-start.14
  77.6 0.9 copy-start.16
  78.6 0.9 copy-start.18
  95.6 5.3 %copy-start.19 = (bf16[128,640]{1,0:T(8,128)(2,1)S(1)}, bf16[128,640]{1,0:T(8,128)(2,1)}, u32[]{:S(2)}) copy-start(bf16[128,640]{1,0:T(8,128)(2,1)} %param.13) | copy-start | bytes 491524
  95.6 34.0 %all-to-all-start = ((bf16[8,1296,128]{2,1,0:T(8,128)(2,1)}), bf16[8,1296,128]{2,1,0:T(8,128)(2,1)}, u32[]{:S(2)}, u32[]{:S(2)}) async-start(bf16[8,1296,128]{2,1,0:T(8,128)(2,1)} %shard_map.100), calls=%async_computation | async-start | bytes 5308416 | tf_op jit(solution)/shard_map/all_to_all | solution.py:181

commit v2 on v1

v2 whole, which is shorter than its diff:
```python
import jax
import jax.numpy as jnp
from jax import lax
from jax.experimental import pallas as pl
from jax.experimental.pallas import tpu as pltpu
from jax.sharding import Mesh, PartitionSpec as P

HEADS = 20
HD = 128
LOG2E = 1.4426950408889634
SCALE2 = HD ** (-0.5) * LOG2E
PAD_MARK = 1e30
PAD_TEST = 1e20
NEG_FILL = -1e30
ROWS = 128
COLS = 640
HPD = 5
GROUP = 8
OUT_ROWS = COLS + 16
MIB = 1024 * 1024

SM = pl.BlockSpec(memory_space=pltpu.SMEM)


def dot(a, b, ca, cb):
    return lax.dot_general(a, b, (((ca,), (cb,)), ((), ())), preferred_element_type=jnp.float32)


def thirds(value):
    hi = value.astype(jnp.bfloat16).astype(jnp.float32)
    rest = value - hi
    mid = rest.astype(jnp.bfloat16).astype(jnp.float32)
    return hi, mid, rest - mid


def columns_of(row):
    return jnp.broadcast_to(row, (ROWS, ROWS)).T


def factor_of(row):
    return lax.rsqrt(columns_of(row) * (1.0 / (HEADS * HD)) + 1e-06)


def sums_kernel(q_ref, k_ref, c_ref, t_ref, out_ref):
    lane = lax.broadcasted_iota(jnp.int32, (ROWS, ROWS), 1)
    table = jnp.zeros((ROWS, ROWS), jnp.float32)
    for n, ref in enumerate((q_ref, k_ref, c_ref)):
        values = ref[...].astype(jnp.float32)
        table = jnp.where(lane == n, jnp.sum(values * values, axis=1, keepdims=True), table)
    table = table.T
    values = t_ref[...].astype(jnp.float32)
    text = jnp.sum(values * values, axis=1, keepdims=True)
    text = jnp.where(lax.broadcasted_iota(jnp.int32, (8, ROWS), 1) == 0, text, 0.0)
    text = jnp.concatenate([text, jnp.zeros((ROWS - 8, ROWS), jnp.float32)], axis=0).T
    row = lax.broadcasted_iota(jnp.int32, (8, ROWS), 0)
    out_ref[...] = jnp.where(row == 3, text[0:1], table[0:8])


def key_kernel(mask_ref, k_ref, v_ref, tk_ref, tv_ref, part_ref, other_ref, gains_ref, out_ref):
    sums = part_ref[...] + other_ref[...]
    k_factor = factor_of(sums[1:2])
    t_factor = factor_of(sums[3:4])[0:8]
    row = lax.broadcasted_iota(jnp.int32, (8, ROWS), 0)
    usable = jnp.zeros((8, ROWS), jnp.int32)
    for n in range(8):
        usable = jnp.where(row == n, mask_ref[n], usable)
    for h in range(HPD):
        cols = slice(h * HD, (h + 1) * HD)
        k = k_ref[:, cols].astype(jnp.float32) * k_factor * gains_ref[1:2, cols]
        out_ref[0:ROWS, cols] = k.astype(jnp.bfloat16)
        t = tk_ref[:, cols].astype(jnp.float32) * t_factor * gains_ref[3:4, cols]
        t = jnp.where(usable > 0, t, PAD_MARK)
        text = jnp.concatenate([t, tv_ref[:, cols].astype(jnp.float32)], axis=0)
        out_ref[2 * ROWS:2 * ROWS + 16, cols] = text.astype(jnp.bfloat16)
    out_ref[ROWS:2 * ROWS, :] = v_ref[...]


def query_kernel(q_ref, c_ref, part_ref, other_ref, gains_ref, q_out, c_out):
    sums = part_ref[...] + other_ref[...]
    q_factor = factor_of(sums[0:1])
    c_factor = factor_of(sums[2:3])
    for h in range(HPD):
        cols = slice(h * HD, (h + 1) * HD)
        q = (q_ref[:, cols].astype(jnp.float32) * q_factor * gains_ref[0:1, cols]).astype(jnp.bfloat16)
        for j in range(GROUP):
            q_out[j, :, cols] = q
        c_out[:, cols] = (c_ref[:, cols].astype(jnp.float32) * c_factor * gains_ref[2:3, cols]).astype(jnp.bfloat16)


def text_kernel(*refs):
    parts = [ref[...].astype(jnp.float32) for ref in refs[:8]]
    out_ref = refs[8]
    keys = jnp.concatenate([part[0:8] for part in parts], axis=0).astype(jnp.bfloat16)
    values = jnp.concatenate([part[8:16] for part in parts], axis=0).astype(jnp.bfloat16)
    for j in range(GROUP):
        out_ref[j, 0:64, :] = keys
        out_ref[j, 64:128, :] = values


def flash_kernel(q_ref, *refs):
    c_refs = refs[:7]
    k4_ref, v4_ref = refs[7:9]
    out_ref = refs[9]
    vt_s, s_s, p_s, stat_s = refs[10:]
    stat_s[...] = jnp.zeros_like(stat_s)
    stat_row = lax.broadcasted_iota(jnp.int32, (16, ROWS), 0)

    def head(h, carry):
        cols = pl.ds(pl.multiple_of(h * HD, HD), HD)
        for n in range(8):
            value = c_refs[n][ROWS:2 * ROWS, cols] if n < 7 else v4_ref[:, cols]
            vt_s[:, n * ROWS:(n + 1) * ROWS] = value.T
        for pair in range(4):
            q = jnp.concatenate([q_ref[2 * pair, :, cols], q_ref[2 * pair + 1, :, cols]], axis=0)
            top = None
            for n in range(8):
                key = c_refs[n][0:ROWS, cols] if n < 7 else k4_ref[:, cols]
                s = dot(key, q, 1, 1)
                s_s[pair % 2, n * ROWS:(n + 1) * ROWS, :] = s
                part = jnp.max(s.reshape(16, 8, 256), axis=0)
                top = part if top is None else jnp.maximum(top, part)
            top = jnp.max(top, axis=0, keepdims=True)
            total = jnp.zeros((8, 256), jnp.float32)
            for n in range(8):
                p = jnp.exp2((s_s[pair % 2, n * ROWS:(n + 1) * ROWS, :] - top) * SCALE2)
                total = total + jnp.sum(p.reshape(16, 8, 256), axis=0)
                p_s[pair % 2, n * ROWS:(n + 1) * ROWS, :] = p.astype(jnp.bfloat16)
            total = jnp.sum(total, axis=0, keepdims=True)
            o = dot(vt_s[...], p_s[pair % 2], 1, 0)
            o = (o * (1.0 / total)).astype(jnp.bfloat16)
            hi, mid, low = thirds(top * SCALE2 + jnp.log2(total))
            for half in range(2):
                slot = 2 * pair + half
                lanes = slice(half * ROWS, (half + 1) * ROWS)
                out_ref[slot, pl.ds(pl.multiple_of(h * HD, HD), HD), :] = o[:, lanes]
                stats = jnp.where(stat_row == 3 * h, hi[:, lanes], stat_s[slot])
                stats = jnp.where(stat_row == 3 * h + 1, mid[:, lanes], stats)
                stat_s[slot] = jnp.where(stat_row == 3 * h + 2, low[:, lanes], stats)
        return carry

    lax.fori_loop(0, HPD, head, 0)
    for slot in range(GROUP):
        out_ref[slot, COLS:OUT_ROWS, :] = stat_s[slot].astype(jnp.bfloat16)


def cross_kernel(text_ref, qc_ref, out_ref):
    for h in range(HPD):
        cols = slice(h * HD, (h + 1) * HD)
        keys = jnp.concatenate([text_ref[j, 0:64, cols] for j in range(GROUP)], axis=0)
        values = jnp.concatenate([text_ref[j, 64:128, cols] for j in range(GROUP)], axis=0)
        s = dot(keys, qc_ref[:, cols], 1, 1)
        real = keys[:, 0:1].astype(jnp.float32) < PAD_TEST
        s = jnp.where(real, s, NEG_FILL)
        top = jnp.max(s, axis=0, keepdims=True)
        p = jnp.where(real, jnp.exp2((s - top) * SCALE2), 0.0)
        total = jnp.sum(p, axis=0, keepdims=True)
        cross = dot(values, p.astype(jnp.bfloat16), 0, 0) * (1.0 / total)
        out_ref[:, cols] = cross.T


def final_kernel(in_ref, cross_ref, gate_ref, out_ref):
    for h in range(HPD):
        cols = slice(h * HD, (h + 1) * HD)
        levels = []
        for j in range(GROUP):
            stats = in_ref[j, COLS:OUT_ROWS, :].astype(jnp.float32)
            levels.append(stats[3 * h:3 * h + 1] + stats[3 * h + 1:3 * h + 2] + stats[3 * h + 2:3 * h + 3])
        top = levels[0]
        for level in levels[1:]:
            top = jnp.maximum(top, level)
        shares = [jnp.exp2(level - top) for level in levels]
        total = shares[0]
        for share in shares[1:]:
            total = total + share
        inverse = 1.0 / total
        own = jnp.zeros((HD, ROWS), jnp.float32)
        for j in range(GROUP):
            own = own + in_ref[j, h * HD:(h + 1) * HD, :].astype(jnp.float32) * (shares[j] * inverse)
        out_ref[:, cols] = (gate_ref[:, cols] * own.T + cross_ref[:, cols]).astype(jnp.bfloat16)


def block(shape, index=None):
    place = (0,) * len(shape) if index is None else index
    return pl.BlockSpec(shape, lambda i: place, pipeline_mode=pl.Buffered(buffer_count=1))


def call(kernel, shapes, arrays, specs=None, scratch=(), cost=None):
    return pl.pallas_call(
        kernel,
        grid=(1,),
        out_shape=[jax.ShapeDtypeStruct(shape, dtype) for shape, dtype in shapes],
        in_specs=specs or [block(array.shape) for array in arrays],
        out_specs=[block(shape) for shape, _ in shapes],
        scratch_shapes=list(scratch),
        compiler_params=pltpu.CompilerParams(vmem_limit_bytes=60 * MIB),
        cost_estimate=cost,
    )(*arrays)


def pass_kernel(*refs):
    pass


def gate(arrays, after=(), micros=10):
    arrays, after = list(arrays), list(after)
    return pl.pallas_call(
        pass_kernel,
        out_shape=[jax.ShapeDtypeStruct(array.shape, array.dtype) for array in arrays],
        in_specs=[pl.BlockSpec(memory_space=pl.ANY)] * (len(arrays) + len(after)),
        out_specs=[pl.BlockSpec(memory_space=pl.ANY)] * len(arrays),
        input_output_aliases={n: n for n in range(len(arrays))},
        compiler_params=pltpu.CompilerParams(vmem_limit_bytes=MIB),
        cost_estimate=pl.CostEstimate(flops=micros * 1150000000, bytes_accessed=1000, transcendentals=0),
    )(*arrays, *after)


def shift(array, step):
    return lax.ppermute(array, "z", [(i, (i + step) % 8) for i in range(8)])


def local(
    video_query,
    video_key,
    video_value,
    cross_query,
    text_key,
    text_value,
    text_mask,
    norm_gains,
    gate_table,
    timestep,
):
    bf16, f32 = jnp.bfloat16, jnp.float32
    (sums,) = call(sums_kernel, [((8, ROWS), f32)], [video_query, video_key, cross_query, text_key])
    part = sums + lax.ppermute(sums, "head", [(0, 1), (1, 0), (2, 3), (3, 2)])
    other = lax.ppermute(part, "head", [(0, 2), (2, 0), (1, 3), (3, 1)])
    arrays = [text_mask, video_key, video_value, text_key, text_value, part, other, norm_gains]
    (own,) = call(
        key_kernel,
        [((2 * ROWS + 16, COLS), bf16)],
        arrays,
        [SM] + [block(array.shape) for array in arrays[1:]],
    )
    up1, down1 = gate([shift(own, 1), shift(own, -1)])
    queries, cross_norm = call(
        query_kernel,
        [((GROUP, ROWS, COLS), bf16), ((ROWS, COLS), bf16)],
        [video_query, cross_query, part, other, norm_gains],
    )
    queries = lax.all_to_all(queries, ("y", "xh"), 0, 0)
    up2, down2 = gate([shift(up1, 1), shift(down1, -1)], micros=2)
    up3, down3 = gate([shift(up2, 1), shift(down2, -1)], after=[queries], micros=2)
    key4 = shift(up3[:ROWS], 1)
    value4 = shift(down3[ROWS:], -1)
    key4, value4 = gate([key4, value4])

    ring = [own, up1, up2, up3, down1, down2, down3]
    (text_part,) = call(
        text_kernel,
        [((GROUP, ROWS, COLS), bf16)],
        ring + [value4],
        [block((16, COLS), (16, 0))] * 7 + [block((16, COLS), (8, 0))],
    )
    text_whole = lax.all_to_all(text_part, ("y", "xh"), 0, 0)

    (partial,) = call(
        flash_kernel,
        [((GROUP, OUT_ROWS, ROWS), bf16)],
        [queries] + ring + [key4, value4],
        [block(queries.shape)] + [block((2 * ROWS, COLS))] * 7 + [block((ROWS, COLS))] * 2,
        [
            pltpu.VMEM((HD, 1024), bf16),
            pltpu.VMEM((2, 1024, 256), f32),
            pltpu.VMEM((2, 1024, 256), bf16),
            pltpu.VMEM((GROUP, 16, ROWS), f32),
        ],
        pl.CostEstimate(flops=15000000000, bytes_accessed=8000000, transcendentals=5242880),
    )

    received = lax.all_to_all(partial, ("y", "xh"), 0, 0)
    gating = lax.dynamic_slice_in_dim(gate_table, timestep[0], 1, 0)
    (cross,) = call(cross_kernel, [((ROWS, COLS), f32)], [text_whole, cross_norm])
    (out,) = call(final_kernel, [((ROWS, COLS), bf16)], [received, cross, gating])
    return out


def solution(mesh):
    grid = Mesh(mesh.devices.reshape(4, 2, 8, 4), ("y", "xh", "z", "head"))
    tokens = ("y", "xh", "z")
    placed = (
        P(tokens, "head"),
        P(tokens, "head"),
        P(tokens, "head"),
        P(tokens, "head"),
        P(tokens, "head"),
        P(tokens, "head"),
        P(tokens),
        P(None, "head"),
        P(None, "head"),
        P(),
    )
    return jax.shard_map(
        local, mesh=grid, in_specs=placed, out_specs=P(tokens, "head"), check_vma=False
    )
```

time: 134 us -> 103 us (0.77)
  waiting for transfers between devices: 47.9 us -> 32 us
  local copies, waits for them, and re-layouts: 15.8 us -> 2.62 us
  Pallas kernels: 19.9 us -> 29.1 us
  other arithmetic: 7.84 us -> 0.69 us
  blocking collectives: 5.82 us -> 0 us
  starting transfers between devices: 35.4 us -> 37.6 us
    all_to_all x1, waiting for transfers between devices: 28.6 us -> 10.2 us  [local(): received = lax.all_to_all(partial, ('y', 'xh'), 0, 0)]
    all_to_all x0 -> x2, starting transfers between devices: none -> 12.9 us  [the longest x1 6.89 us: local(): text_whole = lax.all_to_all(text_part, ('y', 'xh'), 0, 0)]
    ppermute x7 -> x2, starting transfers between devices: 14.2 us -> 2.27 us  [the longest x1 2.27 us: local(): other = lax.ppermute(part, 'head', [(0, 2), (2, 0), (1, 3), (3, 1)])]
    unnamed x40 -> x22, local copies, waits for them, and re-layouts: 13.4 us -> 1.99 us
    pallas_call x2 -> x11, Pallas kernels: 19.9 us -> 29.1 us  [the longest x7 29.1 us: call(): pl.pallas_call(kernel, grid=(1,), out_shape=[jax.ShapeDtypeStruct(shape,...]
    psum x1 -> x0, blocking collectives: 5.82 us -> none  [local(): lax.psum(jnp.concatenate([squares(video_query), squares(video_key), squar...]
    ppermute x8, waiting for transfers between devices: 13.9 us -> 18.7 us  [shift(): return lax.ppermute(array, 'z', [(i, (i + step) % 8) for i in range(8)])]
    reduce_sum x3 -> x0, other arithmetic: 3.14 us -> none  [squares(): return jnp.sum(values * values, axis=1)]
  transfers between devices with their start and end apart: 16 -> 13, of which waited for: 8 -> 7; matrix products, arithmetic and copies ran while one was open for 2% -> 1% of each run, Pallas kernels for 0% -> 20%
where the time goes in v2:
time: 103 us
  starting transfers between devices  37.6 us (37%)
  waiting for transfers between devices  32 us (31%)
  Pallas kernels  29.1 us (28%)
  local copies, waits for them, and re-layouts  2.62 us (3%)
    pallas_call x7, Pallas kernels, call(): pl.pallas_call(kernel, grid=(1,), out_shape=[jax.ShapeDtypeStruct(shape,...  29.1 us
    ppermute x8, waiting for transfers between devices, shift(): return lax.ppermute(array, 'z', [(i, (i + step) % 8) for i in range(8)])  18.7 us
    ppermute x8, starting transfers between devices, shift(): return lax.ppermute(array, 'z', [(i, (i + step) % 8) for i in range(8)])  15.2 us
    all_to_all x1, waiting for transfers between devices, local(): received = lax.all_to_all(partial, ('y', 'xh'), 0, 0)  10.2 us
    all_to_all x1, starting transfers between devices, local(): received = lax.all_to_all(partial, ('y', 'xh'), 0, 0)  7.21 us
    all_to_all x1, starting transfers between devices, local(): text_whole = lax.all_to_all(text_part, ('y', 'xh'), 0, 0)  6.89 us
    all_to_all x1, starting transfers between devices, local(): queries = lax.all_to_all(queries, ('y', 'xh'), 0, 0)  6.03 us
    ppermute x1, starting transfers between devices, local(): other = lax.ppermute(part, 'head', [(0, 2), (2, 0), (1, 3), (3, 1)])  2.27 us
  transfers between devices with their start and end apart: 13, of which 7 were waited for; matrix products, arithmetic and copies ran while one was open for 1% of the time, Pallas kernels for 20%

profile of v2, /device:TPU:2, one launch (start us, length us, event | category | flops | bytes accessed | tf_op | source)
XLA Modules:
  0.0 102.7 jit_solution(7175776619833731713)
XLA Ops:
  0.0 0.0 copy-start
  0.0 2.1 %shard_map.100 = f32[8,128]{1,0:T(8,128)} custom-call(bf16[128,640]{1,0:T(8,128)(2,1)} %q_ref.3, bf16[128,640]{1,0:T(8,128)(2,1)} %k_ref.3, bf16[128,640]{1,0:T(8,128)(2,1)} %c_ref.3, bf16[8,640]{1,0:T(8,128)(2,1)} %tk_ref.1), custom_call_target="tpu_custom_call" | custom-call | tf_op jit(solution)/shard_map/pallas_call | solution.py:188
  2.1 0.0 collective-permute-start
  2.1 1.4 %collective-permute-done = f32[8,128]{1,0:T(8,128)S(1)} collective-permute-done((f32[8,128]{1,0:T(8,128)}, f32[8,128]{1,0:T(8,128)S(1)}, u32[]{:S(2)}, u32[]{:S(2)}) %collective-permute-start) | collective-permute-done | bytes 4128 | tf_op jit(solution)/shard_map/ppermute | solution.py:235
  3.4 0.7 add.6.part_ref
  4.1 0.0 copy-start.9
  4.1 2.3 %collective-permute-start.1 = (f32[8,128]{1,0:T(8,128)S(1)}, f32[8,128]{1,0:T(8,128)S(1)}, u32[]{:S(2)}, u32[]{:S(2)}) collective-permute-start(f32[8,128]{1,0:T(8,128)S(1)} %add.6.part_ref), channel_id=1, source_target_pairs={{0,2},{2,0},{1,3},{3,1},{4,6},{6,4},{5,7},{7,5},{8,10},{10,8},{9,1... | collective-permute-start | bytes 12296 | tf_op jit(solution)/shard_map/ppermute | solution.py:236
  6.4 1.6 %collective-permute-done.1.other_ref = f32[8,128]{1,0:T(8,128)S(1)} collective-permute-done((f32[8,128]{1,0:T(8,128)S(1)}, f32[8,128]{1,0:T(8,128)S(1)}, u32[]{:S(2)}, u32[]{:S(2)}) %collective-permute-start.1) | collective-permute-done | bytes 4128 | tf_op jit(solution)/shard_map/ppermute | solution.py:236
  8.0 0.0 copy-done.9
  8.0 0.0 copy-start.10
  8.0 0.6 copy-done.10
  8.6 1.9 %shard_map.102.refs_0_ = bf16[272,640]{1,0:T(8,128)(2,1)} custom-call(s32[8]{0:T(128)} %mask_ref.1, bf16[128,640]{1,0:T(8,128)(2,1)} %k_ref.3, bf16[128,640]{1,0:T(8,128)(2,1)} %v_ref.1, bf16[8,640]{1,0:T(8,128)(2,1)} %tk_ref.1, bf16[8,640]{1,0:T(8,128)(2,1)} %tv_ref.1, f32[8,128]{1,0:T(8,128)} %copy-done.9, f32[8,128]{1,0:T(8,128)} %copy-done.10, ...), custom_call_target="tpu_custom_call" | custom-call | tf_op jit(solution)/shard_map/pallas_call | solution.py:188
  10.5 1.7 %collective-permute-start.2 = (bf16[272,640]{1,0:T(8,128)(2,1)}, bf16[272,640]{1,0:T(8,128)(2,1)S(1)}, u32[]{:S(2)}, u32[]{:S(2)}) collective-permute-start(bf16[272,640]{1,0:T(8,128)(2,1)} %shard_map.102.refs_0_), channel_id=1, source_target_pairs={{0,4},{4,8},{8,12},{12,16},{16,20},{20,24},{24,28},{28,0},{1,5},{5... | collective-permute-start | bytes 1044488 | tf_op jit(solution)/shard_map/ppermute | solution.py:218
  12.1 3.9 %collective-permute-start.3 = (bf16[272,640]{1,0:T(8,128)(2,1)}, bf16[272,640]{1,0:T(8,128)(2,1)S(1)}, u32[]{:S(2)}, u32[]{:S(2)}) collective-permute-start(bf16[272,640]{1,0:T(8,128)(2,1)} %shard_map.102.refs_0_), channel_id=1, source_target_pairs={{0,28},{4,0},{8,4},{12,8},{16,12},{20,16},{24,20},{28,24},{1,29},{... | collective-permute-start | bytes 1044488 | tf_op jit(solution)/shard_map/ppermute | solution.py:218
  16.1 2.4 %shard_map.101 = (bf16[8,128,640]{2,1,0:T(8,128)(2,1)}, bf16[128,640]{1,0:T(8,128)(2,1)}) custom-call(bf16[128,640]{1,0:T(8,128)(2,1)} %q_ref.3, bf16[128,640]{1,0:T(8,128)(2,1)} %c_ref.3, f32[8,128]{1,0:T(8,128)} %copy-done.9, f32[8,128]{1,0:T(8,128)} %copy-done.10, f32[4,640]{1,0:T(4,128)} %gains_ref.3), custom_call_target="tpu_custom_call" | custom-call | tf_op jit(solution)/shard_map/pallas_call | solution.py:188
  18.5 6.0 %all-to-all-start = ((bf16[8,128,640]{2,1,0:T(8,128)(2,1)}), bf16[8,128,640]{2,1,0:T(8,128)(2,1)}, u32[]{:S(2)}, u32[]{:S(2)}) async-start(bf16[8,128,640]{2,1,0:T(8,128)(2,1)} %get-tuple-element.15), calls=%async_computation | async-start | bytes 2621440 | tf_op jit(solution)/shard_map/all_to_all | solution.py:250
  24.5 0.0 collective-permute-done.2.refs_0_
  24.5 0.0 collective-permute-done.3.refs_1_
  24.6 0.0 copy-start.3
  24.6 0.0 copy-start.4
  24.6 0.1 collective-permute-start.4
  24.7 3.2 %collective-permute-start.5 = (bf16[272,640]{1,0:T(8,128)(2,1)S(1)}, bf16[272,640]{1,0:T(8,128)(2,1)S(1)}, u32[]{:S(2)}, u32[]{:S(2)}) collective-permute-start(bf16[272,640]{1,0:T(8,128)(2,1)S(1)} %get-tuple-element.17.refs_4_), channel_id=1, source_target_pairs={{0,28},{4,0},{8,4},{12,8},{16,12},{20,16},{24,20},{28,24},{1,29},{... | collective-permute-start | bytes 1044488 | tf_op jit(solution)/shard_map/ppermute | solution.py:218
  27.9 6.5 %collective-permute-done.4.refs_0_ = bf16[272,640]{1,0:T(8,128)(2,1)S(1)} collective-permute-done((bf16[272,640]{1,0:T(8,128)(2,1)S(1)}, bf16[272,640]{1,0:T(8,128)(2,1)S(1)}, u32[]{:S(2)}, u32[]{:S(2)}) %collective-permute-start.4) | collective-permute-done | bytes 348192 | tf_op jit(solution)/shard_map/ppermute | solution.py:218
  34.4 0.0 collective-permute-done.5.refs_1_
  34.4 0.0 copy-done.3
  34.4 0.0 copy-done.4
  34.4 0.0 copy-start.5
  34.4 0.0 copy-start.6
  34.4 0.8 collective-permute-start.6
  35.3 2.5 %collective-permute-start.7 = (bf16[272,640]{1,0:T(8,128)(2,1)S(1)}, bf16[272,640]{1,0:T(8,128)(2,1)S(1)}, u32[]{:S(2)}, u32[]{:S(2)}) collective-permute-start(bf16[272,640]{1,0:T(8,128)(2,1)S(1)} %get-tuple-element.19.refs_5_), channel_id=1, source_target_pairs={{0,28},{4,0},{8,4},{12,8},{16,12},{20,16},{24,20},{28,24},{1,29},{... | collective-permute-start | bytes 1044488 | tf_op jit(solution)/shard_map/ppermute | solution.py:218
  37.7 5.7 %collective-permute-done.6.refs_0_ = bf16[272,640]{1,0:T(8,128)(2,1)S(1)} collective-permute-done((bf16[272,640]{1,0:T(8,128)(2,1)S(1)}, bf16[272,640]{1,0:T(8,128)(2,1)S(1)}, u32[]{:S(2)}, u32[]{:S(2)}) %collective-permute-start.6) | collective-permute-done | bytes 348192 | tf_op jit(solution)/shard_map/ppermute | solution.py:218
  43.4 0.0 copy-done.5
  43.4 0.0 copy-done.6
  43.4 0.0 collective-permute-done.7.refs_1_
  43.4 0.1 all-to-all-done.refs_2_.q_ref
  43.6 0.0 copy-start.1
  43.6 0.0 copy-start.2
  43.6 2.9 %collective-permute-start.9 = (bf16[144,640]{1,0:T(8,128)(2,1)S(1)}, bf16[144,640]{1,0:T(8,128)(2,1)S(1)}, u32[]{:S(2)}, u32[]{:S(2)}) collective-permute-start(bf16[144,640]{1,0:T(8,128)(2,1)S(1)} %slice.7), channel_id=1, source_target_pairs={{0,28},{4,0},{8,4},{12,8},{16,12},{20,16},{24,20},{28,24},{1,29},{... | collective-permute-start | bytes 552968 | tf_op jit(solution)/shard_map/ppermute | solution.py:218
  46.5 0.1 collective-permute-start.8
  46.6 6.5 %collective-permute-done.8.refs_0_ = bf16[128,640]{1,0:T(8,128)(2,1)S(1)} collective-permute-done((bf16[128,640]{1,0:T(8,128)(2,1)S(1)}, bf16[128,640]{1,0:T(8,128)(2,1)S(1)}, u32[]{:S(2)}, u32[]{:S(2)}) %collective-permute-start.8) | collective-permute-done | bytes 163872 | tf_op jit(solution)/shard_map/ppermute | solution.py:218
  53.1 0.0 collective-permute-done.9.refs_1_
  53.1 0.0 copy-done.1
  53.1 0.0 copy-done.2
  53.1 0.0 copy-start.7
  53.1 0.7 copy-done.7
  53.8 0.0 copy-start.8
  53.8 0.7 copy-done.8
  54.5 2.0 %shard_map.108 = bf16[8,128,640]{2,1,0:T(8,128)(2,1)} custom-call(bf16[272,640]{1,0:T(8,128)(2,1)} %shard_map.102.refs_0_, bf16[272,640]{1,0:T(8,128)(2,1)} %copy-done.3, bf16[272,640]{1,0:T(8,128)(2,1)} %copy-done.5, bf16[272,640]{1,0:T(8,128)(2,1)} %copy-done.2, bf16[272,640]{1,0:T(8,128)(2,1)} %copy-done.4, bf16[272,640]{1,0:T(8,128)(2,1)} %copy-done.6, ...), custom_call_target="tpu_custom_call" | custom-call | tf_op jit(solution)/shard_map/pallas_call | solution.py:188
  56.5 6.9 %all-to-all-start.2 = ((bf16[8,128,640]{2,1,0:T(8,128)(2,1)}), bf16[8,128,640]{2,1,0:T(8,128)(2,1)}, u32[]{:S(2)}, u32[]{:S(2)}) async-start(bf16[8,128,640]{2,1,0:T(8,128)(2,1)} %shard_map.108), calls=%async_computation.2 | async-start | bytes 2621440 | tf_op jit(solution)/shard_map/all_to_all | solution.py:264
  63.4 14.9 %shard_map.107 = bf16[8,656,128]{2,1,0:T(8,128)(2,1)} custom-call(bf16[8,128,640]{2,1,0:T(8,128)(2,1)} %all-to-all-done.refs_2_.q_ref, bf16[272,640]{1,0:T(8,128)(2,1)} %shard_map.102.refs_0_, bf16[272,640]{1,0:T(8,128)(2,1)} %copy-done.3, bf16[272,640]{1,0:T(8,128)(2,1)} %copy-done.5, bf16[272,640]{1,0:T(8,128)(2,1)} %copy-done.2, ...), custom_call_target="tpu_custom_call" | custom-call | flops 15000000512 | bytes 8000000 | tf_op jit(solution)/shard_map/pallas_call | solution.py:188
  78.3 0.0 all-to-all-done.2.text_ref
  78.3 7.2 %all-to-all-start.1 = ((bf16[8,656,128]{2,1,0:T(8,128)(2,1)}), bf16[8,656,128]{2,1,0:T(8,128)(2,1)}, u32[]{:S(2)}, u32[]{:S(2)}) async-start(bf16[8,656,128]{2,1,0:T(8,128)(2,1)} %shard_map.107), calls=%async_computation.1 | async-start | bytes 2686976 | tf_op jit(solution)/shard_map/all_to_all | solution.py:280
  86.2 0.0 copy-done
  86.2 0.6 constant_dynamic-slice_fusion.gate_ref
  86.8 3.2 %shard_map.109.cross_ref = f32[128,640]{1,0:T(8,128)} custom-call(bf16[8,128,640]{2,1,0:T(8,128)(2,1)} %all-to-all-done.2.text_ref, bf16[128,640]{1,0:T(8,128)(2,1)} %get-tuple-element.24.qc_ref), custom_call_target="tpu_custom_call" | custom-call | tf_op jit(solution)/shard_map/pallas_call | solution.py:188
  90.0 10.2 %all-to-all-done.1.in_ref = bf16[8,656,128]{2,1,0:T(8,128)(2,1)} async-done(((bf16[8,656,128]{2,1,0:T(8,128)(2,1)}), bf16[8,656,128]{2,1,0:T(8,128)(2,1)}, u32[]{:S(2)}, u32[]{:S(2)}) %all-to-all-start.1) | async-done | bytes 1343520 | tf_op jit(solution)/shard_map/all_to_all | solution.py:280
  100.2 2.5 %shard_map.110 = bf16[128,640]{1,0:T(8,128)(2,1)} custom-call(bf16[8,656,128]{2,1,0:T(8,128)(2,1)} %all-to-all-done.1.in_ref, f32[128,640]{1,0:T(8,128)} %shard_map.109.cross_ref, f32[1,640]{1,0:T(1,128)} %constant_dynamic-slice_fusion.gate_ref), custom_call_target="tpu_custom_call" | custom-call | tf_op jit(solution)/shard_map/pallas_call | solution.py:188
  (6 shorter events, 0.0 us)
Async XLA Ops:
  0.0 86.2 %copy-start = (f32[1000,640]{1,0:T(8,128)S(1)}, f32[1000,640]{1,0:T(8,128)}, u32[]{:S(2)}) copy-start(f32[1000,640]{1,0:T(8,128)} %param.18) | copy-start | bytes 7680004
  2.1 1.4 %collective-permute-start = (f32[8,128]{1,0:T(8,128)}, f32[8,128]{1,0:T(8,128)S(1)}, u32[]{:S(2)}, u32[]{:S(2)}) collective-permute-start(f32[8,128]{1,0:T(8,128)} %shard_map.100), channel_id=1, source_target_pairs={{0,1},{1,0},{2,3},{3,2},{4,5},{5,4},{6,7},{7,6},{8,9},{9,8},{10,11... | collective-permute-start | bytes 12296 | tf_op jit(solution)/shard_map/ppermute | solution.py:235
  4.1 3.9 %copy-start.9 = (f32[8,128]{1,0:T(8,128)}, f32[8,128]{1,0:T(8,128)S(1)}, u32[]{:S(2)}) copy-start(f32[8,128]{1,0:T(8,128)S(1)} %add.6.part_ref) | copy-start | bytes 12292
  4.1 3.9 %collective-permute-start.1 = (f32[8,128]{1,0:T(8,128)S(1)}, f32[8,128]{1,0:T(8,128)S(1)}, u32[]{:S(2)}, u32[]{:S(2)}) collective-permute-start(f32[8,128]{1,0:T(8,128)S(1)} %add.6.part_ref), channel_id=1, source_target_pairs={{0,2},{2,0},{1,3},{3,1},{4,6},{6,4},{5,7},{7,5},{8,10},{10,8},{9,1... | collective-permute-start | bytes 12296 | tf_op jit(solution)/shard_map/ppermute | solution.py:236
  8.0 0.6 copy-start.10
  10.5 14.1 %collective-permute-start.2 = (bf16[272,640]{1,0:T(8,128)(2,1)}, bf16[272,640]{1,0:T(8,128)(2,1)S(1)}, u32[]{:S(2)}, u32[]{:S(2)}) collective-permute-start(bf16[272,640]{1,0:T(8,128)(2,1)} %shard_map.102.refs_0_), channel_id=1, source_target_pairs={{0,4},{4,8},{8,12},{12,16},{16,20},{20,24},{24,28},{28,0},{1,5},{5... | collective-permute-start | bytes 1044488 | tf_op jit(solution)/shard_map/ppermute | solution.py:218
  12.1 12.4 %collective-permute-start.3 = (bf16[272,640]{1,0:T(8,128)(2,1)}, bf16[272,640]{1,0:T(8,128)(2,1)S(1)}, u32[]{:S(2)}, u32[]{:S(2)}) collective-permute-start(bf16[272,640]{1,0:T(8,128)(2,1)} %shard_map.102.refs_0_), channel_id=1, source_target_pairs={{0,28},{4,0},{8,4},{12,8},{16,12},{20,16},{24,20},{28,24},{1,29},{... | collective-permute-start | bytes 1044488 | tf_op jit(solution)/shard_map/ppermute | solution.py:218
  18.5 25.1 %all-to-all-start = ((bf16[8,128,640]{2,1,0:T(8,128)(2,1)}), bf16[8,128,640]{2,1,0:T(8,128)(2,1)}, u32[]{:S(2)}, u32[]{:S(2)}) async-start(bf16[8,128,640]{2,1,0:T(8,128)(2,1)} %get-tuple-element.15), calls=%async_computation | async-start | bytes 2621440 | tf_op jit(solution)/shard_map/all_to_all | solution.py:250
  24.6 9.8 %copy-start.3 = (bf16[272,640]{1,0:T(8,128)(2,1)}, bf16[272,640]{1,0:T(8,128)(2,1)S(1)}, u32[]{:S(2)}) copy-start(bf16[272,640]{1,0:T(8,128)(2,1)S(1)} %get-tuple-element.16.refs_1_) | copy-start | bytes 1044484
  24.6 9.8 %copy-start.4 = (bf16[272,640]{1,0:T(8,128)(2,1)}, bf16[272,640]{1,0:T(8,128)(2,1)S(1)}, u32[]{:S(2)}) copy-start(bf16[272,640]{1,0:T(8,128)(2,1)S(1)} %get-tuple-element.17.refs_4_) | copy-start | bytes 1044484
  24.6 9.8 %collective-permute-start.4 = (bf16[272,640]{1,0:T(8,128)(2,1)S(1)}, bf16[272,640]{1,0:T(8,128)(2,1)S(1)}, u32[]{:S(2)}, u32[]{:S(2)}) collective-permute-start(bf16[272,640]{1,0:T(8,128)(2,1)S(1)} %get-tuple-element.16.refs_1_), channel_id=1, source_target_pairs={{0,4},{4,8},{8,12},{12,16},{16,20},{20,24},{24,28},{28,0},{1,5},{5... | collective-permute-start | bytes 1044488 | tf_op jit(solution)/shard_map/ppermute | solution.py:218
  24.7 9.7 %collective-permute-start.5 = (bf16[272,640]{1,0:T(8,128)(2,1)S(1)}, bf16[272,640]{1,0:T(8,128)(2,1)S(1)}, u32[]{:S(2)}, u32[]{:S(2)}) collective-permute-start(bf16[272,640]{1,0:T(8,128)(2,1)S(1)} %get-tuple-element.17.refs_4_), channel_id=1, source_target_pairs={{0,28},{4,0},{8,4},{12,8},{16,12},{20,16},{24,20},{28,24},{1,29},{... | collective-permute-start | bytes 1044488 | tf_op jit(solution)/shard_map/ppermute | solution.py:218
  34.4 9.0 %copy-start.5 = (bf16[272,640]{1,0:T(8,128)(2,1)}, bf16[272,640]{1,0:T(8,128)(2,1)S(1)}, u32[]{:S(2)}) copy-start(bf16[272,640]{1,0:T(8,128)(2,1)S(1)} %get-tuple-element.18.refs_2_) | copy-start | bytes 1044484
  34.4 9.0 %copy-start.6 = (bf16[272,640]{1,0:T(8,128)(2,1)}, bf16[272,640]{1,0:T(8,128)(2,1)S(1)}, u32[]{:S(2)}) copy-start(bf16[272,640]{1,0:T(8,128)(2,1)S(1)} %get-tuple-element.19.refs_5_) | copy-start | bytes 1044484
  34.4 9.0 %collective-permute-start.6 = (bf16[272,640]{1,0:T(8,128)(2,1)S(1)}, bf16[272,640]{1,0:T(8,128)(2,1)S(1)}, u32[]{:S(2)}, u32[]{:S(2)}) collective-permute-start(bf16[272,640]{1,0:T(8,128)(2,1)S(1)} %get-tuple-element.18.refs_2_), channel_id=1, source_target_pairs={{0,4},{4,8},{8,12},{12,16},{16,20},{20,24},{24,28},{28,0},{1,5},{5... | collective-permute-start | bytes 1044488 | tf_op jit(solution)/shard_map/ppermute | solution.py:218
  35.3 8.1 %collective-permute-start.7 = (bf16[272,640]{1,0:T(8,128)(2,1)S(1)}, bf16[272,640]{1,0:T(8,128)(2,1)S(1)}, u32[]{:S(2)}, u32[]{:S(2)}) collective-permute-start(bf16[272,640]{1,0:T(8,128)(2,1)S(1)} %get-tuple-element.19.refs_5_), channel_id=1, source_target_pairs={{0,28},{4,0},{8,4},{12,8},{16,12},{20,16},{24,20},{28,24},{1,29},{... | collective-permute-start | bytes 1044488 | tf_op jit(solution)/shard_map/ppermute | solution.py:218
  43.6 9.5 %copy-start.1 = (bf16[272,640]{1,0:T(8,128)(2,1)}, bf16[272,640]{1,0:T(8,128)(2,1)S(1)}, u32[]{:S(2)}) copy-start(bf16[272,640]{1,0:T(8,128)(2,1)S(1)} %get-tuple-element.21.refs_6_) | copy-start | bytes 1044484
  43.6 9.5 %copy-start.2 = (bf16[272,640]{1,0:T(8,128)(2,1)}, bf16[272,640]{1,0:T(8,128)(2,1)S(1)}, u32[]{:S(2)}) copy-start(bf16[272,640]{1,0:T(8,128)(2,1)S(1)} %get-tuple-element.20.refs_3_) | copy-start | bytes 1044484
  43.6 9.5 %collective-permute-start.9 = (bf16[144,640]{1,0:T(8,128)(2,1)S(1)}, bf16[144,640]{1,0:T(8,128)(2,1)S(1)}, u32[]{:S(2)}, u32[]{:S(2)}) collective-permute-start(bf16[144,640]{1,0:T(8,128)(2,1)S(1)} %slice.7), channel_id=1, source_target_pairs={{0,28},{4,0},{8,4},{12,8},{16,12},{20,16},{24,20},{28,24},{1,29},{... | collective-permute-start | bytes 552968 | tf_op jit(solution)/shard_map/ppermute | solution.py:218
  46.5 6.6 %collective-permute-start.8 = (bf16[128,640]{1,0:T(8,128)(2,1)S(1)}, bf16[128,640]{1,0:T(8,128)(2,1)S(1)}, u32[]{:S(2)}, u32[]{:S(2)}) collective-permute-start(bf16[128,640]{1,0:T(8,128)(2,1)S(1)} %slice.6), channel_id=1, source_target_pairs={{0,4},{4,8},{8,12},{12,16},{16,20},{20,24},{24,28},{28,0},{1,5},{5... | collective-permute-start | bytes 491528 | tf_op jit(solution)/shard_map/ppermute | solution.py:218
  53.1 0.7 copy-start.7
  53.8 0.7 copy-start.8
  56.5 21.8 %all-to-all-start.2 = ((bf16[8,128,640]{2,1,0:T(8,128)(2,1)}), bf16[8,128,640]{2,1,0:T(8,128)(2,1)}, u32[]{:S(2)}, u32[]{:S(2)}) async-start(bf16[8,128,640]{2,1,0:T(8,128)(2,1)} %shard_map.108), calls=%async_computation.2 | async-start | bytes 2621440 | tf_op jit(solution)/shard_map/all_to_all | solution.py:264
  78.3 21.9 %all-to-all-start.1 = ((bf16[8,656,128]{2,1,0:T(8,128)(2,1)}), bf16[8,656,128]{2,1,0:T(8,128)(2,1)}, u32[]{:S(2)}, u32[]{:S(2)}) async-start(bf16[8,656,128]{2,1,0:T(8,128)(2,1)} %shard_map.107), calls=%async_computation.1 | async-start | bytes 2686976 | tf_op jit(solution)/shard_map/all_to_all | solution.py:280

commit v3 on v2

v3 whole, which is shorter than its diff:
```python
import jax
import jax.numpy as jnp
from jax import lax
from jax.experimental import pallas as pl
from jax.experimental.pallas import tpu as pltpu
from jax.sharding import Mesh, PartitionSpec as P

HEADS = 20
HD = 128
LOG2E = 1.4426950408889634
SCALE2 = HD ** (-0.5) * LOG2E
PAD_MARK = 1e30
PAD_TEST = 1e20
NEG_FILL = -1e30
ROWS = 128
COLS = 640
HPD = 5
GROUP = 8
OUT_ROWS = COLS + 16
MIB = 1024 * 1024
SPAN = 256
PIECE = 32
PARTS = 1024 // SPAN
UNITS = HPD * PARTS

SM = pl.BlockSpec(memory_space=pltpu.SMEM)


def dot(a, b, ca, cb):
    return lax.dot_general(a, b, (((ca,), (cb,)), ((), ())), preferred_element_type=jnp.float32)


def thirds(value):
    hi = value.astype(jnp.bfloat16).astype(jnp.float32)
    rest = value - hi
    mid = rest.astype(jnp.bfloat16).astype(jnp.float32)
    return hi, mid, rest - mid


def columns_of(row):
    return jnp.broadcast_to(row, (ROWS, ROWS)).T


def factor_of(row):
    return lax.rsqrt(columns_of(row) * (1.0 / (HEADS * HD)) + 1e-06)


def sums_kernel(q_ref, k_ref, c_ref, t_ref, out_ref):
    lane = lax.broadcasted_iota(jnp.int32, (ROWS, ROWS), 1)
    table = jnp.zeros((ROWS, ROWS), jnp.float32)
    for n, ref in enumerate((q_ref, k_ref, c_ref)):
        values = ref[...].astype(jnp.float32)
        table = jnp.where(lane == n, jnp.sum(values * values, axis=1, keepdims=True), table)
    table = table.T
    values = t_ref[...].astype(jnp.float32)
    text = jnp.sum(values * values, axis=1, keepdims=True)
    text = jnp.where(lax.broadcasted_iota(jnp.int32, (8, ROWS), 1) == 0, text, 0.0)
    text = jnp.concatenate([text, jnp.zeros((ROWS - 8, ROWS), jnp.float32)], axis=0).T
    row = lax.broadcasted_iota(jnp.int32, (8, ROWS), 0)
    out_ref[...] = jnp.where(row == 3, text[0:1], table[0:8])


def key_kernel(mask_ref, k_ref, v_ref, tk_ref, tv_ref, part_ref, other_ref, gains_ref, out_ref, text_out):
    k_factor = factor_of(part_ref[1:2] + other_ref[1:2])
    t_factor = factor_of(part_ref[3:4] + other_ref[3:4])[0:8]
    row = lax.broadcasted_iota(jnp.int32, (8, ROWS), 0)
    usable = jnp.zeros((8, ROWS), jnp.int32)
    for n in range(8):
        usable = jnp.where(row == n, mask_ref[n], usable)
    for h in range(HPD):
        cols = slice(h * HD, (h + 1) * HD)
        k = k_ref[:, cols].astype(jnp.float32) * k_factor * gains_ref[1:2, cols]
        out_ref[0:ROWS, cols] = k.astype(jnp.bfloat16)
        t = tk_ref[:, cols].astype(jnp.float32) * t_factor * gains_ref[3:4, cols]
        t = jnp.where(usable > 0, t, PAD_MARK)
        text = jnp.concatenate([t, tv_ref[:, cols].astype(jnp.float32)], axis=0).astype(jnp.bfloat16)
        out_ref[2 * ROWS:2 * ROWS + 16, cols] = text
        text_out[:, cols] = text
    out_ref[ROWS:2 * ROWS, :] = v_ref[...]


def query_kernel(q_ref, part_ref, other_ref, gains_ref, out_ref):
    factor = factor_of(part_ref[0:1] + other_ref[0:1])
    for h in range(HPD):
        cols = slice(h * HD, (h + 1) * HD)
        q = (q_ref[:, cols].astype(jnp.float32) * factor * gains_ref[0:1, cols]).astype(jnp.bfloat16)
        for j in range(GROUP):
            out_ref[j, :, cols] = q


def text_kernel(*refs):
    parts = [ref[...].astype(jnp.float32) for ref in refs[:8]]
    out_ref = refs[8]
    keys = jnp.concatenate([part[0:8] for part in parts], axis=0).astype(jnp.bfloat16)
    values = jnp.concatenate([part[8:16] for part in parts], axis=0).astype(jnp.bfloat16)
    for j in range(GROUP):
        out_ref[j, 0:64, :] = keys
        out_ref[j, 64:128, :] = values


def unit_place(unit):
    unit = jnp.clip(unit, 0, UNITS - 1)
    head = lax.div(unit, PARTS)
    first = lax.rem(unit, PARTS) * (SPAN // ROWS)
    return head, first, pl.ds(pl.multiple_of(head * HD, HD), HD)


def flash_kernel(q_ref, *refs):
    c_refs = refs[:8]
    out_ref = refs[8]
    k_s, v_s, s_a, s_b, p_a, p_b, i_a, i_b, stat_s = refs[9:]
    lane = lax.broadcasted_iota(jnp.int32, (PIECE, ROWS), 1)
    stat_s[...] = jnp.zeros_like(stat_s)
    for n in range(8):
        rows = slice(n * ROWS, (n + 1) * ROWS)
        k_s[rows, :] = c_refs[n][0:ROWS, :]
        v_s[rows, :] = c_refs[n][ROWS:2 * ROWS, :]

    def score(unit, s_ref, tile):
        _, first, cols = unit_place(unit)
        q = q_ref[pl.ds(first, SPAN // ROWS), :, cols].reshape(SPAN, HD)
        keys = slice(tile * 256, (tile + 1) * 256)
        s_ref[:, keys] = dot(q, k_s[keys, cols], 1, 1)

    def soften(unit, s_ref, p_ref, i_ref, piece):
        head, first, _ = unit_place(unit)
        rows = slice(piece * PIECE, (piece + 1) * PIECE)
        s = s_ref[rows, :]
        top = s[:, 0:ROWS]
        for n in range(1, 8):
            top = jnp.maximum(top, s[:, n * ROWS:(n + 1) * ROWS])
        top = jnp.max(top, axis=1, keepdims=True)
        p = jnp.exp2((s - top) * SCALE2)
        total = p[:, 0:ROWS]
        for n in range(1, 8):
            total = total + p[:, n * ROWS:(n + 1) * ROWS]
        total = jnp.sum(total, axis=1, keepdims=True)
        p_ref[rows, :] = p.astype(jnp.bfloat16)
        i_ref[rows, :] = jnp.broadcast_to(1.0 / total, (PIECE, ROWS))
        hi, mid, low = thirds(jnp.broadcast_to(top * SCALE2 + jnp.log2(total), (PIECE, ROWS)))
        slot = first + piece * PIECE // ROWS
        inner = slice(piece * PIECE % ROWS, piece * PIECE % ROWS + PIECE)
        stats = jnp.where(lane == 3 * head, hi, stat_s[slot, inner, :])
        stats = jnp.where(lane == 3 * head + 1, mid, stats)
        stat_s[slot, inner, :] = jnp.where(lane == 3 * head + 2, low, stats)

    def blend(unit, p_ref, i_ref):
        head, first, cols = unit_place(unit)
        o = (dot(p_ref[...], v_s[:, cols], 1, 0) * i_ref[...]).astype(jnp.bfloat16)
        for n in range(SPAN // ROWS):
            out_ref[first + n, pl.ds(pl.multiple_of(head * HD, HD), HD), :] = o[n * ROWS:(n + 1) * ROWS]

    def phase(unit, s_next, s_now, p_now, i_now, p_last, i_last):
        blend(unit - 1, p_last, i_last)
        pieces = SPAN // PIECE
        for piece in range(pieces):
            if piece % (pieces // 4) == 0:
                score(unit + 1, s_next, piece // (pieces // 4))
            soften(unit, s_now, p_now, i_now, piece)

    for tile in range(4):
        score(0, s_a, tile)

    def step(i, carry):
        phase(2 * i, s_b, s_a, p_a, i_a, p_b, i_b)
        phase(2 * i + 1, s_a, s_b, p_b, i_b, p_a, i_a)
        return carry

    lax.fori_loop(0, UNITS // 2, step, 0)
    blend(UNITS - 1, p_b, i_b)
    for slot in range(GROUP):
        out_ref[slot, COLS:OUT_ROWS, :] = stat_s[slot].T[0:16].astype(jnp.bfloat16)


def cross_kernel(text_ref, c_ref, part_ref, other_ref, gains_ref, out_ref):
    factor = factor_of(part_ref[2:3] + other_ref[2:3])
    for h in range(HPD):
        cols = slice(h * HD, (h + 1) * HD)
        queries = (c_ref[:, cols].astype(jnp.float32) * factor * gains_ref[2:3, cols]).astype(jnp.bfloat16)
        keys = jnp.concatenate([text_ref[j, 0:64, cols] for j in range(GROUP)], axis=0)
        values = jnp.concatenate([text_ref[j, 64:128, cols] for j in range(GROUP)], axis=0)
        s = dot(keys, queries, 1, 1)
        real = keys[:, 0:1].astype(jnp.float32) < PAD_TEST
        s = jnp.where(real, s, NEG_FILL)
        top = jnp.max(s, axis=0, keepdims=True)
        p = jnp.where(real, jnp.exp2((s - top) * SCALE2), 0.0)
        total = jnp.sum(p, axis=0, keepdims=True)
        cross = dot(values, p.astype(jnp.bfloat16), 0, 0) * (1.0 / total)
        out_ref[:, cols] = cross.T


def final_kernel(in_ref, cross_ref, gate_ref, out_ref):
    for h in range(HPD):
        cols = slice(h * HD, (h + 1) * HD)
        levels = []
        for j in range(GROUP):
            stats = in_ref[j, COLS:OUT_ROWS, :].astype(jnp.float32)
            levels.append(stats[3 * h:3 * h + 1] + stats[3 * h + 1:3 * h + 2] + stats[3 * h + 2:3 * h + 3])
        top = levels[0]
        for level in levels[1:]:
            top = jnp.maximum(top, level)
        shares = [jnp.exp2(level - top) for level in levels]
        total = shares[0]
        for share in shares[1:]:
            total = total + share
        inverse = 1.0 / total
        shares = jnp.concatenate([share * inverse for share in shares], axis=0)
        shares = jnp.concatenate([shares, jnp.zeros((ROWS - GROUP, ROWS), jnp.float32)], axis=0).T
        own = jnp.zeros((ROWS, HD), jnp.float32)
        for j in range(GROUP):
            own = own + in_ref[j, h * HD:(h + 1) * HD, :].astype(jnp.float32) * shares[:, j:j + 1]
        out_ref[:, cols] = (gate_ref[:, cols] * own + cross_ref[:, cols]).astype(jnp.bfloat16)


def block(shape, index=None):
    place = (0,) * len(shape) if index is None else index
    return pl.BlockSpec(shape, lambda i: place, pipeline_mode=pl.Buffered(buffer_count=1))


def call(kernel, shapes, arrays, specs=None, scratch=(), cost=None):
    return pl.pallas_call(
        kernel,
        grid=(1,),
        out_shape=[jax.ShapeDtypeStruct(shape, dtype) for shape, dtype in shapes],
        in_specs=specs or [block(array.shape) for array in arrays],
        out_specs=[block(shape) for shape, _ in shapes],
        scratch_shapes=list(scratch),
        compiler_params=pltpu.CompilerParams(vmem_limit_bytes=60 * MIB),
        cost_estimate=cost,
    )(*arrays)


def flash_call(queries, ring):
    bf16, f32 = jnp.bfloat16, jnp.float32
    return call(
        flash_kernel,
        [((GROUP, OUT_ROWS, ROWS), bf16)],
        [queries] + ring,
        [block((GROUP, ROWS, COLS))] + [block((2 * ROWS, COLS))] * 8,
        [
            pltpu.VMEM((1024, COLS), bf16),
            pltpu.VMEM((1024, COLS), bf16),
            pltpu.VMEM((SPAN, 1024), f32),
            pltpu.VMEM((SPAN, 1024), f32),
            pltpu.VMEM((SPAN, 1024), bf16),
            pltpu.VMEM((SPAN, 1024), bf16),
            pltpu.VMEM((SPAN, ROWS), f32),
            pltpu.VMEM((SPAN, ROWS), f32),
            pltpu.VMEM((GROUP, ROWS, ROWS), f32),
        ],
        pl.CostEstimate(flops=15000000000, bytes_accessed=8000000, transcendentals=5242880),
    )


def pass_kernel(*refs):
    pass


def gate(arrays, after=(), micros=10):
    arrays, after = list(arrays), list(after)
    return pl.pallas_call(
        pass_kernel,
        out_shape=[jax.ShapeDtypeStruct(array.shape, array.dtype) for array in arrays],
        in_specs=[pl.BlockSpec(memory_space=pl.ANY)] * (len(arrays) + len(after)),
        out_specs=[pl.BlockSpec(memory_space=pl.ANY)] * len(arrays),
        input_output_aliases={n: n for n in range(len(arrays))},
        compiler_params=pltpu.CompilerParams(vmem_limit_bytes=MIB),
        cost_estimate=pl.CostEstimate(flops=micros * 1150000000, bytes_accessed=1000, transcendentals=0),
    )(*arrays, *after)


def shift(array, step):
    return lax.ppermute(array, "z", [(i, (i + step) % 8) for i in range(8)])


def local(
    video_query,
    video_key,
    video_value,
    cross_query,
    text_key,
    text_value,
    text_mask,
    norm_gains,
    gate_table,
    timestep,
):
    bf16, f32 = jnp.bfloat16, jnp.float32
    (sums,) = call(sums_kernel, [((8, ROWS), f32)], [video_query, video_key, cross_query, text_key])
    part = sums + lax.ppermute(sums, "head", [(0, 1), (1, 0), (2, 3), (3, 2)])
    other = lax.ppermute(part, "head", [(0, 2), (2, 0), (1, 3), (3, 1)])
    arrays = [text_mask, video_key, video_value, text_key, text_value, part, other, norm_gains]
    own, text_own = call(
        key_kernel,
        [((2 * ROWS + 16, COLS), bf16), ((16, COLS), bf16)],
        arrays,
        [SM] + [block(array.shape) for array in arrays[1:]],
    )
    up1, down1 = gate([shift(own, 1), shift(own, -1)])
    (queries,) = call(
        query_kernel, [((GROUP, ROWS, COLS), bf16)], [video_query, part, other, norm_gains]
    )
    queries = lax.all_to_all(queries, ("y", "xh"), 0, 0)
    text4 = shift(text_own, 4)
    up2, down2 = gate([shift(up1, 1), shift(down1, -1)], after=[text4], micros=2)
    up3, down3 = gate([shift(up2, 1), shift(down2, -1)], after=[queries], micros=2)
    (far,) = gate([shift(up3, 1)])

    ring = [own, up1, up2, up3, down1, down2, down3]
    (text,) = call(
        text_kernel,
        [((GROUP, ROWS, COLS), bf16)],
        ring + [text4],
        [block((16, COLS), (16, 0))] * 7 + [block((16, COLS))],
    )
    text = lax.all_to_all(text, ("y", "xh"), 0, 0)

    (partial,) = flash_call(queries, ring + [far])

    received = lax.all_to_all(partial, ("y", "xh"), 0, 0)
    gating = lax.dynamic_slice_in_dim(gate_table, timestep[0], 1, 0)
    (cross,) = call(cross_kernel, [((ROWS, COLS), f32)], [text, cross_query, part, other, norm_gains])
    (out,) = call(final_kernel, [((ROWS, COLS), bf16)], [received, cross, gating])
    return out


def solution(mesh):
    grid = Mesh(mesh.devices.reshape(4, 2, 8, 4), ("y", "xh", "z", "head"))
    tokens = ("y", "xh", "z")
    placed = (
        P(tokens, "head"),
        P(tokens, "head"),
        P(tokens, "head"),
        P(tokens, "head"),
        P(tokens, "head"),
        P(tokens, "head"),
        P(tokens),
        P(None, "head"),
        P(None, "head"),
        P(),
    )
    return jax.shard_map(
        local, mesh=grid, in_specs=placed, out_specs=P(tokens, "head"), check_vma=False
    )
```

time: 103 us -> 99.3 us (0.964)
  waiting for transfers between devices: 32 us -> 26.6 us
  local copies, waits for them, and re-layouts: 2.62 us -> 6.27 us
  Pallas kernels: 29.1 us -> 27.1 us
    ppermute x8, waiting for transfers between devices: 18.7 us -> 10 us  [shift(): return lax.ppermute(array, 'z', [(i, (i + step) % 8) for i in range(8)])]
    unnamed x22 -> x28, local copies, waits for them, and re-layouts: 1.99 us -> 5.67 us
    all_to_all x1, starting transfers between devices: 7.21 us -> 4.52 us  [local(): received = lax.all_to_all(partial, ('y', 'xh'), 0, 0)]
    all_to_all x1, waiting for transfers between devices: 0.01 us -> 2.68 us  [local(): text = lax.all_to_all(text, ('y', 'xh'), 0, 0)]
    pallas_call x7, Pallas kernels: 29.1 us -> 27.1 us  [call(): pl.pallas_call(kernel, grid=(1,), out_shape=[jax.ShapeDtypeStruct(shape,...]
    ppermute x8, starting transfers between devices: 15.2 us -> 16.8 us  [shift(): return lax.ppermute(array, 'z', [(i, (i + step) % 8) for i in range(8)])]
where the time goes in v3:
time: 99.3 us; the launch traced here: 98.1 us
  starting transfers between devices  36.6 us (37%)
  Pallas kernels  27.1 us (27%)
  waiting for transfers between devices  26.6 us (27%)
  local copies, waits for them, and re-layouts  6.27 us (6%)
    pallas_call x7, Pallas kernels, call(): pl.pallas_call(kernel, grid=(1,), out_shape=[jax.ShapeDtypeStruct(shape,...  27.1 us
    ppermute x8, starting transfers between devices, shift(): return lax.ppermute(array, 'z', [(i, (i + step) % 8) for i in range(8)])  16.8 us
    all_to_all x1, waiting for transfers between devices, local(): received = lax.all_to_all(partial, ('y', 'xh'), 0, 0)  10.9 us
    ppermute x8, waiting for transfers between devices, shift(): return lax.ppermute(array, 'z', [(i, (i + step) % 8) for i in range(8)])  10 us
    all_to_all x1, starting transfers between devices, local(): text = lax.all_to_all(text, ('y', 'xh'), 0, 0)  6.92 us
    all_to_all x1, starting transfers between devices, local(): queries = lax.all_to_all(queries, ('y', 'xh'), 0, 0)  6.03 us
    unnamed x28, local copies, waits for them, and re-layouts  5.67 us
    all_to_all x1, starting transfers between devices, local(): received = lax.all_to_all(partial, ('y', 'xh'), 0, 0)  4.52 us
  transfers between devices with their start and end apart: 13, of which 7 were waited for; matrix products, arithmetic and copies ran while one was open for 1% of the time, Pallas kernels for 20%

profile of v3, /device:TPU:2, one launch (start us, length us, event | category | flops | bytes accessed | tf_op | source)
XLA Modules:
  0.0 98.1 jit_solution(18231270398518729201)
XLA Ops:
  0.0 0.0 copy-start
  0.0 2.1 %shard_map.100 = f32[8,128]{1,0:T(8,128)} custom-call(bf16[128,640]{1,0:T(8,128)(2,1)} %q_ref.3, bf16[128,640]{1,0:T(8,128)(2,1)} %k_ref.3, bf16[128,640]{1,0:T(8,128)(2,1)} %c_ref.3, bf16[8,640]{1,0:T(8,128)(2,1)} %tk_ref.1), custom_call_target="tpu_custom_call" | custom-call | tf_op jit(solution)/shard_map/pallas_call | solution.py:221
  2.1 0.0 collective-permute-start
  2.1 1.4 %collective-permute-done = f32[8,128]{1,0:T(8,128)S(1)} collective-permute-done((f32[8,128]{1,0:T(8,128)}, f32[8,128]{1,0:T(8,128)S(1)}, u32[]{:S(2)}, u32[]{:S(2)}) %collective-permute-start) | collective-permute-done | bytes 4128 | tf_op jit(solution)/shard_map/ppermute | solution.py:290
  3.4 0.7 add.6.part_ref
  4.1 0.0 copy-start.11
  4.1 2.3 %collective-permute-start.1 = (f32[8,128]{1,0:T(8,128)S(1)}, f32[8,128]{1,0:T(8,128)S(1)}, u32[]{:S(2)}, u32[]{:S(2)}) collective-permute-start(f32[8,128]{1,0:T(8,128)S(1)} %add.6.part_ref), channel_id=1, source_target_pairs={{0,2},{2,0},{1,3},{3,1},{4,6},{6,4},{5,7},{7,5},{8,10},{10,8},{9,1... | collective-permute-start | bytes 12296 | tf_op jit(solution)/shard_map/ppermute | solution.py:291
  6.4 1.6 %collective-permute-done.1.other_ref = f32[8,128]{1,0:T(8,128)S(1)} collective-permute-done((f32[8,128]{1,0:T(8,128)S(1)}, f32[8,128]{1,0:T(8,128)S(1)}, u32[]{:S(2)}, u32[]{:S(2)}) %collective-permute-start.1) | collective-permute-done | bytes 4128 | tf_op jit(solution)/shard_map/ppermute | solution.py:291
  8.0 0.0 copy-done.11
  8.0 0.0 copy-start.12
  8.0 0.6 copy-done.12
  8.6 1.9 %shard_map.102 = (bf16[272,640]{1,0:T(8,128)(2,1)}, bf16[16,640]{1,0:T(8,128)(2,1)}) custom-call(s32[8]{0:T(128)} %mask_ref.1, bf16[128,640]{1,0:T(8,128)(2,1)} %k_ref.3, bf16[128,640]{1,0:T(8,128)(2,1)} %v_ref.1, bf16[8,640]{1,0:T(8,128)(2,1)} %tk_ref.1, bf16[8,640]{1,0:T(8,128)(2,1)} %tv_ref.1, f32[8,128]{1,0:T(8,128)} %copy-done.11, f32[8,128]{1,0:T(8,128)} %copy-done.12, ...), custom_call_target="tpu_custom_call" | custom-call | tf_op jit(solution)/shard_map/pallas_call | solution.py:221
  10.5 1.7 %collective-permute-start.2 = (bf16[272,640]{1,0:T(8,128)(2,1)}, bf16[272,640]{1,0:T(8,128)(2,1)S(1)}, u32[]{:S(2)}, u32[]{:S(2)}) collective-permute-start(bf16[272,640]{1,0:T(8,128)(2,1)} %get-tuple-element.13.refs_0_), channel_id=1, source_target_pairs={{0,4},{4,8},{8,12},{12,16},{16,20},{20,24},{24,28},{28,0},{1,5},{5... | collective-permute-start | bytes 1044488 | tf_op jit(solution)/shard_map/ppermute | solution.py:273
  12.1 3.9 %collective-permute-start.3 = (bf16[272,640]{1,0:T(8,128)(2,1)}, bf16[272,640]{1,0:T(8,128)(2,1)S(1)}, u32[]{:S(2)}, u32[]{:S(2)}) collective-permute-start(bf16[272,640]{1,0:T(8,128)(2,1)} %get-tuple-element.13.refs_0_), channel_id=1, source_target_pairs={{0,28},{4,0},{8,4},{12,8},{16,12},{20,16},{24,20},{28,24},{1,29},{... | collective-permute-start | bytes 1044488 | tf_op jit(solution)/shard_map/ppermute | solution.py:273
  16.1 2.2 %shard_map.101 = bf16[8,128,640]{2,1,0:T(8,128)(2,1)} custom-call(bf16[128,640]{1,0:T(8,128)(2,1)} %q_ref.3, f32[8,128]{1,0:T(8,128)} %copy-done.11, f32[8,128]{1,0:T(8,128)} %copy-done.12, f32[4,640]{1,0:T(4,128)} %gains_ref.5), custom_call_target="tpu_custom_call" | custom-call | tf_op jit(solution)/shard_map/pallas_call | solution.py:221
  18.3 6.0 %all-to-all-start = ((bf16[8,128,640]{2,1,0:T(8,128)(2,1)}), bf16[8,128,640]{2,1,0:T(8,128)(2,1)}, u32[]{:S(2)}, u32[]{:S(2)}) async-start(bf16[8,128,640]{2,1,0:T(8,128)(2,1)} %shard_map.101), calls=%async_computation | async-start | bytes 2621440 | tf_op jit(solution)/shard_map/all_to_all | solution.py:303
  24.4 0.0 copy-start.13
  24.4 0.0 collective-permute-done.2.refs_0_
  24.4 0.0 collective-permute-done.3.refs_1_
  24.4 0.0 copy-start.5
  24.4 0.7 copy-done.5
  25.1 0.0 copy-start.2
  25.1 0.0 collective-permute-start.4
  25.1 3.2 %collective-permute-start.5 = (bf16[272,640]{1,0:T(8,128)(2,1)}, bf16[272,640]{1,0:T(8,128)(2,1)S(1)}, u32[]{:S(2)}, u32[]{:S(2)}) collective-permute-start(bf16[272,640]{1,0:T(8,128)(2,1)} %copy-done.5), channel_id=1, source_target_pairs={{0,28},{4,0},{8,4},{12,8},{16,12},{20,16},{24,20},{28,24},{1,29},{... | collective-permute-start | bytes 1044488 | tf_op jit(solution)/shard_map/ppermute | solution.py:273
  28.4 0.0 copy-done.13
  28.4 4.6 %collective-permute-start.6 = (bf16[16,640]{1,0:T(8,128)(2,1)S(1)}, bf16[16,640]{1,0:T(8,128)(2,1)S(1)}, u32[]{:S(2)}, u32[]{:S(2)}) collective-permute-start(bf16[16,640]{1,0:T(8,128)(2,1)S(1)} %copy-done.13), channel_id=1, source_target_pairs={{0,16},{4,20},{8,24},{12,28},{16,0},{20,4},{24,8},{28,12},{1,17},{... | collective-permute-start | bytes 61448 | tf_op jit(solution)/shard_map/ppermute | solution.py:273
  32.9 3.9 %collective-permute-done.6.refs_2_.refs_7_ = bf16[16,640]{1,0:T(8,128)(2,1)S(1)} collective-permute-done((bf16[16,640]{1,0:T(8,128)(2,1)S(1)}, bf16[16,640]{1,0:T(8,128)(2,1)S(1)}, u32[]{:S(2)}, u32[]{:S(2)}) %collective-permute-start.6) | collective-permute-done | bytes 20512 | tf_op jit(solution)/shard_map/ppermute | solution.py:273
  36.8 0.0 copy-start.9
  36.8 0.0 collective-permute-done.4.refs_0_
  36.8 0.0 collective-permute-done.5.refs_1_
  36.9 0.0 copy-done.2
  36.9 0.6 copy-done.9
  37.4 0.0 copy-start.3
  37.4 0.0 copy-start.1
  37.5 2.1 %collective-permute-start.7 = (bf16[272,640]{1,0:T(8,128)(2,1)S(1)}, bf16[272,640]{1,0:T(8,128)(2,1)S(1)}, u32[]{:S(2)}, u32[]{:S(2)}) collective-permute-start(bf16[272,640]{1,0:T(8,128)(2,1)S(1)} %get-tuple-element.17.refs_2_), channel_id=1, source_target_pairs={{0,4},{4,8},{8,12},{12,16},{16,20},{20,24},{24,28},{28,0},{1,5},{5... | collective-permute-start | bytes 1044488 | tf_op jit(solution)/shard_map/ppermute | solution.py:273
  39.5 1.2 %collective-permute-start.8 = (bf16[272,640]{1,0:T(8,128)(2,1)S(1)}, bf16[272,640]{1,0:T(8,128)(2,1)S(1)}, u32[]{:S(2)}, u32[]{:S(2)}) collective-permute-start(bf16[272,640]{1,0:T(8,128)(2,1)S(1)} %get-tuple-element.18.refs_5_), channel_id=1, source_target_pairs={{0,28},{4,0},{8,4},{12,8},{16,12},{20,16},{24,20},{28,24},{1,29},{... | collective-permute-start | bytes 1044488 | tf_op jit(solution)/shard_map/ppermute | solution.py:273
  40.7 5.3 %collective-permute-done.7.refs_0_ = bf16[272,640]{1,0:T(8,128)(2,1)S(1)} collective-permute-done((bf16[272,640]{1,0:T(8,128)(2,1)S(1)}, bf16[272,640]{1,0:T(8,128)(2,1)S(1)}, u32[]{:S(2)}, u32[]{:S(2)}) %collective-permute-start.7) | collective-permute-done | bytes 348192 | tf_op jit(solution)/shard_map/ppermute | solution.py:273
  46.0 0.0 copy-done.3
  46.0 0.9 collective-permute-done.8.refs_1_
  46.8 0.0 copy-start.6
  46.8 0.7 copy-done.6
  47.5 0.0 all-to-all-done.refs_2_.q_ref
  47.6 0.0 copy-start.7
  47.6 1.0 copy-done.7
  48.5 0.0 copy-done.1
  48.5 0.0 copy-start.8
  48.5 0.7 copy-done.8
  49.3 0.0 copy-start.4
  49.3 0.2 collective-permute-start.9
  49.5 0.5 copy-done.4
  50.0 2.0 %shard_map.108 = bf16[8,128,640]{2,1,0:T(8,128)(2,1)} custom-call(bf16[272,640]{1,0:T(8,128)(2,1)} %get-tuple-element.13.refs_0_, bf16[272,640]{1,0:T(8,128)(2,1)} %copy-done.2, bf16[272,640]{1,0:T(8,128)(2,1)} %copy-done.1, bf16[272,640]{1,0:T(8,128)(2,1)} %copy-done.4, bf16[272,640]{1,0:T(8,128)(2,1)} %copy-done.5, bf16[272,640]{1,0:T(8,128)(2,1)} %copy-done.3, ...), custom_call_target="tpu_custom_call" | custom-call | tf_op jit(solution)/shard_map/pallas_call | solution.py:221
  52.0 6.9 %all-to-all-start.2 = ((bf16[8,128,640]{2,1,0:T(8,128)(2,1)}), bf16[8,128,640]{2,1,0:T(8,128)(2,1)}, u32[]{:S(2)}, u32[]{:S(2)}) async-start(bf16[8,128,640]{2,1,0:T(8,128)(2,1)} %shard_map.108), calls=%async_computation.2 | async-start | bytes 2621440 | tf_op jit(solution)/shard_map/all_to_all | solution.py:316
  59.0 0.0 collective-permute-done.9.refs_0_
  59.0 0.0 copy-start.10
  59.0 0.8 copy-done.10
  59.7 12.3 %shard_map.107 = bf16[8,656,128]{2,1,0:T(8,128)(2,1)} custom-call(bf16[8,128,640]{2,1,0:T(8,128)(2,1)} %all-to-all-done.refs_2_.q_ref, bf16[272,640]{1,0:T(8,128)(2,1)} %get-tuple-element.13.refs_0_, bf16[272,640]{1,0:T(8,128)(2,1)} %copy-done.2, bf16[272,640]{1,0:T(8,128)(2,1)} %copy-done.1, bf16[272,640]{1,0:T(8,128)(2,1)} %copy-done.4, ...), custom_call_target="tpu_custom_call" | custom-call | flops 15000000512 | bytes 8000000 | tf_op jit(solution)/shard_map/pallas_call | solution.py:221
  72.1 2.7 %all-to-all-done.2.text_ref = bf16[8,128,640]{2,1,0:T(8,128)(2,1)} async-done(((bf16[8,128,640]{2,1,0:T(8,128)(2,1)}), bf16[8,128,640]{2,1,0:T(8,128)(2,1)}, u32[]{:S(2)}, u32[]{:S(2)}) %all-to-all-start.2) | async-done | bytes 1310752 | tf_op jit(solution)/shard_map/all_to_all | solution.py:316
  74.8 4.5 %all-to-all-start.1 = ((bf16[8,656,128]{2,1,0:T(8,128)(2,1)}), bf16[8,656,128]{2,1,0:T(8,128)(2,1)}, u32[]{:S(2)}, u32[]{:S(2)}) async-start(bf16[8,656,128]{2,1,0:T(8,128)(2,1)} %shard_map.107), calls=%async_computation.1 | async-start | bytes 2686976 | tf_op jit(solution)/shard_map/all_to_all | solution.py:320
  79.9 0.0 copy-done
  79.9 0.6 constant_dynamic-slice_fusion.gate_ref
  80.5 3.4 %shard_map.109.cross_ref = f32[128,640]{1,0:T(8,128)} custom-call(bf16[8,128,640]{2,1,0:T(8,128)(2,1)} %all-to-all-done.2.text_ref, bf16[128,640]{1,0:T(8,128)(2,1)} %c_ref.3, f32[8,128]{1,0:T(8,128)} %copy-done.11, f32[8,128]{1,0:T(8,128)} %copy-done.12, f32[4,640]{1,0:T(4,128)} %gains_ref.5), custom_call_target="tpu_custom_call" | custom-call | tf_op jit(solution)/shard_map/pallas_call | solution.py:221
  84.0 10.9 %all-to-all-done.1.in_ref = bf16[8,656,128]{2,1,0:T(8,128)(2,1)} async-done(((bf16[8,656,128]{2,1,0:T(8,128)(2,1)}), bf16[8,656,128]{2,1,0:T(8,128)(2,1)}, u32[]{:S(2)}, u32[]{:S(2)}) %all-to-all-start.1) | async-done | bytes 1343520 | tf_op jit(solution)/shard_map/all_to_all | solution.py:320
  94.9 3.2 %shard_map.110 = bf16[128,640]{1,0:T(8,128)(2,1)} custom-call(bf16[8,656,128]{2,1,0:T(8,128)(2,1)} %all-to-all-done.1.in_ref, f32[128,640]{1,0:T(8,128)} %shard_map.109.cross_ref, f32[1,640]{1,0:T(1,128)} %constant_dynamic-slice_fusion.gate_ref), custom_call_target="tpu_custom_call" | custom-call | tf_op jit(solution)/shard_map/pallas_call | solution.py:221
  (4 shorter events, 0.0 us)
Async XLA Ops:
  0.0 79.9 %copy-start = (f32[1000,640]{1,0:T(8,128)S(1)}, f32[1000,640]{1,0:T(8,128)}, u32[]{:S(2)}) copy-start(f32[1000,640]{1,0:T(8,128)} %param.18) | copy-start | bytes 7680004
  2.1 1.4 %collective-permute-start = (f32[8,128]{1,0:T(8,128)}, f32[8,128]{1,0:T(8,128)S(1)}, u32[]{:S(2)}, u32[]{:S(2)}) collective-permute-start(f32[8,128]{1,0:T(8,128)} %shard_map.100), channel_id=1, source_target_pairs={{0,1},{1,0},{2,3},{3,2},{4,5},{5,4},{6,7},{7,6},{8,9},{9,8},{10,11... | collective-permute-start | bytes 12296 | tf_op jit(solution)/shard_map/ppermute | solution.py:290
  4.1 3.9 %copy-start.11 = (f32[8,128]{1,0:T(8,128)}, f32[8,128]{1,0:T(8,128)S(1)}, u32[]{:S(2)}) copy-start(f32[8,128]{1,0:T(8,128)S(1)} %add.6.part_ref) | copy-start | bytes 12292
  4.1 3.9 %collective-permute-start.1 = (f32[8,128]{1,0:T(8,128)S(1)}, f32[8,128]{1,0:T(8,128)S(1)}, u32[]{:S(2)}, u32[]{:S(2)}) collective-permute-start(f32[8,128]{1,0:T(8,128)S(1)} %add.6.part_ref), channel_id=1, source_target_pairs={{0,2},{2,0},{1,3},{3,1},{4,6},{6,4},{5,7},{7,5},{8,10},{10,8},{9,1... | collective-permute-start | bytes 12296 | tf_op jit(solution)/shard_map/ppermute | solution.py:291
  8.0 0.6 copy-start.12
  10.5 13.9 %collective-permute-start.2 = (bf16[272,640]{1,0:T(8,128)(2,1)}, bf16[272,640]{1,0:T(8,128)(2,1)S(1)}, u32[]{:S(2)}, u32[]{:S(2)}) collective-permute-start(bf16[272,640]{1,0:T(8,128)(2,1)} %get-tuple-element.13.refs_0_), channel_id=1, source_target_pairs={{0,4},{4,8},{8,12},{12,16},{16,20},{20,24},{24,28},{28,0},{1,5},{5... | collective-permute-start | bytes 1044488 | tf_op jit(solution)/shard_map/ppermute | solution.py:273
  12.1 12.2 %collective-permute-start.3 = (bf16[272,640]{1,0:T(8,128)(2,1)}, bf16[272,640]{1,0:T(8,128)(2,1)S(1)}, u32[]{:S(2)}, u32[]{:S(2)}) collective-permute-start(bf16[272,640]{1,0:T(8,128)(2,1)} %get-tuple-element.13.refs_0_), channel_id=1, source_target_pairs={{0,28},{4,0},{8,4},{12,8},{16,12},{20,16},{24,20},{28,24},{1,29},{... | collective-permute-start | bytes 1044488 | tf_op jit(solution)/shard_map/ppermute | solution.py:273
  18.3 29.2 %all-to-all-start = ((bf16[8,128,640]{2,1,0:T(8,128)(2,1)}), bf16[8,128,640]{2,1,0:T(8,128)(2,1)}, u32[]{:S(2)}, u32[]{:S(2)}) async-start(bf16[8,128,640]{2,1,0:T(8,128)(2,1)} %shard_map.101), calls=%async_computation | async-start | bytes 2621440 | tf_op jit(solution)/shard_map/all_to_all | solution.py:303
  24.4 4.0 %copy-start.13 = (bf16[16,640]{1,0:T(8,128)(2,1)S(1)}, bf16[16,640]{1,0:T(8,128)(2,1)}, u32[]{:S(2)}) copy-start(bf16[16,640]{1,0:T(8,128)(2,1)} %get-tuple-element.16) | copy-start | bytes 61444
  24.4 0.7 copy-start.5
  25.1 11.7 %copy-start.2 = (bf16[272,640]{1,0:T(8,128)(2,1)}, bf16[272,640]{1,0:T(8,128)(2,1)S(1)}, u32[]{:S(2)}) copy-start(bf16[272,640]{1,0:T(8,128)(2,1)S(1)} %get-tuple-element.14.refs_1_) | copy-start | bytes 1044484
  25.1 11.7 %collective-permute-start.4 = (bf16[272,640]{1,0:T(8,128)(2,1)S(1)}, bf16[272,640]{1,0:T(8,128)(2,1)S(1)}, u32[]{:S(2)}, u32[]{:S(2)}) collective-permute-start(bf16[272,640]{1,0:T(8,128)(2,1)S(1)} %get-tuple-element.14.refs_1_), channel_id=1, source_target_pairs={{0,4},{4,8},{8,12},{12,16},{16,20},{20,24},{24,28},{28,0},{1,5},{5... | collective-permute-start | bytes 1044488 | tf_op jit(solution)/shard_map/ppermute | solution.py:273
  25.1 11.7 %collective-permute-start.5 = (bf16[272,640]{1,0:T(8,128)(2,1)}, bf16[272,640]{1,0:T(8,128)(2,1)S(1)}, u32[]{:S(2)}, u32[]{:S(2)}) collective-permute-start(bf16[272,640]{1,0:T(8,128)(2,1)} %copy-done.5), channel_id=1, source_target_pairs={{0,28},{4,0},{8,4},{12,8},{16,12},{20,16},{24,20},{28,24},{1,29},{... | collective-permute-start | bytes 1044488 | tf_op jit(solution)/shard_map/ppermute | solution.py:273
  28.4 8.5 %collective-permute-start.6 = (bf16[16,640]{1,0:T(8,128)(2,1)S(1)}, bf16[16,640]{1,0:T(8,128)(2,1)S(1)}, u32[]{:S(2)}, u32[]{:S(2)}) collective-permute-start(bf16[16,640]{1,0:T(8,128)(2,1)S(1)} %copy-done.13), channel_id=1, source_target_pairs={{0,16},{4,20},{8,24},{12,28},{16,0},{20,4},{24,8},{28,12},{1,17},{... | collective-permute-start | bytes 61448 | tf_op jit(solution)/shard_map/ppermute | solution.py:273
  36.8 0.6 copy-start.9
  37.4 8.5 %copy-start.3 = (bf16[272,640]{1,0:T(8,128)(2,1)}, bf16[272,640]{1,0:T(8,128)(2,1)S(1)}, u32[]{:S(2)}) copy-start(bf16[272,640]{1,0:T(8,128)(2,1)S(1)} %get-tuple-element.18.refs_5_) | copy-start | bytes 1044484
  37.4 11.1 %copy-start.1 = (bf16[272,640]{1,0:T(8,128)(2,1)}, bf16[272,640]{1,0:T(8,128)(2,1)S(1)}, u32[]{:S(2)}) copy-start(bf16[272,640]{1,0:T(8,128)(2,1)S(1)} %get-tuple-element.17.refs_2_) | copy-start | bytes 1044484
  37.5 8.5 %collective-permute-start.7 = (bf16[272,640]{1,0:T(8,128)(2,1)S(1)}, bf16[272,640]{1,0:T(8,128)(2,1)S(1)}, u32[]{:S(2)}, u32[]{:S(2)}) collective-permute-start(bf16[272,640]{1,0:T(8,128)(2,1)S(1)} %get-tuple-element.17.refs_2_), channel_id=1, source_target_pairs={{0,4},{4,8},{8,12},{12,16},{16,20},{20,24},{24,28},{28,0},{1,5},{5... | collective-permute-start | bytes 1044488 | tf_op jit(solution)/shard_map/ppermute | solution.py:273
  39.5 7.3 %collective-permute-start.8 = (bf16[272,640]{1,0:T(8,128)(2,1)S(1)}, bf16[272,640]{1,0:T(8,128)(2,1)S(1)}, u32[]{:S(2)}, u32[]{:S(2)}) collective-permute-start(bf16[272,640]{1,0:T(8,128)(2,1)S(1)} %get-tuple-element.18.refs_5_), channel_id=1, source_target_pairs={{0,28},{4,0},{8,4},{12,8},{16,12},{20,16},{24,20},{28,24},{1,29},{... | collective-permute-start | bytes 1044488 | tf_op jit(solution)/shard_map/ppermute | solution.py:273
  46.8 0.7 copy-start.6
  47.6 1.0 %copy-start.7 = (bf16[272,640]{1,0:T(8,128)(2,1)S(1)}, bf16[272,640]{1,0:T(8,128)(2,1)}, u32[]{:S(2)}) copy-start(bf16[272,640]{1,0:T(8,128)(2,1)} %copy-done.6) | copy-start | bytes 1044484
  48.5 0.7 copy-start.8
  49.3 0.7 copy-start.4
  49.3 9.7 %collective-permute-start.9 = (bf16[272,640]{1,0:T(8,128)(2,1)S(1)}, bf16[272,640]{1,0:T(8,128)(2,1)S(1)}, u32[]{:S(2)}, u32[]{:S(2)}) collective-permute-start(bf16[272,640]{1,0:T(8,128)(2,1)S(1)} %get-tuple-element.19.refs_3_), channel_id=1, source_target_pairs={{0,4},{4,8},{8,12},{12,16},{16,20},{20,24},{24,28},{28,0},{1,5},{5... | collective-permute-start | bytes 1044488 | tf_op jit(solution)/shard_map/ppermute | solution.py:273
  52.0 22.7 %all-to-all-start.2 = ((bf16[8,128,640]{2,1,0:T(8,128)(2,1)}), bf16[8,128,640]{2,1,0:T(8,128)(2,1)}, u32[]{:S(2)}, u32[]{:S(2)}) async-start(bf16[8,128,640]{2,1,0:T(8,128)(2,1)} %shard_map.108), calls=%async_computation.2 | async-start | bytes 2621440 | tf_op jit(solution)/shard_map/all_to_all | solution.py:316
  59.0 0.8 copy-start.10
  74.8 20.1 %all-to-all-start.1 = ((bf16[8,656,128]{2,1,0:T(8,128)(2,1)}), bf16[8,656,128]{2,1,0:T(8,128)(2,1)}, u32[]{:S(2)}, u32[]{:S(2)}) async-start(bf16[8,656,128]{2,1,0:T(8,128)(2,1)} %shard_map.107), calls=%async_computation.1 | async-start | bytes 2686976 | tf_op jit(solution)/shard_map/all_to_all | solution.py:320

commit v4 on v3

--- a/solution.py
+++ b/solution.py
@@ -18,12 +18,13 @@
 GROUP = 8
 OUT_ROWS = COLS + 16
 MIB = 1024 * 1024
+LIMIT = 60
 SPAN = 256
 PIECE = 32
 PARTS = 1024 // SPAN
 UNITS = HPD * PARTS
 
-SM = pl.BlockSpec(memory_space=pltpu.SMEM)
+VM = pl.BlockSpec(memory_space=pltpu.VMEM)
 
 
 def dot(a, b, ca, cb):
@@ -60,7 +61,7 @@
     out_ref[...] = jnp.where(row == 3, text[0:1], table[0:8])
 
 
-def key_kernel(mask_ref, k_ref, v_ref, tk_ref, tv_ref, part_ref, other_ref, gains_ref, out_ref, text_out):
+def key_kernel(mask_ref, k_ref, v_ref, tk_ref, tv_ref, gains_ref, part_ref, other_ref, out_ref, text_out):
     k_factor = factor_of(part_ref[1:2] + other_ref[1:2])
     t_factor = factor_of(part_ref[3:4] + other_ref[3:4])[0:8]
     row = lax.broadcasted_iota(jnp.int32, (8, ROWS), 0)
@@ -79,7 +80,7 @@
     out_ref[ROWS:2 * ROWS, :] = v_ref[...]
 
 
-def query_kernel(q_ref, part_ref, other_ref, gains_ref, out_ref):
+def query_kernel(q_ref, gains_ref, part_ref, other_ref, out_ref):
     factor = factor_of(part_ref[0:1] + other_ref[0:1])
     for h in range(HPD):
         cols = slice(h * HD, (h + 1) * HD)
@@ -172,7 +173,7 @@
         out_ref[slot, COLS:OUT_ROWS, :] = stat_s[slot].T[0:16].astype(jnp.bfloat16)
 
 
-def cross_kernel(text_ref, c_ref, part_ref, other_ref, gains_ref, out_ref):
+def cross_kernel(text_ref, c_ref, gains_ref, part_ref, other_ref, out_ref):
     factor = factor_of(part_ref[2:3] + other_ref[2:3])
     for h in range(HPD):
         cols = slice(h * HD, (h + 1) * HD)
@@ -212,31 +213,54 @@
         out_ref[:, cols] = (gate_ref[:, cols] * own + cross_ref[:, cols]).astype(jnp.bfloat16)
 
 
+def in_hbm(array):
+    return pltpu.with_memory_space_constraint(array, pltpu.HBM)
+
+
+def in_vmem(array):
+    return pltpu.with_memory_space_constraint(array, pltpu.VMEM)
+
+
 def block(shape, index=None):
     place = (0,) * len(shape) if index is None else index
     return pl.BlockSpec(shape, lambda i: place, pipeline_mode=pl.Buffered(buffer_count=1))
 
 
-def call(kernel, shapes, arrays, specs=None, scratch=(), cost=None):
+def call(kernel, shapes, arrays, near=(), scalars=0, scratch=(), cost=None, free=()):
+    ins, specs = [], []
+    for n, array in enumerate(arrays):
+        ins.append(array if n < scalars else in_hbm(array))
+        specs.append(pl.BlockSpec(memory_space=pltpu.SMEM) if n < scalars else block(array.shape))
+    for array in near:
+        ins.append(in_vmem(array))
+        specs.append(VM)
+    for array, shape, index in free:
+        ins.append(array)
+        specs.append(block(shape, index))
+    out_shape, out_specs = [], []
+    for shape, dtype, place in shapes:
+        out_shape.append(place(shape, dtype))
+        out_specs.append(VM if place is pltpu.VMEM else block(shape))
     return pl.pallas_call(
         kernel,
         grid=(1,),
-        out_shape=[jax.ShapeDtypeStruct(shape, dtype) for shape, dtype in shapes],
-        in_specs=specs or [block(array.shape) for array in arrays],
-        out_specs=[block(shape) for shape, _ in shapes],
+        out_shape=out_shape,
+        in_specs=specs,
+        out_specs=out_specs,
         scratch_shapes=list(scratch),
-        compiler_params=pltpu.CompilerParams(vmem_limit_bytes=60 * MIB),
+        compiler_params=pltpu.CompilerParams(vmem_limit_bytes=LIMIT * MIB),
         cost_estimate=cost,
-    )(*arrays)
+    )(*ins)
 
 
 def flash_call(queries, ring):
     bf16, f32 = jnp.bfloat16, jnp.float32
     return call(
         flash_kernel,
-        [((GROUP, OUT_ROWS, ROWS), bf16)],
-        [queries] + ring,
-        [block((GROUP, ROWS, COLS))] + [block((2 * ROWS, COLS))] * 8,
+        [((GROUP, OUT_ROWS, ROWS), bf16, pltpu.HBM)],
+        [queries],
+        (),
+        0,
         [
             pltpu.VMEM((1024, COLS), bf16),
             pltpu.VMEM((1024, COLS), bf16),
@@ -249,6 +273,7 @@
             pltpu.VMEM((GROUP, ROWS, ROWS), f32),
         ],
         pl.CostEstimate(flops=15000000000, bytes_accessed=8000000, transcendentals=5242880),
+        [(array, (2 * ROWS, COLS), (0, 0)) for array in ring],
     )
 
 
@@ -286,32 +311,34 @@
     timestep,
 ):
     bf16, f32 = jnp.bfloat16, jnp.float32
-    (sums,) = call(sums_kernel, [((8, ROWS), f32)], [video_query, video_key, cross_query, text_key])
+    (sums,) = call(
+        sums_kernel, [((8, ROWS), f32, pltpu.VMEM)], [video_query, video_key, cross_query, text_key]
+    )
     part = sums + lax.ppermute(sums, "head", [(0, 1), (1, 0), (2, 3), (3, 2)])
     other = lax.ppermute(part, "head", [(0, 2), (2, 0), (1, 3), (3, 1)])
-    arrays = [text_mask, video_key, video_value, text_key, text_value, part, other, norm_gains]
     own, text_own = call(
         key_kernel,
-        [((2 * ROWS + 16, COLS), bf16), ((16, COLS), bf16)],
-        arrays,
-        [SM] + [block(array.shape) for array in arrays[1:]],
+        [((2 * ROWS + 16, COLS), bf16, jax.ShapeDtypeStruct), ((16, COLS), bf16, jax.ShapeDtypeStruct)],
+        [text_mask, video_key, video_value, text_key, text_value, norm_gains],
+        [part, other],
+        1,
     )
     up1, down1 = gate([shift(own, 1), shift(own, -1)])
     (queries,) = call(
-        query_kernel, [((GROUP, ROWS, COLS), bf16)], [video_query, part, other, norm_gains]
+        query_kernel, [((GROUP, ROWS, COLS), bf16, pltpu.HBM)], [video_query, norm_gains], [part, other]
     )
     queries = lax.all_to_all(queries, ("y", "xh"), 0, 0)
+    up2, down2 = gate([shift(up1, 1), shift(down1, -1)], micros=2)
     text4 = shift(text_own, 4)
-    up2, down2 = gate([shift(up1, 1), shift(down1, -1)], after=[text4], micros=2)
-    up3, down3 = gate([shift(up2, 1), shift(down2, -1)], after=[queries], micros=2)
+    up3, down3 = gate([shift(up2, 1), shift(down2, -1)], after=[queries, text4], micros=2)
     (far,) = gate([shift(up3, 1)])
 
     ring = [own, up1, up2, up3, down1, down2, down3]
     (text,) = call(
         text_kernel,
-        [((GROUP, ROWS, COLS), bf16)],
-        ring + [text4],
-        [block((16, COLS), (16, 0))] * 7 + [block((16, COLS))],
+        [((GROUP, ROWS, COLS), bf16, pltpu.HBM)],
+        [],
+        free=[(array, (16, COLS), (16, 0)) for array in ring] + [(text4, (16, COLS), (0, 0))],
     )
     text = lax.all_to_all(text, ("y", "xh"), 0, 0)
 
@@ -319,8 +346,10 @@
 
     received = lax.all_to_all(partial, ("y", "xh"), 0, 0)
     gating = lax.dynamic_slice_in_dim(gate_table, timestep[0], 1, 0)
-    (cross,) = call(cross_kernel, [((ROWS, COLS), f32)], [text, cross_query, part, other, norm_gains])
-    (out,) = call(final_kernel, [((ROWS, COLS), bf16)], [received, cross, gating])
+    (cross,) = call(
+        cross_kernel, [((ROWS, COLS), f32, pltpu.VMEM)], [text, cross_query, norm_gains], [part, other]
+    )
+    (out,) = call(final_kernel, [((ROWS, COLS), bf16, pltpu.HBM)], [received], [cross, gating])
     return out
 
 

time: 99.3 us -> 94.2 us (0.949)
  local copies, waits for them, and re-layouts: 6.27 us -> 2.09 us
  Pallas kernels: 27.1 us -> 25.6 us
  starting transfers between devices: 36.6 us -> 37.7 us
    unnamed x28 -> x20, local copies, waits for them, and re-layouts: 5.67 us -> 2.08 us
    pallas_call x7, Pallas kernels: 27.1 us -> 25.6 us  [call(): pl.pallas_call(kernel, grid=(1,), out_shape=out_shape, in_specs=specs, ou...]
    ppermute x8, starting transfers between devices: 16.8 us -> 18.2 us  [shift(): return lax.ppermute(array, 'z', [(i, (i + step) % 8) for i in range(8)])]
    all_to_all x1, waiting for transfers between devices: 10.9 us -> 12.1 us  [local(): received = lax.all_to_all(partial, ('y', 'xh'), 0, 0)]
  transfers between devices with their start and end apart: 13 -> 13, of which waited for: 7 -> 6; matrix products, arithmetic and copies ran while one was open for 1% -> 0% of each run, Pallas kernels for 20% -> 21%
where the time goes in v4:
time: 94.2 us; the launch traced here: 93.7 us
  starting transfers between devices  37.7 us (40%)
  waiting for transfers between devices  27.4 us (29%)
  Pallas kernels  25.6 us (27%)
  local copies, waits for them, and re-layouts  2.09 us (2%)
    pallas_call x7, Pallas kernels, call(): pl.pallas_call(kernel, grid=(1,), out_shape=out_shape, in_specs=specs, ou...  25.6 us
    ppermute x8, starting transfers between devices, shift(): return lax.ppermute(array, 'z', [(i, (i + step) % 8) for i in range(8)])  18.2 us
    all_to_all x1, waiting for transfers between devices, local(): received = lax.all_to_all(partial, ('y', 'xh'), 0, 0)  12.1 us
    ppermute x8, waiting for transfers between devices, shift(): return lax.ppermute(array, 'z', [(i, (i + step) % 8) for i in range(8)])  9.9 us
    all_to_all x1, starting transfers between devices, local(): text = lax.all_to_all(text, ('y', 'xh'), 0, 0)  6.64 us
    all_to_all x1, starting transfers between devices, local(): queries = lax.all_to_all(queries, ('y', 'xh'), 0, 0)  6.03 us
    all_to_all x1, starting transfers between devices, local(): received = lax.all_to_all(partial, ('y', 'xh'), 0, 0)  4.58 us
    all_to_all x1, waiting for transfers between devices, local(): text = lax.all_to_all(text, ('y', 'xh'), 0, 0)  2.62 us
  transfers between devices with their start and end apart: 13, of which 6 were waited for; matrix products, arithmetic and copies ran while one was open for 0% of the time, Pallas kernels for 21%

profile of v4, /device:TPU:2, one launch (start us, length us, event | category | flops | bytes accessed | tf_op | source)
XLA Modules:
  0.0 93.7 jit_solution(16706954284282636191)
XLA Ops:
  0.0 0.0 copy-start
  0.0 1.4 %shard_map.100 = f32[8,128]{1,0:T(8,128)S(1)} custom-call(bf16[128,640]{1,0:T(8,128)(2,1)} %q_ref.3, bf16[128,640]{1,0:T(8,128)(2,1)} %k_ref.3, bf16[128,640]{1,0:T(8,128)(2,1)} %c_ref.3, bf16[8,640]{1,0:T(8,128)(2,1)} %tk_ref.1), custom_call_target="tpu_custom_call" | custom-call | tf_op jit(solution)/shard_map/pallas_call | solution.py:244
  1.4 0.1 collective-permute-start
  1.5 1.2 %collective-permute-done = f32[8,128]{1,0:T(8,128)S(1)} collective-permute-done((f32[8,128]{1,0:T(8,128)S(1)}, f32[8,128]{1,0:T(8,128)S(1)}, u32[]{:S(2)}, u32[]{:S(2)}) %collective-permute-start) | collective-permute-done | bytes 4128 | tf_op jit(solution)/shard_map/ppermute | solution.py:317
  2.7 2.3 %collective-permute-start.1 = (f32[8,128]{1,0:T(8,128)S(1)}, f32[8,128]{1,0:T(8,128)S(1)}, u32[]{:S(2)}, u32[]{:S(2)}) collective-permute-start(f32[8,128]{1,0:T(8,128)S(1)} %add.6.part_ref), channel_id=1, source_target_pairs={{0,2},{2,0},{1,3},{3,1},{4,6},{6,4},{5,7},{7,5},{8,10},{10,8},{9,1... | collective-permute-start | bytes 12296 | tf_op jit(solution)/shard_map/ppermute | solution.py:318
  4.9 1.6 %collective-permute-done.1.other_ref = f32[8,128]{1,0:T(8,128)S(1)} collective-permute-done((f32[8,128]{1,0:T(8,128)S(1)}, f32[8,128]{1,0:T(8,128)S(1)}, u32[]{:S(2)}, u32[]{:S(2)}) %collective-permute-start.1) | collective-permute-done | bytes 4128 | tf_op jit(solution)/shard_map/ppermute | solution.py:318
  6.5 1.9 %shard_map.102 = (bf16[272,640]{1,0:T(8,128)(2,1)}, bf16[16,640]{1,0:T(8,128)(2,1)}) custom-call(s32[8]{0:T(128)} %mask_ref.1, bf16[128,640]{1,0:T(8,128)(2,1)} %k_ref.3, bf16[128,640]{1,0:T(8,128)(2,1)} %v_ref.1, bf16[8,640]{1,0:T(8,128)(2,1)} %tk_ref.1, bf16[8,640]{1,0:T(8,128)(2,1)} %tv_ref.1, f32[4,640]{1,0:T(4,128)} %gains_ref.5, ...), custom_call_target="tpu_custom_call" | custom-call | tf_op jit(solution)/shard_map/pallas_call | solution.py:244
  8.4 1.7 %collective-permute-start.2 = (bf16[272,640]{1,0:T(8,128)(2,1)}, bf16[272,640]{1,0:T(8,128)(2,1)S(1)}, u32[]{:S(2)}, u32[]{:S(2)}) collective-permute-start(bf16[272,640]{1,0:T(8,128)(2,1)} %get-tuple-element.13.refs_0_), channel_id=1, source_target_pairs={{0,4},{4,8},{8,12},{12,16},{16,20},{20,24},{24,28},{28,0},{1,5},{5... | collective-permute-start | bytes 1044488 | tf_op jit(solution)/shard_map/ppermute | solution.py:298
  10.1 3.9 %collective-permute-start.3 = (bf16[272,640]{1,0:T(8,128)(2,1)}, bf16[272,640]{1,0:T(8,128)(2,1)S(1)}, u32[]{:S(2)}, u32[]{:S(2)}) collective-permute-start(bf16[272,640]{1,0:T(8,128)(2,1)} %get-tuple-element.13.refs_0_), channel_id=1, source_target_pairs={{0,28},{4,0},{8,4},{12,8},{16,12},{20,16},{24,20},{28,24},{1,29},{... | collective-permute-start | bytes 1044488 | tf_op jit(solution)/shard_map/ppermute | solution.py:298
  14.0 2.2 %shard_map.101 = bf16[8,128,640]{2,1,0:T(8,128)(2,1)} custom-call(bf16[128,640]{1,0:T(8,128)(2,1)} %q_ref.3, f32[4,640]{1,0:T(4,128)} %gains_ref.5, f32[8,128]{1,0:T(8,128)S(1)} %add.6.part_ref, f32[8,128]{1,0:T(8,128)S(1)} %collective-permute-done.1.other_ref), custom_call_target="tpu_custom_call" | custom-call | tf_op jit(solution)/shard_map/pallas_call | solution.py:244
  16.3 6.0 %all-to-all-start = ((bf16[8,128,640]{2,1,0:T(8,128)(2,1)}), bf16[8,128,640]{2,1,0:T(8,128)(2,1)}, u32[]{:S(2)}, u32[]{:S(2)}) async-start(bf16[8,128,640]{2,1,0:T(8,128)(2,1)} %shard_map.101), calls=%async_computation | async-start | bytes 2621440 | tf_op jit(solution)/shard_map/all_to_all | solution.py:330
  22.3 0.0 collective-permute-done.2.refs_0_
  22.3 0.0 collective-permute-done.3.refs_1_
  22.3 0.0 copy-start.3
  22.3 0.0 copy-start.4
  22.3 0.1 collective-permute-start.4
  22.4 0.0 copy-start.9
  22.4 3.2 %collective-permute-start.5 = (bf16[272,640]{1,0:T(8,128)(2,1)S(1)}, bf16[272,640]{1,0:T(8,128)(2,1)S(1)}, u32[]{:S(2)}, u32[]{:S(2)}) collective-permute-start(bf16[272,640]{1,0:T(8,128)(2,1)S(1)} %get-tuple-element.15.refs_4_), channel_id=1, source_target_pairs={{0,28},{4,0},{8,4},{12,8},{16,12},{20,16},{24,20},{28,24},{1,29},{... | collective-permute-start | bytes 1044488 | tf_op jit(solution)/shard_map/ppermute | solution.py:298
  25.6 6.5 %collective-permute-done.4.refs_0_ = bf16[272,640]{1,0:T(8,128)(2,1)S(1)} collective-permute-done((bf16[272,640]{1,0:T(8,128)(2,1)S(1)}, bf16[272,640]{1,0:T(8,128)(2,1)S(1)}, u32[]{:S(2)}, u32[]{:S(2)}) %collective-permute-start.4) | collective-permute-done | bytes 348192 | tf_op jit(solution)/shard_map/ppermute | solution.py:298
  32.1 0.0 collective-permute-done.5.refs_1_
  32.1 0.0 copy-done.3
  32.1 0.0 copy-done.4
  32.1 0.0 copy-start.5
  32.2 0.0 copy-start.6
  32.2 1.0 %collective-permute-start.6 = (bf16[272,640]{1,0:T(8,128)(2,1)S(1)}, bf16[272,640]{1,0:T(8,128)(2,1)S(1)}, u32[]{:S(2)}, u32[]{:S(2)}) collective-permute-start(bf16[272,640]{1,0:T(8,128)(2,1)S(1)} %get-tuple-element.16.refs_2_), channel_id=1, source_target_pairs={{0,4},{4,8},{8,12},{12,16},{16,20},{20,24},{24,28},{28,0},{1,5},{5... | collective-permute-start | bytes 1044488 | tf_op jit(solution)/shard_map/ppermute | solution.py:298
  33.2 2.3 %collective-permute-start.7 = (bf16[272,640]{1,0:T(8,128)(2,1)S(1)}, bf16[272,640]{1,0:T(8,128)(2,1)S(1)}, u32[]{:S(2)}, u32[]{:S(2)}) collective-permute-start(bf16[272,640]{1,0:T(8,128)(2,1)S(1)} %get-tuple-element.17.refs_5_), channel_id=1, source_target_pairs={{0,28},{4,0},{8,4},{12,8},{16,12},{20,16},{24,20},{28,24},{1,29},{... | collective-permute-start | bytes 1044488 | tf_op jit(solution)/shard_map/ppermute | solution.py:298
  35.5 0.0 copy-done.9
  35.5 4.3 %collective-permute-start.8 = (bf16[16,640]{1,0:T(8,128)(2,1)S(1)}, bf16[16,640]{1,0:T(8,128)(2,1)S(1)}, u32[]{:S(2)}, u32[]{:S(2)}) collective-permute-start(bf16[16,640]{1,0:T(8,128)(2,1)S(1)} %copy-done.9), channel_id=1, source_target_pairs={{0,16},{4,20},{8,24},{12,28},{16,0},{20,4},{24,8},{28,12},{1,17},{... | collective-permute-start | bytes 61448 | tf_op jit(solution)/shard_map/ppermute | solution.py:298
  39.8 3.4 %collective-permute-done.8.refs_3_.refs_7_ = bf16[16,640]{1,0:T(8,128)(2,1)S(1)} collective-permute-done((bf16[16,640]{1,0:T(8,128)(2,1)S(1)}, bf16[16,640]{1,0:T(8,128)(2,1)S(1)}, u32[]{:S(2)}, u32[]{:S(2)}) %collective-permute-start.8) | collective-permute-done | bytes 20512 | tf_op jit(solution)/shard_map/ppermute | solution.py:298
  43.2 0.0 copy-start.7
  43.2 0.0 collective-permute-done.6.refs_0_
  43.2 0.0 copy-done.5
  43.2 0.0 copy-done.6
  43.2 0.0 collective-permute-done.7.refs_1_
  43.2 0.0 all-to-all-done.refs_2_.q_ref
  43.2 0.6 copy-done.7
  43.8 0.0 copy-start.2
  43.8 0.7 copy-done.2
  44.5 0.0 copy-start.1
  44.5 1.6 %collective-permute-start.9 = (bf16[272,640]{1,0:T(8,128)(2,1)S(1)}, bf16[272,640]{1,0:T(8,128)(2,1)S(1)}, u32[]{:S(2)}, u32[]{:S(2)}) collective-permute-start(bf16[272,640]{1,0:T(8,128)(2,1)S(1)} %get-tuple-element.19.refs_3_), channel_id=1, source_target_pairs={{0,4},{4,8},{8,12},{12,16},{16,20},{20,24},{24,28},{28,0},{1,5},{5... | collective-permute-start | bytes 1044488 | tf_op jit(solution)/shard_map/ppermute | solution.py:298
  46.2 0.0 copy-done.1
  46.2 2.1 %shard_map.108 = bf16[8,128,640]{2,1,0:T(8,128)(2,1)} custom-call(bf16[272,640]{1,0:T(8,128)(2,1)} %get-tuple-element.13.refs_0_, bf16[272,640]{1,0:T(8,128)(2,1)} %copy-done.3, bf16[272,640]{1,0:T(8,128)(2,1)} %copy-done.5, bf16[272,640]{1,0:T(8,128)(2,1)} %copy-done.1, bf16[272,640]{1,0:T(8,128)(2,1)} %copy-done.4, bf16[272,640]{1,0:T(8,128)(2,1)} %copy-done.6, ...), custom_call_target="tpu_custom_call" | custom-call | tf_op jit(solution)/shard_map/pallas_call | solution.py:244
  48.2 6.6 %all-to-all-start.2 = ((bf16[8,128,640]{2,1,0:T(8,128)(2,1)}), bf16[8,128,640]{2,1,0:T(8,128)(2,1)}, u32[]{:S(2)}, u32[]{:S(2)}) async-start(bf16[8,128,640]{2,1,0:T(8,128)(2,1)} %shard_map.108), calls=%async_computation.2 | async-start | bytes 2621440 | tf_op jit(solution)/shard_map/all_to_all | solution.py:343
  54.9 0.0 collective-permute-done.9.refs_0_
  54.9 0.0 copy-start.8
  54.9 0.8 copy-done.8
  55.7 12.3 %shard_map.107 = bf16[8,656,128]{2,1,0:T(8,128)(2,1)} custom-call(bf16[8,128,640]{2,1,0:T(8,128)(2,1)} %all-to-all-done.refs_2_.q_ref, bf16[272,640]{1,0:T(8,128)(2,1)} %get-tuple-element.13.refs_0_, bf16[272,640]{1,0:T(8,128)(2,1)} %copy-done.3, bf16[272,640]{1,0:T(8,128)(2,1)} %copy-done.5, bf16[272,640]{1,0:T(8,128)(2,1)} %copy-done.1, ...), custom_call_target="tpu_custom_call" | custom-call | flops 15000000512 | bytes 8000000 | tf_op jit(solution)/shard_map/pallas_call | solution.py:244
  67.9 2.6 %all-to-all-done.2.text_ref = bf16[8,128,640]{2,1,0:T(8,128)(2,1)} async-done(((bf16[8,128,640]{2,1,0:T(8,128)(2,1)}), bf16[8,128,640]{2,1,0:T(8,128)(2,1)}, u32[]{:S(2)}, u32[]{:S(2)}) %all-to-all-start.2) | async-done | bytes 1310752 | tf_op jit(solution)/shard_map/all_to_all | solution.py:343
  70.6 4.6 %all-to-all-start.1 = ((bf16[8,656,128]{2,1,0:T(8,128)(2,1)}), bf16[8,656,128]{2,1,0:T(8,128)(2,1)}, u32[]{:S(2)}, u32[]{:S(2)}) async-start(bf16[8,656,128]{2,1,0:T(8,128)(2,1)} %shard_map.107), calls=%async_computation.1 | async-start | bytes 2686976 | tf_op jit(solution)/shard_map/all_to_all | solution.py:347
  75.8 0.0 copy-done
  75.8 2.7 %shard_map.109.cross_ref = f32[128,640]{1,0:T(8,128)S(1)} custom-call(bf16[8,128,640]{2,1,0:T(8,128)(2,1)} %all-to-all-done.2.text_ref, bf16[128,640]{1,0:T(8,128)(2,1)} %c_ref.3, f32[4,640]{1,0:T(4,128)} %gains_ref.5, f32[8,128]{1,0:T(8,128)S(1)} %add.6.part_ref, f32[8,128]{1,0:T(8,128)S(1)} %collective-permute-done.1.other_ref), custom_call_target="tpu_custom_call" | custom-call | tf_op jit(solution)/shard_map/pallas_call | solution.py:244
  78.5 12.1 %all-to-all-done.1.in_ref = bf16[8,656,128]{2,1,0:T(8,128)(2,1)} async-done(((bf16[8,656,128]{2,1,0:T(8,128)(2,1)}), bf16[8,656,128]{2,1,0:T(8,128)(2,1)}, u32[]{:S(2)}, u32[]{:S(2)}) %all-to-all-start.1) | async-done | bytes 1343520 | tf_op jit(solution)/shard_map/all_to_all | solution.py:347
  90.6 3.1 %shard_map.110 = bf16[128,640]{1,0:T(8,128)(2,1)} custom-call(bf16[8,656,128]{2,1,0:T(8,128)(2,1)} %all-to-all-done.1.in_ref, f32[128,640]{1,0:T(8,128)S(1)} %shard_map.109.cross_ref, f32[1,640]{1,0:T(1,128)S(1)} %constant_dynamic-slice_fusion.gate_ref), custom_call_target="tpu_custom_call" | custom-call | tf_op jit(solution)/shard_map/pallas_call | solution.py:244
  (6 shorter events, 0.0 us)
Async XLA Ops:
  0.0 75.8 %copy-start = (f32[1000,640]{1,0:T(8,128)S(1)}, f32[1000,640]{1,0:T(8,128)}, u32[]{:S(2)}) copy-start(f32[1000,640]{1,0:T(8,128)} %param.18) | copy-start | bytes 7680004
  1.4 1.2 %collective-permute-start = (f32[8,128]{1,0:T(8,128)S(1)}, f32[8,128]{1,0:T(8,128)S(1)}, u32[]{:S(2)}, u32[]{:S(2)}) collective-permute-start(f32[8,128]{1,0:T(8,128)S(1)} %shard_map.100), channel_id=1, source_target_pairs={{0,1},{1,0},{2,3},{3,2},{4,5},{5,4},{6,7},{7,6},{8,9},{9,8},{10,11... | collective-permute-start | bytes 12296 | tf_op jit(solution)/shard_map/ppermute | solution.py:317
  2.7 3.9 %collective-permute-start.1 = (f32[8,128]{1,0:T(8,128)S(1)}, f32[8,128]{1,0:T(8,128)S(1)}, u32[]{:S(2)}, u32[]{:S(2)}) collective-permute-start(f32[8,128]{1,0:T(8,128)S(1)} %add.6.part_ref), channel_id=1, source_target_pairs={{0,2},{2,0},{1,3},{3,1},{4,6},{6,4},{5,7},{7,5},{8,10},{10,8},{9,1... | collective-permute-start | bytes 12296 | tf_op jit(solution)/shard_map/ppermute | solution.py:318
  8.4 13.9 %collective-permute-start.2 = (bf16[272,640]{1,0:T(8,128)(2,1)}, bf16[272,640]{1,0:T(8,128)(2,1)S(1)}, u32[]{:S(2)}, u32[]{:S(2)}) collective-permute-start(bf16[272,640]{1,0:T(8,128)(2,1)} %get-tuple-element.13.refs_0_), channel_id=1, source_target_pairs={{0,4},{4,8},{8,12},{12,16},{16,20},{20,24},{24,28},{28,0},{1,5},{5... | collective-permute-start | bytes 1044488 | tf_op jit(solution)/shard_map/ppermute | solution.py:298
  10.1 12.2 %collective-permute-start.3 = (bf16[272,640]{1,0:T(8,128)(2,1)}, bf16[272,640]{1,0:T(8,128)(2,1)S(1)}, u32[]{:S(2)}, u32[]{:S(2)}) collective-permute-start(bf16[272,640]{1,0:T(8,128)(2,1)} %get-tuple-element.13.refs_0_), channel_id=1, source_target_pairs={{0,28},{4,0},{8,4},{12,8},{16,12},{20,16},{24,20},{28,24},{1,29},{... | collective-permute-start | bytes 1044488 | tf_op jit(solution)/shard_map/ppermute | solution.py:298
  16.3 27.0 %all-to-all-start = ((bf16[8,128,640]{2,1,0:T(8,128)(2,1)}), bf16[8,128,640]{2,1,0:T(8,128)(2,1)}, u32[]{:S(2)}, u32[]{:S(2)}) async-start(bf16[8,128,640]{2,1,0:T(8,128)(2,1)} %shard_map.101), calls=%async_computation | async-start | bytes 2621440 | tf_op jit(solution)/shard_map/all_to_all | solution.py:330
  22.3 9.8 %copy-start.3 = (bf16[272,640]{1,0:T(8,128)(2,1)}, bf16[272,640]{1,0:T(8,128)(2,1)S(1)}, u32[]{:S(2)}) copy-start(bf16[272,640]{1,0:T(8,128)(2,1)S(1)} %get-tuple-element.14.refs_1_) | copy-start | bytes 1044484
  22.3 9.8 %copy-start.4 = (bf16[272,640]{1,0:T(8,128)(2,1)}, bf16[272,640]{1,0:T(8,128)(2,1)S(1)}, u32[]{:S(2)}) copy-start(bf16[272,640]{1,0:T(8,128)(2,1)S(1)} %get-tuple-element.15.refs_4_) | copy-start | bytes 1044484
  22.3 9.8 %collective-permute-start.4 = (bf16[272,640]{1,0:T(8,128)(2,1)S(1)}, bf16[272,640]{1,0:T(8,128)(2,1)S(1)}, u32[]{:S(2)}, u32[]{:S(2)}) collective-permute-start(bf16[272,640]{1,0:T(8,128)(2,1)S(1)} %get-tuple-element.14.refs_1_), channel_id=1, source_target_pairs={{0,4},{4,8},{8,12},{12,16},{16,20},{20,24},{24,28},{28,0},{1,5},{5... | collective-permute-start | bytes 1044488 | tf_op jit(solution)/shard_map/ppermute | solution.py:298
  22.4 13.1 %copy-start.9 = (bf16[16,640]{1,0:T(8,128)(2,1)S(1)}, bf16[16,640]{1,0:T(8,128)(2,1)}, u32[]{:S(2)}) copy-start(bf16[16,640]{1,0:T(8,128)(2,1)} %get-tuple-element.18) | copy-start | bytes 61444
  22.4 9.7 %collective-permute-start.5 = (bf16[272,640]{1,0:T(8,128)(2,1)S(1)}, bf16[272,640]{1,0:T(8,128)(2,1)S(1)}, u32[]{:S(2)}, u32[]{:S(2)}) collective-permute-start(bf16[272,640]{1,0:T(8,128)(2,1)S(1)} %get-tuple-element.15.refs_4_), channel_id=1, source_target_pairs={{0,28},{4,0},{8,4},{12,8},{16,12},{20,16},{24,20},{28,24},{1,29},{... | collective-permute-start | bytes 1044488 | tf_op jit(solution)/shard_map/ppermute | solution.py:298
  32.1 11.0 %copy-start.5 = (bf16[272,640]{1,0:T(8,128)(2,1)}, bf16[272,640]{1,0:T(8,128)(2,1)S(1)}, u32[]{:S(2)}) copy-start(bf16[272,640]{1,0:T(8,128)(2,1)S(1)} %get-tuple-element.16.refs_2_) | copy-start | bytes 1044484
  32.2 11.0 %copy-start.6 = (bf16[272,640]{1,0:T(8,128)(2,1)}, bf16[272,640]{1,0:T(8,128)(2,1)S(1)}, u32[]{:S(2)}) copy-start(bf16[272,640]{1,0:T(8,128)(2,1)S(1)} %get-tuple-element.17.refs_5_) | copy-start | bytes 1044484
  32.2 11.0 %collective-permute-start.6 = (bf16[272,640]{1,0:T(8,128)(2,1)S(1)}, bf16[272,640]{1,0:T(8,128)(2,1)S(1)}, u32[]{:S(2)}, u32[]{:S(2)}) collective-permute-start(bf16[272,640]{1,0:T(8,128)(2,1)S(1)} %get-tuple-element.16.refs_2_), channel_id=1, source_target_pairs={{0,4},{4,8},{8,12},{12,16},{16,20},{20,24},{24,28},{28,0},{1,5},{5... | collective-permute-start | bytes 1044488 | tf_op jit(solution)/shard_map/ppermute | solution.py:298
  33.2 10.0 %collective-permute-start.7 = (bf16[272,640]{1,0:T(8,128)(2,1)S(1)}, bf16[272,640]{1,0:T(8,128)(2,1)S(1)}, u32[]{:S(2)}, u32[]{:S(2)}) collective-permute-start(bf16[272,640]{1,0:T(8,128)(2,1)S(1)} %get-tuple-element.17.refs_5_), channel_id=1, source_target_pairs={{0,28},{4,0},{8,4},{12,8},{16,12},{20,16},{24,20},{28,24},{1,29},{... | collective-permute-start | bytes 1044488 | tf_op jit(solution)/shard_map/ppermute | solution.py:298
  35.5 7.7 %collective-permute-start.8 = (bf16[16,640]{1,0:T(8,128)(2,1)S(1)}, bf16[16,640]{1,0:T(8,128)(2,1)S(1)}, u32[]{:S(2)}, u32[]{:S(2)}) collective-permute-start(bf16[16,640]{1,0:T(8,128)(2,1)S(1)} %copy-done.9), channel_id=1, source_target_pairs={{0,16},{4,20},{8,24},{12,28},{16,0},{20,4},{24,8},{28,12},{1,17},{... | collective-permute-start | bytes 61448 | tf_op jit(solution)/shard_map/ppermute | solution.py:298
  43.2 0.6 copy-start.7
  43.8 0.7 copy-start.2
  44.5 1.7 %copy-start.1 = (bf16[272,640]{1,0:T(8,128)(2,1)}, bf16[272,640]{1,0:T(8,128)(2,1)S(1)}, u32[]{:S(2)}) copy-start(bf16[272,640]{1,0:T(8,128)(2,1)S(1)} %get-tuple-element.19.refs_3_) | copy-start | bytes 1044484
  44.5 10.4 %collective-permute-start.9 = (bf16[272,640]{1,0:T(8,128)(2,1)S(1)}, bf16[272,640]{1,0:T(8,128)(2,1)S(1)}, u32[]{:S(2)}, u32[]{:S(2)}) collective-permute-start(bf16[272,640]{1,0:T(8,128)(2,1)S(1)} %get-tuple-element.19.refs_3_), channel_id=1, source_target_pairs={{0,4},{4,8},{8,12},{12,16},{16,20},{20,24},{24,28},{28,0},{1,5},{5... | collective-permute-start | bytes 1044488 | tf_op jit(solution)/shard_map/ppermute | solution.py:298
  48.2 22.3 %all-to-all-start.2 = ((bf16[8,128,640]{2,1,0:T(8,128)(2,1)}), bf16[8,128,640]{2,1,0:T(8,128)(2,1)}, u32[]{:S(2)}, u32[]{:S(2)}) async-start(bf16[8,128,640]{2,1,0:T(8,128)(2,1)} %shard_map.108), calls=%async_computation.2 | async-start | bytes 2621440 | tf_op jit(solution)/shard_map/all_to_all | solution.py:343
  54.9 0.8 copy-start.8
  70.6 20.1 %all-to-all-start.1 = ((bf16[8,656,128]{2,1,0:T(8,128)(2,1)}), bf16[8,656,128]{2,1,0:T(8,128)(2,1)}, u32[]{:S(2)}, u32[]{:S(2)}) async-start(bf16[8,656,128]{2,1,0:T(8,128)(2,1)} %shard_map.107), calls=%async_computation.1 | async-start | bytes 2686976 | tf_op jit(solution)/shard_map/all_to_all | solution.py:347

commit v5 on v4

--- a/solution.py
+++ b/solution.py
@@ -18,7 +18,6 @@
 GROUP = 8
 OUT_ROWS = COLS + 16
 MIB = 1024 * 1024
-LIMIT = 60
 SPAN = 256
 PIECE = 32
 PARTS = 1024 // SPAN
@@ -61,9 +60,13 @@
     out_ref[...] = jnp.where(row == 3, text[0:1], table[0:8])
 
 
-def key_kernel(mask_ref, k_ref, v_ref, tk_ref, tv_ref, gains_ref, part_ref, other_ref, out_ref, text_out):
-    k_factor = factor_of(part_ref[1:2] + other_ref[1:2])
-    t_factor = factor_of(part_ref[3:4] + other_ref[3:4])[0:8]
+def norm_kernel(
+    mask_ref, k_ref, v_ref, tk_ref, tv_ref, q_ref, gains_ref, part_ref, other_ref, out_ref, text_out, q_out
+):
+    sums = part_ref[...] + other_ref[...]
+    q_factor = factor_of(sums[0:1])
+    k_factor = factor_of(sums[1:2])
+    t_factor = factor_of(sums[3:4])[0:8]
     row = lax.broadcasted_iota(jnp.int32, (8, ROWS), 0)
     usable = jnp.zeros((8, ROWS), jnp.int32)
     for n in range(8):
@@ -77,20 +80,16 @@
         text = jnp.concatenate([t, tv_ref[:, cols].astype(jnp.float32)], axis=0).astype(jnp.bfloat16)
         out_ref[2 * ROWS:2 * ROWS + 16, cols] = text
         text_out[:, cols] = text
+        q = (q_ref[:, cols].astype(jnp.float32) * q_factor * gains_ref[0:1, cols]).astype(jnp.bfloat16)
+        for j in range(GROUP):
+            q_out[j, :, cols] = q
     out_ref[ROWS:2 * ROWS, :] = v_ref[...]
 
 
-def query_kernel(q_ref, gains_ref, part_ref, other_ref, out_ref):
-    factor = factor_of(part_ref[0:1] + other_ref[0:1])
-    for h in range(HPD):
-        cols = slice(h * HD, (h + 1) * HD)
-        q = (q_ref[:, cols].astype(jnp.float32) * factor * gains_ref[0:1, cols]).astype(jnp.bfloat16)
-        for j in range(GROUP):
-            out_ref[j, :, cols] = q
-
-
 def text_kernel(*refs):
-    parts = [ref[...].astype(jnp.float32) for ref in refs[:8]]
+    parts = [ref[...].astype(jnp.float32) for ref in refs[:5]]
+    parts += [ref[2 * ROWS:2 * ROWS + 16, :].astype(jnp.float32) for ref in refs[5:7]]
+    parts.append(refs[7][...].astype(jnp.float32))
     out_ref = refs[8]
     keys = jnp.concatenate([part[0:8] for part in parts], axis=0).astype(jnp.bfloat16)
     values = jnp.concatenate([part[8:16] for part in parts], axis=0).astype(jnp.bfloat16)
@@ -226,17 +225,17 @@
     return pl.BlockSpec(shape, lambda i: place, pipeline_mode=pl.Buffered(buffer_count=1))
 
 
-def call(kernel, shapes, arrays, near=(), scalars=0, scratch=(), cost=None, free=()):
+def call(kernel, shapes, arrays, near=(), scalars=0, scratch=(), cost=None, free=(), limit=60):
     ins, specs = [], []
     for n, array in enumerate(arrays):
         ins.append(array if n < scalars else in_hbm(array))
         specs.append(pl.BlockSpec(memory_space=pltpu.SMEM) if n < scalars else block(array.shape))
+    for array, shape, index in free:
+        ins.append(in_hbm(array) if limit < 60 else array)
+        specs.append(block(shape, index))
     for array in near:
         ins.append(in_vmem(array))
         specs.append(VM)
-    for array, shape, index in free:
-        ins.append(array)
-        specs.append(block(shape, index))
     out_shape, out_specs = [], []
     for shape, dtype, place in shapes:
         out_shape.append(place(shape, dtype))
@@ -248,7 +247,7 @@
         in_specs=specs,
         out_specs=out_specs,
         scratch_shapes=list(scratch),
-        compiler_params=pltpu.CompilerParams(vmem_limit_bytes=LIMIT * MIB),
+        compiler_params=pltpu.CompilerParams(vmem_limit_bytes=limit * MIB),
         cost_estimate=cost,
     )(*ins)
 
@@ -259,7 +258,7 @@
         flash_kernel,
         [((GROUP, OUT_ROWS, ROWS), bf16, pltpu.HBM)],
         [queries],
-        (),
+        ring[7:],
         0,
         [
             pltpu.VMEM((1024, COLS), bf16),
@@ -273,7 +272,8 @@
             pltpu.VMEM((GROUP, ROWS, ROWS), f32),
         ],
         pl.CostEstimate(flops=15000000000, bytes_accessed=8000000, transcendentals=5242880),
-        [(array, (2 * ROWS, COLS), (0, 0)) for array in ring],
+        [(array, (2 * ROWS, COLS), (0, 0)) for array in ring[:7]],
+        40,
     )
 
 
@@ -316,17 +316,18 @@
     )
     part = sums + lax.ppermute(sums, "head", [(0, 1), (1, 0), (2, 3), (3, 2)])
     other = lax.ppermute(part, "head", [(0, 2), (2, 0), (1, 3), (3, 1)])
-    own, text_own = call(
-        key_kernel,
-        [((2 * ROWS + 16, COLS), bf16, jax.ShapeDtypeStruct), ((16, COLS), bf16, jax.ShapeDtypeStruct)],
-        [text_mask, video_key, video_value, text_key, text_value, norm_gains],
+    own, text_own, queries = call(
+        norm_kernel,
+        [
+            ((2 * ROWS + 16, COLS), bf16, jax.ShapeDtypeStruct),
+            ((16, COLS), bf16, jax.ShapeDtypeStruct),
+            ((GROUP, ROWS, COLS), bf16, pltpu.HBM),
+        ],
+        [text_mask, video_key, video_value, text_key, text_value, video_query, norm_gains],
         [part, other],
         1,
     )
     up1, down1 = gate([shift(own, 1), shift(own, -1)])
-    (queries,) = call(
-        query_kernel, [((GROUP, ROWS, COLS), bf16, pltpu.HBM)], [video_query, norm_gains], [part, other]
-    )
     queries = lax.all_to_all(queries, ("y", "xh"), 0, 0)
     up2, down2 = gate([shift(up1, 1), shift(down1, -1)], micros=2)
     text4 = shift(text_own, 4)
@@ -338,7 +339,9 @@
         text_kernel,
         [((GROUP, ROWS, COLS), bf16, pltpu.HBM)],
         [],
-        free=[(array, (16, COLS), (16, 0)) for array in ring] + [(text4, (16, COLS), (0, 0))],
+        [up3, down3, text4],
+        free=[(array, (16, COLS), (16, 0)) for array in (own, up1, up2, down1, down2)],
+        limit=16,
     )
     text = lax.all_to_all(text, ("y", "xh"), 0, 0)
 

time: 94.2 us -> 91.3 us (0.969)
  waiting for transfers between devices: 27.4 us -> 29.6 us
  local copies, waits for them, and re-layouts: 2.09 us -> 0.05 us
  Pallas kernels: 25.6 us -> 24.1 us
  starting transfers between devices: 37.7 us -> 36.3 us
    unnamed x20 -> x16, local copies, waits for them, and re-layouts: 2.08 us -> 0.03 us
    ppermute x8, waiting for transfers between devices: 9.9 us -> 11.6 us  [shift(): return lax.ppermute(array, 'z', [(i, (i + step) % 8) for i in range(8)])]
    pallas_call x7 -> x6, Pallas kernels: 25.6 us -> 24.1 us  [call(): pl.pallas_call(kernel, grid=(1,), out_shape=out_shape, in_specs=specs, ou...]
  transfers between devices with their start and end apart: 13 -> 13, of which waited for: 6 -> 7; matrix products, arithmetic and copies ran while one was open for 0% -> 0% of each run, Pallas kernels for 21% -> 19%
where the time goes in v5:
time: 91.3 us; the launch traced here: 90.8 us
  starting transfers between devices  36.3 us (40%)
  waiting for transfers between devices  29.6 us (32%)
  Pallas kernels  24.1 us (26%)
    pallas_call x6, Pallas kernels, call(): pl.pallas_call(kernel, grid=(1,), out_shape=out_shape, in_specs=specs, ou...  24.1 us
    ppermute x8, starting transfers between devices, shift(): return lax.ppermute(array, 'z', [(i, (i + step) % 8) for i in range(8)])  17.6 us
    all_to_all x1, waiting for transfers between devices, local(): received = lax.all_to_all(partial, ('y', 'xh'), 0, 0)  11.8 us
    ppermute x8, waiting for transfers between devices, shift(): return lax.ppermute(array, 'z', [(i, (i + step) % 8) for i in range(8)])  11.6 us
    all_to_all x1, starting transfers between devices, local(): queries = lax.all_to_all(queries, ('y', 'xh'), 0, 0)  6.03 us
    all_to_all x1, starting transfers between devices, local(): text = lax.all_to_all(text, ('y', 'xh'), 0, 0)  6.03 us
    all_to_all x1, starting transfers between devices, local(): received = lax.all_to_all(partial, ('y', 'xh'), 0, 0)  4.29 us
    all_to_all x1, waiting for transfers between devices, local(): text = lax.all_to_all(text, ('y', 'xh'), 0, 0)  3.39 us
  transfers between devices with their start and end apart: 13, of which 7 were waited for; matrix products, arithmetic and copies ran while one was open for 0% of the time, Pallas kernels for 19%

profile of v5, /device:TPU:2, one launch (start us, length us, event | category | flops | bytes accessed | tf_op | source)
XLA Modules:
  0.0 90.8 jit_solution(2346044408362855947)
XLA Ops:
  0.0 0.0 copy-start
  0.0 1.4 %shard_map.100 = f32[8,128]{1,0:T(8,128)S(1)} custom-call(bf16[128,640]{1,0:T(8,128)(2,1)} %q_ref.3, bf16[128,640]{1,0:T(8,128)(2,1)} %k_ref.3, bf16[128,640]{1,0:T(8,128)(2,1)} %c_ref.3, bf16[8,640]{1,0:T(8,128)(2,1)} %tk_ref.1), custom_call_target="tpu_custom_call" | custom-call | tf_op jit(solution)/shard_map/pallas_call | solution.py:243
  1.4 0.1 collective-permute-start
  1.5 1.2 %collective-permute-done = f32[8,128]{1,0:T(8,128)S(1)} collective-permute-done((f32[8,128]{1,0:T(8,128)S(1)}, f32[8,128]{1,0:T(8,128)S(1)}, u32[]{:S(2)}, u32[]{:S(2)}) %collective-permute-start) | collective-permute-done | bytes 4128 | tf_op jit(solution)/shard_map/ppermute | solution.py:317
  2.7 2.3 %collective-permute-start.1 = (f32[8,128]{1,0:T(8,128)S(1)}, f32[8,128]{1,0:T(8,128)S(1)}, u32[]{:S(2)}, u32[]{:S(2)}) collective-permute-start(f32[8,128]{1,0:T(8,128)S(1)} %add.6.part_ref), channel_id=1, source_target_pairs={{0,2},{2,0},{1,3},{3,1},{4,6},{6,4},{5,7},{7,5},{8,10},{10,8},{9,1... | collective-permute-start | bytes 12296 | tf_op jit(solution)/shard_map/ppermute | solution.py:318
  4.9 1.6 %collective-permute-done.1.other_ref = f32[8,128]{1,0:T(8,128)S(1)} collective-permute-done((f32[8,128]{1,0:T(8,128)S(1)}, f32[8,128]{1,0:T(8,128)S(1)}, u32[]{:S(2)}, u32[]{:S(2)}) %collective-permute-start.1) | collective-permute-done | bytes 4128 | tf_op jit(solution)/shard_map/ppermute | solution.py:318
  6.5 2.6 %shard_map.101 = (bf16[272,640]{1,0:T(8,128)(2,1)}, bf16[16,640]{1,0:T(8,128)(2,1)}, bf16[8,128,640]{2,1,0:T(8,128)(2,1)}) custom-call(s32[8]{0:T(128)} %mask_ref.1, bf16[128,640]{1,0:T(8,128)(2,1)} %k_ref.3, bf16[128,640]{1,0:T(8,128)(2,1)} %v_ref.1, bf16[8,640]{1,0:T(8,128)(2,1)} %tk_ref.1, bf16[8,640]{1,0:T(8,128)(2,1)} %tv_ref.1, ...), custom_call_target="tpu_custom_call" | custom-call | tf_op jit(solution)/shard_map/pallas_call | solution.py:243
  9.1 1.7 %collective-permute-start.2 = (bf16[272,640]{1,0:T(8,128)(2,1)}, bf16[272,640]{1,0:T(8,128)(2,1)S(1)}, u32[]{:S(2)}, u32[]{:S(2)}) collective-permute-start(bf16[272,640]{1,0:T(8,128)(2,1)} %get-tuple-element.15.refs_0_), channel_id=1, source_target_pairs={{0,4},{4,8},{8,12},{12,16},{16,20},{20,24},{24,28},{28,0},{1,5},{5... | collective-permute-start | bytes 1044488 | tf_op jit(solution)/shard_map/ppermute | solution.py:298
  10.8 3.9 %collective-permute-start.3 = (bf16[272,640]{1,0:T(8,128)(2,1)}, bf16[272,640]{1,0:T(8,128)(2,1)S(1)}, u32[]{:S(2)}, u32[]{:S(2)}) collective-permute-start(bf16[272,640]{1,0:T(8,128)(2,1)} %get-tuple-element.15.refs_0_), channel_id=1, source_target_pairs={{0,28},{4,0},{8,4},{12,8},{16,12},{20,16},{24,20},{28,24},{1,29},{... | collective-permute-start | bytes 1044488 | tf_op jit(solution)/shard_map/ppermute | solution.py:298
  14.7 6.0 %all-to-all-start = ((bf16[8,128,640]{2,1,0:T(8,128)(2,1)}), bf16[8,128,640]{2,1,0:T(8,128)(2,1)}, u32[]{:S(2)}, u32[]{:S(2)}) async-start(bf16[8,128,640]{2,1,0:T(8,128)(2,1)} %get-tuple-element.14), calls=%async_computation | async-start | bytes 2621440 | tf_op jit(solution)/shard_map/all_to_all | solution.py:331
  20.8 1.5 %collective-permute-done.2.refs_0_ = bf16[272,640]{1,0:T(8,128)(2,1)S(1)} collective-permute-done((bf16[272,640]{1,0:T(8,128)(2,1)}, bf16[272,640]{1,0:T(8,128)(2,1)S(1)}, u32[]{:S(2)}, u32[]{:S(2)}) %collective-permute-start.2) | collective-permute-done | bytes 348192 | tf_op jit(solution)/shard_map/ppermute | solution.py:298
  22.3 0.0 collective-permute-done.3.refs_1_
  22.3 0.0 copy-start.3
  22.3 0.0 copy-start.4
  22.3 0.1 collective-permute-start.4
  22.4 0.0 copy-start.7
  22.4 3.2 %collective-permute-start.5 = (bf16[272,640]{1,0:T(8,128)(2,1)S(1)}, bf16[272,640]{1,0:T(8,128)(2,1)S(1)}, u32[]{:S(2)}, u32[]{:S(2)}) collective-permute-start(bf16[272,640]{1,0:T(8,128)(2,1)S(1)} %get-tuple-element.17.refs_4_.refs_3_), channel_id=1, source_target_pairs={{0,28},{4,0},{8,4},{12,8},{16,12},{20,16},{24,20},{28,24},{1,29},{... | collective-permute-start | bytes 1044488 | tf_op jit(solution)/shard_map/ppermute | solution.py:298
  25.6 6.4 %collective-permute-done.4.refs_0_ = bf16[272,640]{1,0:T(8,128)(2,1)S(1)} collective-permute-done((bf16[272,640]{1,0:T(8,128)(2,1)S(1)}, bf16[272,640]{1,0:T(8,128)(2,1)S(1)}, u32[]{:S(2)}, u32[]{:S(2)}) %collective-permute-start.4) | collective-permute-done | bytes 348192 | tf_op jit(solution)/shard_map/ppermute | solution.py:298
  32.0 0.0 collective-permute-done.5.refs_1_
  32.0 0.0 copy-done.3
  32.0 0.0 copy-done.4
  32.0 0.0 copy-start.5
  32.0 0.0 copy-start.6
  32.0 1.9 %collective-permute-start.6 = (bf16[272,640]{1,0:T(8,128)(2,1)S(1)}, bf16[272,640]{1,0:T(8,128)(2,1)S(1)}, u32[]{:S(2)}, u32[]{:S(2)}) collective-permute-start(bf16[272,640]{1,0:T(8,128)(2,1)S(1)} %get-tuple-element.18.refs_2_), channel_id=1, source_target_pairs={{0,4},{4,8},{8,12},{12,16},{16,20},{20,24},{24,28},{28,0},{1,5},{5... | collective-permute-start | bytes 1044488 | tf_op jit(solution)/shard_map/ppermute | solution.py:298
  33.9 1.4 %collective-permute-start.7 = (bf16[272,640]{1,0:T(8,128)(2,1)S(1)}, bf16[272,640]{1,0:T(8,128)(2,1)S(1)}, u32[]{:S(2)}, u32[]{:S(2)}) collective-permute-start(bf16[272,640]{1,0:T(8,128)(2,1)S(1)} %get-tuple-element.19.refs_5_.refs_4_), channel_id=1, source_target_pairs={{0,28},{4,0},{8,4},{12,8},{16,12},{20,16},{24,20},{28,24},{1,29},{... | collective-permute-start | bytes 1044488 | tf_op jit(solution)/shard_map/ppermute | solution.py:298
  35.4 0.0 copy-done.7
  35.4 4.0 %collective-permute-start.8 = (bf16[16,640]{1,0:T(8,128)(2,1)S(1)}, bf16[16,640]{1,0:T(8,128)(2,1)S(1)}, u32[]{:S(2)}, u32[]{:S(2)}) collective-permute-start(bf16[16,640]{1,0:T(8,128)(2,1)S(1)} %copy-done.7), channel_id=1, source_target_pairs={{0,16},{4,20},{8,24},{12,28},{16,0},{20,4},{24,8},{28,12},{1,17},{... | collective-permute-start | bytes 61448 | tf_op jit(solution)/shard_map/ppermute | solution.py:298
  39.4 3.7 %collective-permute-done.8.refs_3_.refs_7_ = bf16[16,640]{1,0:T(8,128)(2,1)S(1)} collective-permute-done((bf16[16,640]{1,0:T(8,128)(2,1)S(1)}, bf16[16,640]{1,0:T(8,128)(2,1)S(1)}, u32[]{:S(2)}, u32[]{:S(2)}) %collective-permute-start.8) | collective-permute-done | bytes 20512 | tf_op jit(solution)/shard_map/ppermute | solution.py:298
  43.1 0.0 collective-permute-done.6.refs_0_
  43.1 0.0 copy-done.5
  43.1 0.0 copy-done.6
  43.1 0.0 collective-permute-done.7.refs_1_
  43.1 0.0 all-to-all-done.refs_2_.q_ref
  43.1 0.0 copy-start.1
  43.1 0.0 copy-start.2
  43.1 1.4 %collective-permute-start.9 = (bf16[272,640]{1,0:T(8,128)(2,1)S(1)}, bf16[272,640]{1,0:T(8,128)(2,1)}, u32[]{:S(2)}, u32[]{:S(2)}) collective-permute-start(bf16[272,640]{1,0:T(8,128)(2,1)S(1)} %get-tuple-element.21.refs_3_.refs_5_), channel_id=1, source_target_pairs={{0,4},{4,8},{8,12},{12,16},{16,20},{20,24},{24,28},{28,0},{1,5},{5... | collective-permute-start | bytes 1044488 | tf_op jit(solution)/shard_map/ppermute | solution.py:298
  44.5 2.0 %shard_map.107 = bf16[8,128,640]{2,1,0:T(8,128)(2,1)} custom-call(bf16[272,640]{1,0:T(8,128)(2,1)} %get-tuple-element.15.refs_0_, bf16[272,640]{1,0:T(8,128)(2,1)} %copy-done.3, bf16[272,640]{1,0:T(8,128)(2,1)} %copy-done.5, bf16[272,640]{1,0:T(8,128)(2,1)} %copy-done.4, bf16[272,640]{1,0:T(8,128)(2,1)} %copy-done.6, ...), custom_call_target="tpu_custom_call" | custom-call | tf_op jit(solution)/shard_map/pallas_call | solution.py:243
  46.5 0.0 copy-done.1
  46.5 0.0 copy-done.2
  46.5 6.0 %all-to-all-start.2 = ((bf16[8,128,640]{2,1,0:T(8,128)(2,1)}), bf16[8,128,640]{2,1,0:T(8,128)(2,1)}, u32[]{:S(2)}, u32[]{:S(2)}) async-start(bf16[8,128,640]{2,1,0:T(8,128)(2,1)} %shard_map.107), calls=%async_computation.2 | async-start | bytes 2621440 | tf_op jit(solution)/shard_map/all_to_all | solution.py:346
  52.5 0.0 collective-permute-done.9.refs_0_
  52.5 12.4 %shard_map.106 = bf16[8,656,128]{2,1,0:T(8,128)(2,1)} custom-call(bf16[8,128,640]{2,1,0:T(8,128)(2,1)} %all-to-all-done.refs_2_.q_ref, bf16[272,640]{1,0:T(8,128)(2,1)} %get-tuple-element.15.refs_0_, bf16[272,640]{1,0:T(8,128)(2,1)} %copy-done.3, bf16[272,640]{1,0:T(8,128)(2,1)} %copy-done.5, bf16[272,640]{1,0:T(8,128)(2,1)} %copy-done.1, ...), custom_call_target="tpu_custom_call" | custom-call | flops 15000000512 | bytes 8000000 | tf_op jit(solution)/shard_map/pallas_call | solution.py:243
  64.9 3.4 %all-to-all-done.2.text_ref = bf16[8,128,640]{2,1,0:T(8,128)(2,1)} async-done(((bf16[8,128,640]{2,1,0:T(8,128)(2,1)}), bf16[8,128,640]{2,1,0:T(8,128)(2,1)}, u32[]{:S(2)}, u32[]{:S(2)}) %all-to-all-start.2) | async-done | bytes 1310752 | tf_op jit(solution)/shard_map/all_to_all | solution.py:346
  68.3 4.3 %all-to-all-start.1 = ((bf16[8,656,128]{2,1,0:T(8,128)(2,1)}), bf16[8,656,128]{2,1,0:T(8,128)(2,1)}, u32[]{:S(2)}, u32[]{:S(2)}) async-start(bf16[8,656,128]{2,1,0:T(8,128)(2,1)} %shard_map.106), calls=%async_computation.1 | async-start | bytes 2686976 | tf_op jit(solution)/shard_map/all_to_all | solution.py:350
  73.2 0.0 copy-done
  73.3 2.7 %shard_map.108.cross_ref = f32[128,640]{1,0:T(8,128)S(1)} custom-call(bf16[8,128,640]{2,1,0:T(8,128)(2,1)} %all-to-all-done.2.text_ref, bf16[128,640]{1,0:T(8,128)(2,1)} %c_ref.3, f32[4,640]{1,0:T(4,128)} %gains_ref.3, f32[8,128]{1,0:T(8,128)S(1)} %add.6.part_ref, f32[8,128]{1,0:T(8,128)S(1)} %collective-permute-done.1.other_ref), custom_call_target="tpu_custom_call" | custom-call | tf_op jit(solution)/shard_map/pallas_call | solution.py:243
  75.9 11.8 %all-to-all-done.1.in_ref = bf16[8,656,128]{2,1,0:T(8,128)(2,1)} async-done(((bf16[8,656,128]{2,1,0:T(8,128)(2,1)}), bf16[8,656,128]{2,1,0:T(8,128)(2,1)}, u32[]{:S(2)}, u32[]{:S(2)}) %all-to-all-start.1) | async-done | bytes 1343520 | tf_op jit(solution)/shard_map/all_to_all | solution.py:350
  87.8 3.1 %shard_map.109 = bf16[128,640]{1,0:T(8,128)(2,1)} custom-call(bf16[8,656,128]{2,1,0:T(8,128)(2,1)} %all-to-all-done.1.in_ref, f32[128,640]{1,0:T(8,128)S(1)} %shard_map.108.cross_ref, f32[1,640]{1,0:T(1,128)S(1)} %constant_dynamic-slice_fusion.gate_ref), custom_call_target="tpu_custom_call" | custom-call | tf_op jit(solution)/shard_map/pallas_call | solution.py:243
  (6 shorter events, 0.0 us)
Async XLA Ops:
  0.0 73.2 %copy-start = (f32[1000,640]{1,0:T(8,128)S(1)}, f32[1000,640]{1,0:T(8,128)}, u32[]{:S(2)}) copy-start(f32[1000,640]{1,0:T(8,128)} %param.18) | copy-start | bytes 7680004
  1.4 1.2 %collective-permute-start = (f32[8,128]{1,0:T(8,128)S(1)}, f32[8,128]{1,0:T(8,128)S(1)}, u32[]{:S(2)}, u32[]{:S(2)}) collective-permute-start(f32[8,128]{1,0:T(8,128)S(1)} %shard_map.100), channel_id=1, source_target_pairs={{0,1},{1,0},{2,3},{3,2},{4,5},{5,4},{6,7},{7,6},{8,9},{9,8},{10,11... | collective-permute-start | bytes 12296 | tf_op jit(solution)/shard_map/ppermute | solution.py:317
  2.7 3.9 %collective-permute-start.1 = (f32[8,128]{1,0:T(8,128)S(1)}, f32[8,128]{1,0:T(8,128)S(1)}, u32[]{:S(2)}, u32[]{:S(2)}) collective-permute-start(f32[8,128]{1,0:T(8,128)S(1)} %add.6.part_ref), channel_id=1, source_target_pairs={{0,2},{2,0},{1,3},{3,1},{4,6},{6,4},{5,7},{7,5},{8,10},{10,8},{9,1... | collective-permute-start | bytes 12296 | tf_op jit(solution)/shard_map/ppermute | solution.py:318
  9.1 13.1 %collective-permute-start.2 = (bf16[272,640]{1,0:T(8,128)(2,1)}, bf16[272,640]{1,0:T(8,128)(2,1)S(1)}, u32[]{:S(2)}, u32[]{:S(2)}) collective-permute-start(bf16[272,640]{1,0:T(8,128)(2,1)} %get-tuple-element.15.refs_0_), channel_id=1, source_target_pairs={{0,4},{4,8},{8,12},{12,16},{16,20},{20,24},{24,28},{28,0},{1,5},{5... | collective-permute-start | bytes 1044488 | tf_op jit(solution)/shard_map/ppermute | solution.py:298
  10.8 11.5 %collective-permute-start.3 = (bf16[272,640]{1,0:T(8,128)(2,1)}, bf16[272,640]{1,0:T(8,128)(2,1)S(1)}, u32[]{:S(2)}, u32[]{:S(2)}) collective-permute-start(bf16[272,640]{1,0:T(8,128)(2,1)} %get-tuple-element.15.refs_0_), channel_id=1, source_target_pairs={{0,28},{4,0},{8,4},{12,8},{16,12},{20,16},{24,20},{28,24},{1,29},{... | collective-permute-start | bytes 1044488 | tf_op jit(solution)/shard_map/ppermute | solution.py:298
  14.7 28.3 %all-to-all-start = ((bf16[8,128,640]{2,1,0:T(8,128)(2,1)}), bf16[8,128,640]{2,1,0:T(8,128)(2,1)}, u32[]{:S(2)}, u32[]{:S(2)}) async-start(bf16[8,128,640]{2,1,0:T(8,128)(2,1)} %get-tuple-element.14), calls=%async_computation | async-start | bytes 2621440 | tf_op jit(solution)/shard_map/all_to_all | solution.py:331
  22.3 9.7 %copy-start.3 = (bf16[272,640]{1,0:T(8,128)(2,1)}, bf16[272,640]{1,0:T(8,128)(2,1)S(1)}, u32[]{:S(2)}) copy-start(bf16[272,640]{1,0:T(8,128)(2,1)S(1)} %get-tuple-element.16.refs_1_) | copy-start | bytes 1044484
  22.3 9.7 %copy-start.4 = (bf16[272,640]{1,0:T(8,128)(2,1)}, bf16[272,640]{1,0:T(8,128)(2,1)S(1)}, u32[]{:S(2)}) copy-start(bf16[272,640]{1,0:T(8,128)(2,1)S(1)} %get-tuple-element.17.refs_4_.refs_3_) | copy-start | bytes 1044484
  22.3 9.7 %collective-permute-start.4 = (bf16[272,640]{1,0:T(8,128)(2,1)S(1)}, bf16[272,640]{1,0:T(8,128)(2,1)S(1)}, u32[]{:S(2)}, u32[]{:S(2)}) collective-permute-start(bf16[272,640]{1,0:T(8,128)(2,1)S(1)} %get-tuple-element.16.refs_1_), channel_id=1, source_target_pairs={{0,4},{4,8},{8,12},{12,16},{16,20},{20,24},{24,28},{28,0},{1,5},{5... | collective-permute-start | bytes 1044488 | tf_op jit(solution)/shard_map/ppermute | solution.py:298
  22.4 13.0 %copy-start.7 = (bf16[16,640]{1,0:T(8,128)(2,1)S(1)}, bf16[16,640]{1,0:T(8,128)(2,1)}, u32[]{:S(2)}) copy-start(bf16[16,640]{1,0:T(8,128)(2,1)} %get-tuple-element.20) | copy-start | bytes 61444
  22.4 9.6 %collective-permute-start.5 = (bf16[272,640]{1,0:T(8,128)(2,1)S(1)}, bf16[272,640]{1,0:T(8,128)(2,1)S(1)}, u32[]{:S(2)}, u32[]{:S(2)}) collective-permute-start(bf16[272,640]{1,0:T(8,128)(2,1)S(1)} %get-tuple-element.17.refs_4_.refs_3_), channel_id=1, source_target_pairs={{0,28},{4,0},{8,4},{12,8},{16,12},{20,16},{24,20},{28,24},{1,29},{... | collective-permute-start | bytes 1044488 | tf_op jit(solution)/shard_map/ppermute | solution.py:298
  32.0 11.0 %copy-start.5 = (bf16[272,640]{1,0:T(8,128)(2,1)}, bf16[272,640]{1,0:T(8,128)(2,1)S(1)}, u32[]{:S(2)}) copy-start(bf16[272,640]{1,0:T(8,128)(2,1)S(1)} %get-tuple-element.18.refs_2_) | copy-start | bytes 1044484
  32.0 11.0 %copy-start.6 = (bf16[272,640]{1,0:T(8,128)(2,1)}, bf16[272,640]{1,0:T(8,128)(2,1)S(1)}, u32[]{:S(2)}) copy-start(bf16[272,640]{1,0:T(8,128)(2,1)S(1)} %get-tuple-element.19.refs_5_.refs_4_) | copy-start | bytes 1044484
  32.0 11.0 %collective-permute-start.6 = (bf16[272,640]{1,0:T(8,128)(2,1)S(1)}, bf16[272,640]{1,0:T(8,128)(2,1)S(1)}, u32[]{:S(2)}, u32[]{:S(2)}) collective-permute-start(bf16[272,640]{1,0:T(8,128)(2,1)S(1)} %get-tuple-element.18.refs_2_), channel_id=1, source_target_pairs={{0,4},{4,8},{8,12},{12,16},{16,20},{20,24},{24,28},{28,0},{1,5},{5... | collective-permute-start | bytes 1044488 | tf_op jit(solution)/shard_map/ppermute | solution.py:298
  33.9 9.1 %collective-permute-start.7 = (bf16[272,640]{1,0:T(8,128)(2,1)S(1)}, bf16[272,640]{1,0:T(8,128)(2,1)S(1)}, u32[]{:S(2)}, u32[]{:S(2)}) collective-permute-start(bf16[272,640]{1,0:T(8,128)(2,1)S(1)} %get-tuple-element.19.refs_5_.refs_4_), channel_id=1, source_target_pairs={{0,28},{4,0},{8,4},{12,8},{16,12},{20,16},{24,20},{28,24},{1,29},{... | collective-permute-start | bytes 1044488 | tf_op jit(solution)/shard_map/ppermute | solution.py:298
  35.4 7.7 %collective-permute-start.8 = (bf16[16,640]{1,0:T(8,128)(2,1)S(1)}, bf16[16,640]{1,0:T(8,128)(2,1)S(1)}, u32[]{:S(2)}, u32[]{:S(2)}) collective-permute-start(bf16[16,640]{1,0:T(8,128)(2,1)S(1)} %copy-done.7), channel_id=1, source_target_pairs={{0,16},{4,20},{8,24},{12,28},{16,0},{20,4},{24,8},{28,12},{1,17},{... | collective-permute-start | bytes 61448 | tf_op jit(solution)/shard_map/ppermute | solution.py:298
  43.1 3.4 %copy-start.1 = (bf16[272,640]{1,0:T(8,128)(2,1)}, bf16[272,640]{1,0:T(8,128)(2,1)S(1)}, u32[]{:S(2)}) copy-start(bf16[272,640]{1,0:T(8,128)(2,1)S(1)} %get-tuple-element.21.refs_3_.refs_5_) | copy-start | bytes 1044484
  43.1 3.4 %copy-start.2 = (bf16[272,640]{1,0:T(8,128)(2,1)}, bf16[272,640]{1,0:T(8,128)(2,1)S(1)}, u32[]{:S(2)}) copy-start(bf16[272,640]{1,0:T(8,128)(2,1)S(1)} %get-tuple-element.22.refs_6_) | copy-start | bytes 1044484
  43.1 9.4 %collective-permute-start.9 = (bf16[272,640]{1,0:T(8,128)(2,1)S(1)}, bf16[272,640]{1,0:T(8,128)(2,1)}, u32[]{:S(2)}, u32[]{:S(2)}) collective-permute-start(bf16[272,640]{1,0:T(8,128)(2,1)S(1)} %get-tuple-element.21.refs_3_.refs_5_), channel_id=1, source_target_pairs={{0,4},{4,8},{8,12},{12,16},{16,20},{20,24},{24,28},{28,0},{1,5},{5... | collective-permute-start | bytes 1044488 | tf_op jit(solution)/shard_map/ppermute | solution.py:298
  46.5 21.8 %all-to-all-start.2 = ((bf16[8,128,640]{2,1,0:T(8,128)(2,1)}), bf16[8,128,640]{2,1,0:T(8,128)(2,1)}, u32[]{:S(2)}, u32[]{:S(2)}) async-start(bf16[8,128,640]{2,1,0:T(8,128)(2,1)} %shard_map.107), calls=%async_computation.2 | async-start | bytes 2621440 | tf_op jit(solution)/shard_map/all_to_all | solution.py:346
  68.3 19.5 %all-to-all-start.1 = ((bf16[8,656,128]{2,1,0:T(8,128)(2,1)}), bf16[8,656,128]{2,1,0:T(8,128)(2,1)}, u32[]{:S(2)}, u32[]{:S(2)}) async-start(bf16[8,656,128]{2,1,0:T(8,128)(2,1)} %shard_map.106), calls=%async_computation.1 | async-start | bytes 2686976 | tf_op jit(solution)/shard_map/all_to_all | solution.py:350

commit v6 on v5

--- a/solution.py
+++ b/solution.py
@@ -61,7 +61,7 @@
 
 
 def norm_kernel(
-    mask_ref, k_ref, v_ref, tk_ref, tv_ref, q_ref, gains_ref, part_ref, other_ref, out_ref, text_out, q_out
+    mask_ref, k_ref, v_ref, tk_ref, tv_ref, q_ref, gains_ref, part_ref, other_ref, out_ref, q_out
 ):
     sums = part_ref[...] + other_ref[...]
     q_factor = factor_of(sums[0:1])
@@ -79,23 +79,33 @@
         t = jnp.where(usable > 0, t, PAD_MARK)
         text = jnp.concatenate([t, tv_ref[:, cols].astype(jnp.float32)], axis=0).astype(jnp.bfloat16)
         out_ref[2 * ROWS:2 * ROWS + 16, cols] = text
-        text_out[:, cols] = text
         q = (q_ref[:, cols].astype(jnp.float32) * q_factor * gains_ref[0:1, cols]).astype(jnp.bfloat16)
         for j in range(GROUP):
             q_out[j, :, cols] = q
     out_ref[ROWS:2 * ROWS, :] = v_ref[...]
 
 
-def text_kernel(*refs):
-    parts = [ref[...].astype(jnp.float32) for ref in refs[:5]]
-    parts += [ref[2 * ROWS:2 * ROWS + 16, :].astype(jnp.float32) for ref in refs[5:7]]
-    parts.append(refs[7][...].astype(jnp.float32))
-    out_ref = refs[8]
-    keys = jnp.concatenate([part[0:8] for part in parts], axis=0).astype(jnp.bfloat16)
-    values = jnp.concatenate([part[8:16] for part in parts], axis=0).astype(jnp.bfloat16)
+def pick_kernel(own_ref, near_up_ref, near_down_ref, down_ref, up_ref, picked_ref, pass_ref):
+    parts = [ref[...].astype(jnp.float32) for ref in (own_ref, near_up_ref, near_down_ref, down_ref)]
+    up = up_ref[...]
+    pass_ref[...] = up
+    parts.append(up.astype(jnp.float32))
+    parts.append(jnp.zeros_like(parts[0]))
+    picked_ref[0:48, :] = jnp.concatenate([part[0:8] for part in parts], axis=0).astype(jnp.bfloat16)
+    picked_ref[48:96, :] = jnp.concatenate([part[8:16] for part in parts], axis=0).astype(jnp.bfloat16)
+
+
+def text_kernel(picked_ref, far_ref, up_ref, down_ref, out_ref):
+    parts = [far_ref[...].astype(jnp.float32)]
+    for ref in (up_ref, down_ref):
+        parts.append(ref[2 * ROWS:2 * ROWS + 16, :].astype(jnp.float32))
+    keys = jnp.concatenate([picked_ref[32:48, :].astype(jnp.float32)[0:8]] + [part[0:8] for part in parts], axis=0)
+    values = jnp.concatenate([picked_ref[80:96, :].astype(jnp.float32)[0:8]] + [part[8:16] for part in parts], axis=0)
     for j in range(GROUP):
-        out_ref[j, 0:64, :] = keys
-        out_ref[j, 64:128, :] = values
+        out_ref[j, 0:32, :] = picked_ref[0:32, :]
+        out_ref[j, 32:64, :] = keys.astype(jnp.bfloat16)
+        out_ref[j, 64:96, :] = picked_ref[48:80, :]
+        out_ref[j, 96:128, :] = values.astype(jnp.bfloat16)
 
 
 def unit_place(unit):
@@ -146,9 +156,9 @@
 
     def blend(unit, p_ref, i_ref):
         head, first, cols = unit_place(unit)
-        o = (dot(p_ref[...], v_s[:, cols], 1, 0) * i_ref[...]).astype(jnp.bfloat16)
+        o = (dot(p_ref[...], v_s[:, cols], 1, 0) * i_ref[...]).T.astype(jnp.bfloat16)
         for n in range(SPAN // ROWS):
-            out_ref[first + n, pl.ds(pl.multiple_of(head * HD, HD), HD), :] = o[n * ROWS:(n + 1) * ROWS]
+            out_ref[first + n, pl.ds(pl.multiple_of(head * HD, HD), HD), :] = o[:, n * ROWS:(n + 1) * ROWS]
 
     def phase(unit, s_next, s_now, p_now, i_now, p_last, i_last):
         blend(unit - 1, p_last, i_last)
@@ -204,12 +214,10 @@
         for share in shares[1:]:
             total = total + share
         inverse = 1.0 / total
-        shares = jnp.concatenate([share * inverse for share in shares], axis=0)
-        shares = jnp.concatenate([shares, jnp.zeros((ROWS - GROUP, ROWS), jnp.float32)], axis=0).T
-        own = jnp.zeros((ROWS, HD), jnp.float32)
+        own = jnp.zeros((HD, ROWS), jnp.float32)
         for j in range(GROUP):
-            own = own + in_ref[j, h * HD:(h + 1) * HD, :].astype(jnp.float32) * shares[:, j:j + 1]
-        out_ref[:, cols] = (gate_ref[:, cols] * own + cross_ref[:, cols]).astype(jnp.bfloat16)
+            own = own + in_ref[j, h * HD:(h + 1) * HD, :].astype(jnp.float32) * (shares[j] * inverse)
+        out_ref[:, cols] = (gate_ref[:, cols] * own.T + cross_ref[:, cols]).astype(jnp.bfloat16)
 
 
 def in_hbm(array):
@@ -316,11 +324,10 @@
     )
     part = sums + lax.ppermute(sums, "head", [(0, 1), (1, 0), (2, 3), (3, 2)])
     other = lax.ppermute(part, "head", [(0, 2), (2, 0), (1, 3), (3, 1)])
-    own, text_own, queries = call(
+    own, queries = call(
         norm_kernel,
         [
             ((2 * ROWS + 16, COLS), bf16, jax.ShapeDtypeStruct),
-            ((16, COLS), bf16, jax.ShapeDtypeStruct),
             ((GROUP, ROWS, COLS), bf16, pltpu.HBM),
         ],
         [text_mask, video_key, video_value, text_key, text_value, video_query, norm_gains],
@@ -330,18 +337,21 @@
     up1, down1 = gate([shift(own, 1), shift(own, -1)])
     queries = lax.all_to_all(queries, ("y", "xh"), 0, 0)
     up2, down2 = gate([shift(up1, 1), shift(down1, -1)], micros=2)
-    text4 = shift(text_own, 4)
+    picked, passing = call(
+        pick_kernel,
+        [((96, COLS), bf16, jax.ShapeDtypeStruct), ((16, COLS), bf16, jax.ShapeDtypeStruct)],
+        [],
+        [],
+        limit=16,
+        free=[(array, (16, COLS), (16, 0)) for array in (own, up1, down1, down2, up2)],
+    )
+    text4 = shift(passing, 2)
     up3, down3 = gate([shift(up2, 1), shift(down2, -1)], after=[queries, text4], micros=2)
     (far,) = gate([shift(up3, 1)])
 
     ring = [own, up1, up2, up3, down1, down2, down3]
     (text,) = call(
-        text_kernel,
-        [((GROUP, ROWS, COLS), bf16, pltpu.HBM)],
-        [],
-        [up3, down3, text4],
-        free=[(array, (16, COLS), (16, 0)) for array in (own, up1, up2, down1, down2)],
-        limit=16,
+        text_kernel, [((GROUP, ROWS, COLS), bf16, pltpu.HBM)], [], [picked, text4, up3, down3], limit=16
     )
     text = lax.all_to_all(text, ("y", "xh"), 0, 0)
 

time: 91.3 us -> 90 us (0.986)
  starting transfers between devices: 36.3 us -> 33.5 us
  waiting for transfers between devices: 29.6 us -> 30.6 us
    ppermute x8, starting transfers between devices: 17.6 us -> 14.5 us  [shift(): return lax.ppermute(array, 'z', [(i, (i + step) % 8) for i in range(8)])]
    ppermute x8, waiting for transfers between devices: 11.6 us -> 13.8 us  [shift(): return lax.ppermute(array, 'z', [(i, (i + step) % 8) for i in range(8)])]
    all_to_all x1, waiting for transfers between devices: 3.39 us -> 1.79 us  [local(): text = lax.all_to_all(text, ('y', 'xh'), 0, 0)]
    pallas_call x6 -> x7, Pallas kernels: 24.1 us -> 24.3 us  [call(): pl.pallas_call(kernel, grid=(1,), out_shape=out_shape, in_specs=specs, ou...]
  transfers between devices with their start and end apart: 13 -> 13, of which waited for: 7 -> 8; matrix products, arithmetic and copies ran while one was open for 0% -> 0% of each run, Pallas kernels for 19% -> 20%
where the time goes in v6:
time: 90 us; the launch traced here: 89.2 us
  starting transfers between devices  33.5 us (37%)
  waiting for transfers between devices  30.6 us (34%)
  Pallas kernels  24.3 us (27%)
    pallas_call x7, Pallas kernels, call(): pl.pallas_call(kernel, grid=(1,), out_shape=out_shape, in_specs=specs, ou...  24.3 us
    ppermute x8, starting transfers between devices, shift(): return lax.ppermute(array, 'z', [(i, (i + step) % 8) for i in range(8)])  14.5 us
    ppermute x8, waiting for transfers between devices, shift(): return lax.ppermute(array, 'z', [(i, (i + step) % 8) for i in range(8)])  13.8 us
    all_to_all x1, waiting for transfers between devices, local(): received = lax.all_to_all(partial, ('y', 'xh'), 0, 0)  12.3 us
    all_to_all x1, starting transfers between devices, local(): text = lax.all_to_all(text, ('y', 'xh'), 0, 0)  6.05 us
    all_to_all x1, starting transfers between devices, local(): queries = lax.all_to_all(queries, ('y', 'xh'), 0, 0)  6.03 us
    all_to_all x1, starting transfers between devices, local(): received = lax.all_to_all(partial, ('y', 'xh'), 0, 0)  4.55 us
    ppermute x1, starting transfers between devices, local(): other = lax.ppermute(part, 'head', [(0, 2), (2, 0), (1, 3), (3, 1)])  2.27 us
  transfers between devices with their start and end apart: 13, of which 8 were waited for; matrix products, arithmetic and copies ran while one was open for 0% of the time, Pallas kernels for 20%

profile of v6, /device:TPU:2, one launch (start us, length us, event | category | flops | bytes accessed | tf_op | source)
XLA Modules:
  0.0 89.2 jit_solution(8930378082339360298)
XLA Ops:
  0.0 0.0 copy-start
  0.0 1.4 %shard_map.100 = f32[8,128]{1,0:T(8,128)S(1)} custom-call(bf16[128,640]{1,0:T(8,128)(2,1)} %q_ref.3, bf16[128,640]{1,0:T(8,128)(2,1)} %k_ref.3, bf16[128,640]{1,0:T(8,128)(2,1)} %c_ref.3, bf16[8,640]{1,0:T(8,128)(2,1)} %tk_ref.1), custom_call_target="tpu_custom_call" | custom-call | tf_op jit(solution)/shard_map/pallas_call | solution.py:251
  1.4 0.1 collective-permute-start
  1.5 1.2 %collective-permute-done = f32[8,128]{1,0:T(8,128)S(1)} collective-permute-done((f32[8,128]{1,0:T(8,128)S(1)}, f32[8,128]{1,0:T(8,128)S(1)}, u32[]{:S(2)}, u32[]{:S(2)}) %collective-permute-start) | collective-permute-done | bytes 4128 | tf_op jit(solution)/shard_map/ppermute | solution.py:325
  2.7 2.3 %collective-permute-start.1 = (f32[8,128]{1,0:T(8,128)S(1)}, f32[8,128]{1,0:T(8,128)S(1)}, u32[]{:S(2)}, u32[]{:S(2)}) collective-permute-start(f32[8,128]{1,0:T(8,128)S(1)} %add.6.part_ref), channel_id=1, source_target_pairs={{0,2},{2,0},{1,3},{3,1},{4,6},{6,4},{5,7},{7,5},{8,10},{10,8},{9,1... | collective-permute-start | bytes 12296 | tf_op jit(solution)/shard_map/ppermute | solution.py:326
  4.9 1.6 %collective-permute-done.1.other_ref = f32[8,128]{1,0:T(8,128)S(1)} collective-permute-done((f32[8,128]{1,0:T(8,128)S(1)}, f32[8,128]{1,0:T(8,128)S(1)}, u32[]{:S(2)}, u32[]{:S(2)}) %collective-permute-start.1) | collective-permute-done | bytes 4128 | tf_op jit(solution)/shard_map/ppermute | solution.py:326
  6.5 2.6 %shard_map.101 = (bf16[272,640]{1,0:T(8,128)(2,1)}, bf16[8,128,640]{2,1,0:T(8,128)(2,1)}) custom-call(s32[8]{0:T(128)} %mask_ref.1, bf16[128,640]{1,0:T(8,128)(2,1)} %k_ref.3, bf16[128,640]{1,0:T(8,128)(2,1)} %v_ref.1, bf16[8,640]{1,0:T(8,128)(2,1)} %tk_ref.1, bf16[8,640]{1,0:T(8,128)(2,1)} %tv_ref.1, bf16[128,640]{1,0:T(8,128)(2,1)} %q_ref.3, ...), custom_call_target="tpu_custom_call" | custom-call | tf_op jit(solution)/shard_map/pallas_call | solution.py:251
  9.1 1.7 %collective-permute-start.2 = (bf16[272,640]{1,0:T(8,128)(2,1)}, bf16[272,640]{1,0:T(8,128)(2,1)S(1)}, u32[]{:S(2)}, u32[]{:S(2)}) collective-permute-start(bf16[272,640]{1,0:T(8,128)(2,1)} %get-tuple-element.16.own_ref.refs_0_), channel_id=1, source_target_pairs={{0,4},{4,8},{8,12},{12,16},{16,20},{20,24},{24,28},{28,0},{1,5},{5... | collective-permute-start | bytes 1044488 | tf_op jit(solution)/shard_map/ppermute | solution.py:306
  10.8 3.9 %collective-permute-start.3 = (bf16[272,640]{1,0:T(8,128)(2,1)}, bf16[272,640]{1,0:T(8,128)(2,1)S(1)}, u32[]{:S(2)}, u32[]{:S(2)}) collective-permute-start(bf16[272,640]{1,0:T(8,128)(2,1)} %get-tuple-element.16.own_ref.refs_0_), channel_id=1, source_target_pairs={{0,28},{4,0},{8,4},{12,8},{16,12},{20,16},{24,20},{28,24},{1,29},{... | collective-permute-start | bytes 1044488 | tf_op jit(solution)/shard_map/ppermute | solution.py:306
  14.7 6.0 %all-to-all-start = ((bf16[8,128,640]{2,1,0:T(8,128)(2,1)}), bf16[8,128,640]{2,1,0:T(8,128)(2,1)}, u32[]{:S(2)}, u32[]{:S(2)}) async-start(bf16[8,128,640]{2,1,0:T(8,128)(2,1)} %get-tuple-element.15), calls=%async_computation | async-start | bytes 2621440 | tf_op jit(solution)/shard_map/all_to_all | solution.py:338
  20.8 1.5 %collective-permute-done.2.refs_0_ = bf16[272,640]{1,0:T(8,128)(2,1)S(1)} collective-permute-done((bf16[272,640]{1,0:T(8,128)(2,1)}, bf16[272,640]{1,0:T(8,128)(2,1)S(1)}, u32[]{:S(2)}, u32[]{:S(2)}) %collective-permute-start.2) | collective-permute-done | bytes 348192 | tf_op jit(solution)/shard_map/ppermute | solution.py:306
  22.3 0.0 collective-permute-done.3.refs_1_
  22.3 0.0 copy-start.1
  22.3 0.0 copy-start.2
  22.3 0.1 collective-permute-start.4
  22.4 3.2 %collective-permute-start.5 = (bf16[272,640]{1,0:T(8,128)(2,1)S(1)}, bf16[272,640]{1,0:T(8,128)(2,1)S(1)}, u32[]{:S(2)}, u32[]{:S(2)}) collective-permute-start(bf16[272,640]{1,0:T(8,128)(2,1)S(1)} %get-tuple-element.18.near_down_ref.refs_4_), channel_id=1, source_target_pairs={{0,28},{4,0},{8,4},{12,8},{16,12},{20,16},{24,20},{28,24},{1,29},{... | collective-permute-start | bytes 1044488 | tf_op jit(solution)/shard_map/ppermute | solution.py:306
  25.6 6.4 %collective-permute-done.4.refs_0_ = bf16[272,640]{1,0:T(8,128)(2,1)S(1)} collective-permute-done((bf16[272,640]{1,0:T(8,128)(2,1)S(1)}, bf16[272,640]{1,0:T(8,128)(2,1)S(1)}, u32[]{:S(2)}, u32[]{:S(2)}) %collective-permute-start.4) | collective-permute-done | bytes 348192 | tf_op jit(solution)/shard_map/ppermute | solution.py:306
  32.0 0.0 collective-permute-done.5.refs_1_
  32.0 0.0 copy-done.1
  32.0 0.0 copy-done.2
  32.0 0.0 copy-start.3
  32.0 0.0 copy-start.4
  32.0 1.9 %collective-permute-start.6 = (bf16[272,640]{1,0:T(8,128)(2,1)S(1)}, bf16[272,640]{1,0:T(8,128)(2,1)S(1)}, u32[]{:S(2)}, u32[]{:S(2)}) collective-permute-start(bf16[272,640]{1,0:T(8,128)(2,1)S(1)} %get-tuple-element.19.up_ref.refs_2_), channel_id=1, source_target_pairs={{0,4},{4,8},{8,12},{12,16},{16,20},{20,24},{24,28},{28,0},{1,5},{5... | collective-permute-start | bytes 1044488 | tf_op jit(solution)/shard_map/ppermute | solution.py:306
  33.9 1.4 %collective-permute-start.7 = (bf16[272,640]{1,0:T(8,128)(2,1)S(1)}, bf16[272,640]{1,0:T(8,128)(2,1)S(1)}, u32[]{:S(2)}, u32[]{:S(2)}) collective-permute-start(bf16[272,640]{1,0:T(8,128)(2,1)S(1)} %get-tuple-element.20.down_ref.refs_5_), channel_id=1, source_target_pairs={{0,28},{4,0},{8,4},{12,8},{16,12},{20,16},{24,20},{28,24},{1,29},{... | collective-permute-start | bytes 1044488 | tf_op jit(solution)/shard_map/ppermute | solution.py:306
  35.3 0.0 copy-done.3
  35.3 0.0 copy-done.4
  35.3 0.8 shard_map.104
  36.2 1.9 %collective-permute-start.8 = (bf16[16,640]{1,0:T(8,128)(2,1)S(1)}, bf16[16,640]{1,0:T(8,128)(2,1)S(1)}, u32[]{:S(2)}, u32[]{:S(2)}) collective-permute-start(bf16[16,640]{1,0:T(8,128)(2,1)S(1)} %get-tuple-element.21), channel_id=1, source_target_pairs={{0,8},{4,12},{8,16},{12,20},{16,24},{20,28},{24,0},{28,4},{1,9},{5... | collective-permute-start | bytes 61448 | tf_op jit(solution)/shard_map/ppermute | solution.py:306
  38.0 4.8 %collective-permute-done.8.refs_3_.far_ref = bf16[16,640]{1,0:T(8,128)(2,1)S(1)} collective-permute-done((bf16[16,640]{1,0:T(8,128)(2,1)S(1)}, bf16[16,640]{1,0:T(8,128)(2,1)S(1)}, u32[]{:S(2)}, u32[]{:S(2)}) %collective-permute-start.8) | collective-permute-done | bytes 20512 | tf_op jit(solution)/shard_map/ppermute | solution.py:306
  42.8 0.0 collective-permute-done.6.refs_0_
  42.8 0.0 collective-permute-done.7.refs_1_
  42.8 0.0 all-to-all-done.refs_2_.q_ref
  42.9 0.0 copy-start.5
  42.9 0.0 copy-start.6
  42.9 0.4 collective-permute-start.9
  43.3 1.2 %shard_map.108 = bf16[8,128,640]{2,1,0:T(8,128)(2,1)} custom-call(bf16[96,640]{1,0:T(8,128)(2,1)S(1)} %get-tuple-element.24.picked_ref, bf16[16,640]{1,0:T(8,128)(2,1)S(1)} %collective-permute-done.8.refs_3_.far_ref, bf16[272,640]{1,0:T(8,128)(2,1)S(1)} %get-tuple-element.22.refs_3_.up_ref, bf16[272,640]{1,0:T(8,128)(2,1)S(1)} %get-tuple-element.23.refs_6_.down_ref), custom_call_target="tpu_custom_call" | custom-call | tf_op jit(solution)/shard_map/pallas_call | solution.py:251
  44.5 0.0 copy-done.5
  44.5 0.0 copy-done.6
  44.5 6.1 %all-to-all-start.2 = ((bf16[8,128,640]{2,1,0:T(8,128)(2,1)}), bf16[8,128,640]{2,1,0:T(8,128)(2,1)}, u32[]{:S(2)}, u32[]{:S(2)}) async-start(bf16[8,128,640]{2,1,0:T(8,128)(2,1)} %shard_map.108), calls=%async_computation.2 | async-start | bytes 2621440 | tf_op jit(solution)/shard_map/all_to_all | solution.py:356
  50.5 1.0 %collective-permute-done.9.refs_0_ = bf16[272,640]{1,0:T(8,128)(2,1)} collective-permute-done((bf16[272,640]{1,0:T(8,128)(2,1)S(1)}, bf16[272,640]{1,0:T(8,128)(2,1)}, u32[]{:S(2)}, u32[]{:S(2)}) %collective-permute-start.9) | collective-permute-done | bytes 348192 | tf_op jit(solution)/shard_map/ppermute | solution.py:306
  51.6 13.2 %shard_map.107 = bf16[8,656,128]{2,1,0:T(8,128)(2,1)} custom-call(bf16[8,128,640]{2,1,0:T(8,128)(2,1)} %all-to-all-done.refs_2_.q_ref, bf16[272,640]{1,0:T(8,128)(2,1)} %get-tuple-element.16.own_ref.refs_0_, bf16[272,640]{1,0:T(8,128)(2,1)} %copy-done.1, bf16[272,640]{1,0:T(8,128)(2,1)} %copy-done.3, bf16[272,640]{1,0:T(8,128)(2,1)} %copy-done.5, ...), custom_call_target="tpu_custom_call" | custom-call | flops 15000000512 | bytes 8000000 | tf_op jit(solution)/shard_map/pallas_call | solution.py:251
  64.8 1.8 %all-to-all-done.2.text_ref = bf16[8,128,640]{2,1,0:T(8,128)(2,1)} async-done(((bf16[8,128,640]{2,1,0:T(8,128)(2,1)}), bf16[8,128,640]{2,1,0:T(8,128)(2,1)}, u32[]{:S(2)}, u32[]{:S(2)}) %all-to-all-start.2) | async-done | bytes 1310752 | tf_op jit(solution)/shard_map/all_to_all | solution.py:356
  66.6 4.6 %all-to-all-start.1 = ((bf16[8,656,128]{2,1,0:T(8,128)(2,1)}), bf16[8,656,128]{2,1,0:T(8,128)(2,1)}, u32[]{:S(2)}, u32[]{:S(2)}) async-start(bf16[8,656,128]{2,1,0:T(8,128)(2,1)} %shard_map.107), calls=%async_computation.1 | async-start | bytes 2686976 | tf_op jit(solution)/shard_map/all_to_all | solution.py:360
  71.8 0.0 copy-done
  71.8 2.7 %shard_map.109.cross_ref = f32[128,640]{1,0:T(8,128)S(1)} custom-call(bf16[8,128,640]{2,1,0:T(8,128)(2,1)} %all-to-all-done.2.text_ref, bf16[128,640]{1,0:T(8,128)(2,1)} %c_ref.3, f32[4,640]{1,0:T(4,128)} %gains_ref.3, f32[8,128]{1,0:T(8,128)S(1)} %add.6.part_ref, f32[8,128]{1,0:T(8,128)S(1)} %collective-permute-done.1.other_ref), custom_call_target="tpu_custom_call" | custom-call | tf_op jit(solution)/shard_map/pallas_call | solution.py:251
  74.5 12.3 %all-to-all-done.1.in_ref = bf16[8,656,128]{2,1,0:T(8,128)(2,1)} async-done(((bf16[8,656,128]{2,1,0:T(8,128)(2,1)}), bf16[8,656,128]{2,1,0:T(8,128)(2,1)}, u32[]{:S(2)}, u32[]{:S(2)}) %all-to-all-start.1) | async-done | bytes 1343520 | tf_op jit(solution)/shard_map/all_to_all | solution.py:360
  86.8 2.4 %shard_map.110 = bf16[128,640]{1,0:T(8,128)(2,1)} custom-call(bf16[8,656,128]{2,1,0:T(8,128)(2,1)} %all-to-all-done.1.in_ref, f32[128,640]{1,0:T(8,128)S(1)} %shard_map.109.cross_ref, f32[1,640]{1,0:T(1,128)S(1)} %constant_dynamic-slice_fusion.gate_ref), custom_call_target="tpu_custom_call" | custom-call | tf_op jit(solution)/shard_map/pallas_call | solution.py:251
  (6 shorter events, 0.0 us)
Async XLA Ops:
  0.0 71.8 %copy-start = (f32[1000,640]{1,0:T(8,128)S(1)}, f32[1000,640]{1,0:T(8,128)}, u32[]{:S(2)}) copy-start(f32[1000,640]{1,0:T(8,128)} %param.18) | copy-start | bytes 7680004
  1.4 1.2 %collective-permute-start = (f32[8,128]{1,0:T(8,128)S(1)}, f32[8,128]{1,0:T(8,128)S(1)}, u32[]{:S(2)}, u32[]{:S(2)}) collective-permute-start(f32[8,128]{1,0:T(8,128)S(1)} %shard_map.100), channel_id=1, source_target_pairs={{0,1},{1,0},{2,3},{3,2},{4,5},{5,4},{6,7},{7,6},{8,9},{9,8},{10,11... | collective-permute-start | bytes 12296 | tf_op jit(solution)/shard_map/ppermute | solution.py:325
  2.7 3.9 %collective-permute-start.1 = (f32[8,128]{1,0:T(8,128)S(1)}, f32[8,128]{1,0:T(8,128)S(1)}, u32[]{:S(2)}, u32[]{:S(2)}) collective-permute-start(f32[8,128]{1,0:T(8,128)S(1)} %add.6.part_ref), channel_id=1, source_target_pairs={{0,2},{2,0},{1,3},{3,1},{4,6},{6,4},{5,7},{7,5},{8,10},{10,8},{9,1... | collective-permute-start | bytes 12296 | tf_op jit(solution)/shard_map/ppermute | solution.py:326
  9.1 13.1 %collective-permute-start.2 = (bf16[272,640]{1,0:T(8,128)(2,1)}, bf16[272,640]{1,0:T(8,128)(2,1)S(1)}, u32[]{:S(2)}, u32[]{:S(2)}) collective-permute-start(bf16[272,640]{1,0:T(8,128)(2,1)} %get-tuple-element.16.own_ref.refs_0_), channel_id=1, source_target_pairs={{0,4},{4,8},{8,12},{12,16},{16,20},{20,24},{24,28},{28,0},{1,5},{5... | collective-permute-start | bytes 1044488 | tf_op jit(solution)/shard_map/ppermute | solution.py:306
  10.8 11.5 %collective-permute-start.3 = (bf16[272,640]{1,0:T(8,128)(2,1)}, bf16[272,640]{1,0:T(8,128)(2,1)S(1)}, u32[]{:S(2)}, u32[]{:S(2)}) collective-permute-start(bf16[272,640]{1,0:T(8,128)(2,1)} %get-tuple-element.16.own_ref.refs_0_), channel_id=1, source_target_pairs={{0,28},{4,0},{8,4},{12,8},{16,12},{20,16},{24,20},{28,24},{1,29},{... | collective-permute-start | bytes 1044488 | tf_op jit(solution)/shard_map/ppermute | solution.py:306
  14.7 28.1 %all-to-all-start = ((bf16[8,128,640]{2,1,0:T(8,128)(2,1)}), bf16[8,128,640]{2,1,0:T(8,128)(2,1)}, u32[]{:S(2)}, u32[]{:S(2)}) async-start(bf16[8,128,640]{2,1,0:T(8,128)(2,1)} %get-tuple-element.15), calls=%async_computation | async-start | bytes 2621440 | tf_op jit(solution)/shard_map/all_to_all | solution.py:338
  22.3 9.7 %copy-start.1 = (bf16[272,640]{1,0:T(8,128)(2,1)}, bf16[272,640]{1,0:T(8,128)(2,1)S(1)}, u32[]{:S(2)}) copy-start(bf16[272,640]{1,0:T(8,128)(2,1)S(1)} %get-tuple-element.17.near_up_ref.refs_1_) | copy-start | bytes 1044484
  22.3 9.7 %copy-start.2 = (bf16[272,640]{1,0:T(8,128)(2,1)}, bf16[272,640]{1,0:T(8,128)(2,1)S(1)}, u32[]{:S(2)}) copy-start(bf16[272,640]{1,0:T(8,128)(2,1)S(1)} %get-tuple-element.18.near_down_ref.refs_4_) | copy-start | bytes 1044484
  22.3 9.7 %collective-permute-start.4 = (bf16[272,640]{1,0:T(8,128)(2,1)S(1)}, bf16[272,640]{1,0:T(8,128)(2,1)S(1)}, u32[]{:S(2)}, u32[]{:S(2)}) collective-permute-start(bf16[272,640]{1,0:T(8,128)(2,1)S(1)} %get-tuple-element.17.near_up_ref.refs_1_), channel_id=1, source_target_pairs={{0,4},{4,8},{8,12},{12,16},{16,20},{20,24},{24,28},{28,0},{1,5},{5... | collective-permute-start | bytes 1044488 | tf_op jit(solution)/shard_map/ppermute | solution.py:306
  22.4 9.6 %collective-permute-start.5 = (bf16[272,640]{1,0:T(8,128)(2,1)S(1)}, bf16[272,640]{1,0:T(8,128)(2,1)S(1)}, u32[]{:S(2)}, u32[]{:S(2)}) collective-permute-start(bf16[272,640]{1,0:T(8,128)(2,1)S(1)} %get-tuple-element.18.near_down_ref.refs_4_), channel_id=1, source_target_pairs={{0,28},{4,0},{8,4},{12,8},{16,12},{20,16},{24,20},{28,24},{1,29},{... | collective-permute-start | bytes 1044488 | tf_op jit(solution)/shard_map/ppermute | solution.py:306
  32.0 3.3 %copy-start.3 = (bf16[272,640]{1,0:T(8,128)(2,1)}, bf16[272,640]{1,0:T(8,128)(2,1)S(1)}, u32[]{:S(2)}) copy-start(bf16[272,640]{1,0:T(8,128)(2,1)S(1)} %get-tuple-element.19.up_ref.refs_2_) | copy-start | bytes 1044484
  32.0 3.3 %copy-start.4 = (bf16[272,640]{1,0:T(8,128)(2,1)}, bf16[272,640]{1,0:T(8,128)(2,1)S(1)}, u32[]{:S(2)}) copy-start(bf16[272,640]{1,0:T(8,128)(2,1)S(1)} %get-tuple-element.20.down_ref.refs_5_) | copy-start | bytes 1044484
  32.0 10.8 %collective-permute-start.6 = (bf16[272,640]{1,0:T(8,128)(2,1)S(1)}, bf16[272,640]{1,0:T(8,128)(2,1)S(1)}, u32[]{:S(2)}, u32[]{:S(2)}) collective-permute-start(bf16[272,640]{1,0:T(8,128)(2,1)S(1)} %get-tuple-element.19.up_ref.refs_2_), channel_id=1, source_target_pairs={{0,4},{4,8},{8,12},{12,16},{16,20},{20,24},{24,28},{28,0},{1,5},{5... | collective-permute-start | bytes 1044488 | tf_op jit(solution)/shard_map/ppermute | solution.py:306
  33.9 8.9 %collective-permute-start.7 = (bf16[272,640]{1,0:T(8,128)(2,1)S(1)}, bf16[272,640]{1,0:T(8,128)(2,1)S(1)}, u32[]{:S(2)}, u32[]{:S(2)}) collective-permute-start(bf16[272,640]{1,0:T(8,128)(2,1)S(1)} %get-tuple-element.20.down_ref.refs_5_), channel_id=1, source_target_pairs={{0,28},{4,0},{8,4},{12,8},{16,12},{20,16},{24,20},{28,24},{1,29},{... | collective-permute-start | bytes 1044488 | tf_op jit(solution)/shard_map/ppermute | solution.py:306
  36.2 6.7 %collective-permute-start.8 = (bf16[16,640]{1,0:T(8,128)(2,1)S(1)}, bf16[16,640]{1,0:T(8,128)(2,1)S(1)}, u32[]{:S(2)}, u32[]{:S(2)}) collective-permute-start(bf16[16,640]{1,0:T(8,128)(2,1)S(1)} %get-tuple-element.21), channel_id=1, source_target_pairs={{0,8},{4,12},{8,16},{12,20},{16,24},{20,28},{24,0},{28,4},{1,9},{5... | collective-permute-start | bytes 61448 | tf_op jit(solution)/shard_map/ppermute | solution.py:306
  42.9 1.6 %copy-start.5 = (bf16[272,640]{1,0:T(8,128)(2,1)}, bf16[272,640]{1,0:T(8,128)(2,1)S(1)}, u32[]{:S(2)}) copy-start(bf16[272,640]{1,0:T(8,128)(2,1)S(1)} %get-tuple-element.22.refs_3_.up_ref) | copy-start | bytes 1044484
  42.9 1.6 %copy-start.6 = (bf16[272,640]{1,0:T(8,128)(2,1)}, bf16[272,640]{1,0:T(8,128)(2,1)S(1)}, u32[]{:S(2)}) copy-start(bf16[272,640]{1,0:T(8,128)(2,1)S(1)} %get-tuple-element.23.refs_6_.down_ref) | copy-start | bytes 1044484
  42.9 8.7 %collective-permute-start.9 = (bf16[272,640]{1,0:T(8,128)(2,1)S(1)}, bf16[272,640]{1,0:T(8,128)(2,1)}, u32[]{:S(2)}, u32[]{:S(2)}) collective-permute-start(bf16[272,640]{1,0:T(8,128)(2,1)S(1)} %get-tuple-element.22.refs_3_.up_ref), channel_id=1, source_target_pairs={{0,4},{4,8},{8,12},{12,16},{16,20},{20,24},{24,28},{28,0},{1,5},{5... | collective-permute-start | bytes 1044488 | tf_op jit(solution)/shard_map/ppermute | solution.py:306
  44.5 22.1 %all-to-all-start.2 = ((bf16[8,128,640]{2,1,0:T(8,128)(2,1)}), bf16[8,128,640]{2,1,0:T(8,128)(2,1)}, u32[]{:S(2)}, u32[]{:S(2)}) async-start(bf16[8,128,640]{2,1,0:T(8,128)(2,1)} %shard_map.108), calls=%async_computation.2 | async-start | bytes 2621440 | tf_op jit(solution)/shard_map/all_to_all | solution.py:356
  66.6 20.2 %all-to-all-start.1 = ((bf16[8,656,128]{2,1,0:T(8,128)(2,1)}), bf16[8,656,128]{2,1,0:T(8,128)(2,1)}, u32[]{:S(2)}, u32[]{:S(2)}) async-start(bf16[8,656,128]{2,1,0:T(8,128)(2,1)} %shard_map.107), calls=%async_computation.1 | async-start | bytes 2686976 | tf_op jit(solution)/shard_map/all_to_all | solution.py:360

commit v7 on v6

--- a/solution.py
+++ b/solution.py
@@ -64,9 +64,11 @@
     mask_ref, k_ref, v_ref, tk_ref, tv_ref, q_ref, gains_ref, part_ref, other_ref, out_ref, q_out
 ):
     sums = part_ref[...] + other_ref[...]
-    q_factor = factor_of(sums[0:1])
-    k_factor = factor_of(sums[1:2])
-    t_factor = factor_of(sums[3:4])[0:8]
+    table = jnp.concatenate([sums, jnp.zeros((ROWS - 8, ROWS), jnp.float32)], axis=0).T
+    factors = lax.rsqrt(table * (1.0 / (HEADS * HD)) + 1e-06)
+    q_factor = jnp.broadcast_to(factors[:, 0:1], (ROWS, ROWS))
+    k_factor = jnp.broadcast_to(factors[:, 1:2], (ROWS, ROWS))
+    t_factor = jnp.broadcast_to(factors[0:8, 3:4], (8, ROWS))
     row = lax.broadcasted_iota(jnp.int32, (8, ROWS), 0)
     usable = jnp.zeros((8, ROWS), jnp.int32)
     for n in range(8):
@@ -322,8 +324,10 @@
     (sums,) = call(
         sums_kernel, [((8, ROWS), f32, pltpu.VMEM)], [video_query, video_key, cross_query, text_key]
     )
-    part = sums + lax.ppermute(sums, "head", [(0, 1), (1, 0), (2, 3), (3, 2)])
-    other = lax.ppermute(part, "head", [(0, 2), (2, 0), (1, 3), (3, 1)])
+    beside = lax.ppermute(sums, "head", [(0, 1), (1, 0), (2, 3), (3, 2)])
+    across = lax.ppermute(sums, "head", [(0, 2), (2, 0), (1, 3), (3, 1)])
+    corner = lax.ppermute(sums, "head", [(0, 3), (3, 0), (1, 2), (2, 1)])
+    part, other = sums + beside, across + corner
     own, queries = call(
         norm_kernel,
         [

time: 90 us -> 95.1 us (1.057)
  waiting for transfers between devices: 30.6 us -> 36.8 us
  starting transfers between devices: 33.5 us -> 32.5 us
    ppermute x8, waiting for transfers between devices: 13.8 us -> 16.6 us  [shift(): return lax.ppermute(array, 'z', [(i, (i + step) % 8) for i in range(8)])]
    all_to_all x1, waiting for transfers between devices: 1.79 us -> 3.61 us  [local(): text = lax.all_to_all(text, ('y', 'xh'), 0, 0)]
    ppermute x8, starting transfers between devices: 14.5 us -> 13 us  [shift(): return lax.ppermute(array, 'z', [(i, (i + step) % 8) for i in range(8)])]
    all_to_all x1, waiting for transfers between devices: 12.3 us -> 13.6 us  [local(): received = lax.all_to_all(partial, ('y', 'xh'), 0, 0)]
    ppermute x2 -> x3, waiting for transfers between devices: 2.74 us -> 2.98 us  [the longest x1 1.53 us: local(): across = lax.ppermute(sums, 'head', [(0, 2), (2, 0), (1, 3), (3, 1)])]
    ppermute x2 -> x3, starting transfers between devices: 2.34 us -> 2.48 us  [the longest x1 2.36 us: local(): across = lax.ppermute(sums, 'head', [(0, 2), (2, 0), (1, 3), (3, 1)])]
  transfers between devices with their start and end apart: 13 -> 14, of which waited for: 8 -> 8; matrix products, arithmetic and copies ran while one was open for 0% -> 0% of each run, Pallas kernels for 20% -> 19%
where the time goes in v7:
time: 95.1 us; the launch traced here: 94.5 us
  waiting for transfers between devices  36.8 us (39%)
  starting transfers between devices  32.5 us (34%)
  Pallas kernels  24.4 us (26%)
    pallas_call x7, Pallas kernels, call(): pl.pallas_call(kernel, grid=(1,), out_shape=out_shape, in_specs=specs, ou...  24.4 us
    ppermute x8, waiting for transfers between devices, shift(): return lax.ppermute(array, 'z', [(i, (i + step) % 8) for i in range(8)])  16.6 us
    all_to_all x1, waiting for transfers between devices, local(): received = lax.all_to_all(partial, ('y', 'xh'), 0, 0)  13.6 us
    ppermute x8, starting transfers between devices, shift(): return lax.ppermute(array, 'z', [(i, (i + step) % 8) for i in range(8)])  13 us
    all_to_all x1, starting transfers between devices, local(): text = lax.all_to_all(text, ('y', 'xh'), 0, 0)  6.41 us
    all_to_all x1, starting transfers between devices, local(): queries = lax.all_to_all(queries, ('y', 'xh'), 0, 0)  6.28 us
    all_to_all x1, starting transfers between devices, local(): received = lax.all_to_all(partial, ('y', 'xh'), 0, 0)  4.29 us
    all_to_all x1, waiting for transfers between devices, local(): text = lax.all_to_all(text, ('y', 'xh'), 0, 0)  3.61 us
  transfers between devices with their start and end apart: 14, of which 8 were waited for; matrix products, arithmetic and copies ran while one was open for 0% of the time, Pallas kernels for 19%

profile of v7, /device:TPU:2, one launch (start us, length us, event | category | flops | bytes accessed | tf_op | source)
XLA Modules:
  0.0 94.5 jit_solution(2607746987362290749)
XLA Ops:
  0.0 0.0 copy-start
  0.0 1.4 %shard_map.100 = f32[8,128]{1,0:T(8,128)S(1)} custom-call(bf16[128,640]{1,0:T(8,128)(2,1)} %q_ref.3, bf16[128,640]{1,0:T(8,128)(2,1)} %k_ref.3, bf16[128,640]{1,0:T(8,128)(2,1)} %c_ref.3, bf16[8,640]{1,0:T(8,128)(2,1)} %tk_ref.1), custom_call_target="tpu_custom_call" | custom-call | tf_op jit(solution)/shard_map/pallas_call | solution.py:253
  1.4 0.1 collective-permute-start
  1.5 2.4 %collective-permute-start.1 = (f32[8,128]{1,0:T(8,128)S(1)}, f32[8,128]{1,0:T(8,128)S(1)}, u32[]{:S(2)}, u32[]{:S(2)}) collective-permute-start(f32[8,128]{1,0:T(8,128)S(1)} %shard_map.100), channel_id=1, source_target_pairs={{0,2},{2,0},{1,3},{3,1},{4,6},{6,4},{5,7},{7,5},{8,10},{10,8},{9,1... | collective-permute-start | bytes 12296 | tf_op jit(solution)/shard_map/ppermute | solution.py:328
  3.9 0.1 collective-permute-start.2
  3.9 0.0 collective-permute-done
  3.9 1.5 %collective-permute-done.1 = f32[8,128]{1,0:T(8,128)S(1)} collective-permute-done((f32[8,128]{1,0:T(8,128)S(1)}, f32[8,128]{1,0:T(8,128)S(1)}, u32[]{:S(2)}, u32[]{:S(2)}) %collective-permute-start.1) | collective-permute-done | bytes 4128 | tf_op jit(solution)/shard_map/ppermute | solution.py:328
  5.4 1.4 %collective-permute-done.2 = f32[8,128]{1,0:T(8,128)S(1)} collective-permute-done((f32[8,128]{1,0:T(8,128)S(1)}, f32[8,128]{1,0:T(8,128)S(1)}, u32[]{:S(2)}, u32[]{:S(2)}) %collective-permute-start.2) | collective-permute-done | bytes 4128 | tf_op jit(solution)/shard_map/ppermute | solution.py:329
  6.9 2.7 %shard_map.101 = (bf16[272,640]{1,0:T(8,128)(2,1)}, bf16[8,128,640]{2,1,0:T(8,128)(2,1)}) custom-call(s32[8]{0:T(128)} %mask_ref.1, bf16[128,640]{1,0:T(8,128)(2,1)} %k_ref.3, bf16[128,640]{1,0:T(8,128)(2,1)} %v_ref.1, bf16[8,640]{1,0:T(8,128)(2,1)} %tk_ref.1, bf16[8,640]{1,0:T(8,128)(2,1)} %tv_ref.1, bf16[128,640]{1,0:T(8,128)(2,1)} %q_ref.3, ...), custom_call_target="tpu_custom_call" | custom-call | tf_op jit(solution)/shard_map/pallas_call | solution.py:253
  9.6 0.2 collective-permute-start.3
  9.8 3.9 %collective-permute-start.4 = (bf16[272,640]{1,0:T(8,128)(2,1)}, bf16[272,640]{1,0:T(8,128)(2,1)S(1)}, u32[]{:S(2)}, u32[]{:S(2)}) collective-permute-start(bf16[272,640]{1,0:T(8,128)(2,1)} %get-tuple-element.16.own_ref.refs_0_), channel_id=1, source_target_pairs={{0,28},{4,0},{8,4},{12,8},{16,12},{20,16},{24,20},{28,24},{1,29},{... | collective-permute-start | bytes 1044488 | tf_op jit(solution)/shard_map/ppermute | solution.py:308
  13.7 6.3 %all-to-all-start = ((bf16[8,128,640]{2,1,0:T(8,128)(2,1)}), bf16[8,128,640]{2,1,0:T(8,128)(2,1)}, u32[]{:S(2)}, u32[]{:S(2)}) async-start(bf16[8,128,640]{2,1,0:T(8,128)(2,1)} %get-tuple-element.15), calls=%async_computation | async-start | bytes 2621440 | tf_op jit(solution)/shard_map/all_to_all | solution.py:342
  20.0 2.4 %collective-permute-done.3.refs_0_ = bf16[272,640]{1,0:T(8,128)(2,1)S(1)} collective-permute-done((bf16[272,640]{1,0:T(8,128)(2,1)}, bf16[272,640]{1,0:T(8,128)(2,1)S(1)}, u32[]{:S(2)}, u32[]{:S(2)}) %collective-permute-start.3) | collective-permute-done | bytes 348192 | tf_op jit(solution)/shard_map/ppermute | solution.py:308
  22.4 0.0 collective-permute-done.4.refs_1_
  22.4 0.0 copy-start.1
  22.4 0.0 copy-start.2
  22.4 0.1 collective-permute-start.5
  22.5 3.2 %collective-permute-start.6 = (bf16[272,640]{1,0:T(8,128)(2,1)S(1)}, bf16[272,640]{1,0:T(8,128)(2,1)S(1)}, u32[]{:S(2)}, u32[]{:S(2)}) collective-permute-start(bf16[272,640]{1,0:T(8,128)(2,1)S(1)} %get-tuple-element.18.near_down_ref.refs_4_), channel_id=1, source_target_pairs={{0,28},{4,0},{8,4},{12,8},{16,12},{20,16},{24,20},{28,24},{1,29},{... | collective-permute-start | bytes 1044488 | tf_op jit(solution)/shard_map/ppermute | solution.py:308
  25.7 7.6 %collective-permute-done.5.refs_0_ = bf16[272,640]{1,0:T(8,128)(2,1)S(1)} collective-permute-done((bf16[272,640]{1,0:T(8,128)(2,1)S(1)}, bf16[272,640]{1,0:T(8,128)(2,1)S(1)}, u32[]{:S(2)}, u32[]{:S(2)}) %collective-permute-start.5) | collective-permute-done | bytes 348192 | tf_op jit(solution)/shard_map/ppermute | solution.py:308
  33.3 0.0 collective-permute-done.6.refs_1_
  33.3 0.0 copy-done.1
  33.3 0.0 copy-done.2
  33.3 0.0 copy-start.3
  33.3 0.0 copy-start.4
  33.3 1.8 %collective-permute-start.7 = (bf16[272,640]{1,0:T(8,128)(2,1)S(1)}, bf16[272,640]{1,0:T(8,128)(2,1)S(1)}, u32[]{:S(2)}, u32[]{:S(2)}) collective-permute-start(bf16[272,640]{1,0:T(8,128)(2,1)S(1)} %get-tuple-element.19.up_ref.refs_2_), channel_id=1, source_target_pairs={{0,4},{4,8},{8,12},{12,16},{16,20},{20,24},{24,28},{28,0},{1,5},{5... | collective-permute-start | bytes 1044488 | tf_op jit(solution)/shard_map/ppermute | solution.py:308
  35.1 1.5 %collective-permute-start.8 = (bf16[272,640]{1,0:T(8,128)(2,1)S(1)}, bf16[272,640]{1,0:T(8,128)(2,1)S(1)}, u32[]{:S(2)}, u32[]{:S(2)}) collective-permute-start(bf16[272,640]{1,0:T(8,128)(2,1)S(1)} %get-tuple-element.20.down_ref.refs_5_), channel_id=1, source_target_pairs={{0,28},{4,0},{8,4},{12,8},{16,12},{20,16},{24,20},{28,24},{1,29},{... | collective-permute-start | bytes 1044488 | tf_op jit(solution)/shard_map/ppermute | solution.py:308
  36.6 0.0 copy-done.3
  36.7 0.0 copy-done.4
  36.7 0.8 shard_map.104
  37.5 1.8 %collective-permute-start.9 = (bf16[16,640]{1,0:T(8,128)(2,1)S(1)}, bf16[16,640]{1,0:T(8,128)(2,1)S(1)}, u32[]{:S(2)}, u32[]{:S(2)}) collective-permute-start(bf16[16,640]{1,0:T(8,128)(2,1)S(1)} %get-tuple-element.21), channel_id=1, source_target_pairs={{0,8},{4,12},{8,16},{12,20},{16,24},{20,28},{24,0},{28,4},{1,9},{5... | collective-permute-start | bytes 61448 | tf_op jit(solution)/shard_map/ppermute | solution.py:308
  39.2 6.0 %collective-permute-done.9.refs_3_.far_ref = bf16[16,640]{1,0:T(8,128)(2,1)S(1)} collective-permute-done((bf16[16,640]{1,0:T(8,128)(2,1)S(1)}, bf16[16,640]{1,0:T(8,128)(2,1)S(1)}, u32[]{:S(2)}, u32[]{:S(2)}) %collective-permute-start.9) | collective-permute-done | bytes 20512 | tf_op jit(solution)/shard_map/ppermute | solution.py:308
  45.2 0.0 collective-permute-done.7.refs_0_
  45.2 0.0 collective-permute-done.8.refs_1_
  45.2 0.0 all-to-all-done.refs_2_.q_ref
  45.2 0.0 copy-start.5
  45.3 0.0 copy-start.6
  45.3 0.4 collective-permute-start.10
  45.7 1.2 %shard_map.108 = bf16[8,128,640]{2,1,0:T(8,128)(2,1)} custom-call(bf16[96,640]{1,0:T(8,128)(2,1)S(1)} %get-tuple-element.24.picked_ref, bf16[16,640]{1,0:T(8,128)(2,1)S(1)} %collective-permute-done.9.refs_3_.far_ref, bf16[272,640]{1,0:T(8,128)(2,1)S(1)} %get-tuple-element.22.refs_3_.up_ref, bf16[272,640]{1,0:T(8,128)(2,1)S(1)} %get-tuple-element.23.refs_6_.down_ref), custom_call_target="tpu_custom_call" | custom-call | tf_op jit(solution)/shard_map/pallas_call | solution.py:253
  46.9 0.0 copy-done.5
  46.9 0.0 copy-done.6
  46.9 6.4 %all-to-all-start.2 = ((bf16[8,128,640]{2,1,0:T(8,128)(2,1)}), bf16[8,128,640]{2,1,0:T(8,128)(2,1)}, u32[]{:S(2)}, u32[]{:S(2)}) async-start(bf16[8,128,640]{2,1,0:T(8,128)(2,1)} %shard_map.108), calls=%async_computation.2 | async-start | bytes 2621440 | tf_op jit(solution)/shard_map/all_to_all | solution.py:360
  53.3 0.6 collective-permute-done.10.refs_0_
  54.0 13.2 %shard_map.107 = bf16[8,656,128]{2,1,0:T(8,128)(2,1)} custom-call(bf16[8,128,640]{2,1,0:T(8,128)(2,1)} %all-to-all-done.refs_2_.q_ref, bf16[272,640]{1,0:T(8,128)(2,1)} %get-tuple-element.16.own_ref.refs_0_, bf16[272,640]{1,0:T(8,128)(2,1)} %copy-done.1, bf16[272,640]{1,0:T(8,128)(2,1)} %copy-done.3, bf16[272,640]{1,0:T(8,128)(2,1)} %copy-done.5, ...), custom_call_target="tpu_custom_call" | custom-call | flops 15000000512 | bytes 8000000 | tf_op jit(solution)/shard_map/pallas_call | solution.py:253
  67.2 3.6 %all-to-all-done.2.text_ref = bf16[8,128,640]{2,1,0:T(8,128)(2,1)} async-done(((bf16[8,128,640]{2,1,0:T(8,128)(2,1)}), bf16[8,128,640]{2,1,0:T(8,128)(2,1)}, u32[]{:S(2)}, u32[]{:S(2)}) %all-to-all-start.2) | async-done | bytes 1310752 | tf_op jit(solution)/shard_map/all_to_all | solution.py:360
  70.8 4.3 %all-to-all-start.1 = ((bf16[8,656,128]{2,1,0:T(8,128)(2,1)}), bf16[8,656,128]{2,1,0:T(8,128)(2,1)}, u32[]{:S(2)}, u32[]{:S(2)}) async-start(bf16[8,656,128]{2,1,0:T(8,128)(2,1)} %shard_map.107), calls=%async_computation.1 | async-start | bytes 2686976 | tf_op jit(solution)/shard_map/all_to_all | solution.py:364
  75.7 0.0 copy-done
  75.8 2.7 %shard_map.109.cross_ref = f32[128,640]{1,0:T(8,128)S(1)} custom-call(bf16[8,128,640]{2,1,0:T(8,128)(2,1)} %all-to-all-done.2.text_ref, bf16[128,640]{1,0:T(8,128)(2,1)} %c_ref.3, f32[4,640]{1,0:T(4,128)} %gains_ref.3, f32[8,128]{1,0:T(8,128)S(1)} %add.9.part_ref, f32[8,128]{1,0:T(8,128)S(1)} %add.10.other_ref), custom_call_target="tpu_custom_call" | custom-call | tf_op jit(solution)/shard_map/pallas_call | solution.py:253
  78.4 13.6 %all-to-all-done.1.in_ref = bf16[8,656,128]{2,1,0:T(8,128)(2,1)} async-done(((bf16[8,656,128]{2,1,0:T(8,128)(2,1)}), bf16[8,656,128]{2,1,0:T(8,128)(2,1)}, u32[]{:S(2)}, u32[]{:S(2)}) %all-to-all-start.1) | async-done | bytes 1343520 | tf_op jit(solution)/shard_map/all_to_all | solution.py:364
  92.1 2.4 %shard_map.110 = bf16[128,640]{1,0:T(8,128)(2,1)} custom-call(bf16[8,656,128]{2,1,0:T(8,128)(2,1)} %all-to-all-done.1.in_ref, f32[128,640]{1,0:T(8,128)S(1)} %shard_map.109.cross_ref, f32[1,640]{1,0:T(1,128)S(1)} %constant_dynamic-slice_fusion.gate_ref), custom_call_target="tpu_custom_call" | custom-call | tf_op jit(solution)/shard_map/pallas_call | solution.py:253
  (7 shorter events, 0.0 us)
Async XLA Ops:
  0.0 75.7 %copy-start = (f32[1000,640]{1,0:T(8,128)S(1)}, f32[1000,640]{1,0:T(8,128)}, u32[]{:S(2)}) copy-start(f32[1000,640]{1,0:T(8,128)} %param.18) | copy-start | bytes 7680004
  1.4 2.5 %collective-permute-start = (f32[8,128]{1,0:T(8,128)S(1)}, f32[8,128]{1,0:T(8,128)S(1)}, u32[]{:S(2)}, u32[]{:S(2)}) collective-permute-start(f32[8,128]{1,0:T(8,128)S(1)} %shard_map.100), channel_id=1, source_target_pairs={{0,1},{1,0},{2,3},{3,2},{4,5},{5,4},{6,7},{7,6},{8,9},{9,8},{10,11... | collective-permute-start | bytes 12296 | tf_op jit(solution)/shard_map/ppermute | solution.py:327
  1.5 3.9 %collective-permute-start.1 = (f32[8,128]{1,0:T(8,128)S(1)}, f32[8,128]{1,0:T(8,128)S(1)}, u32[]{:S(2)}, u32[]{:S(2)}) collective-permute-start(f32[8,128]{1,0:T(8,128)S(1)} %shard_map.100), channel_id=1, source_target_pairs={{0,2},{2,0},{1,3},{3,1},{4,6},{6,4},{5,7},{7,5},{8,10},{10,8},{9,1... | collective-permute-start | bytes 12296 | tf_op jit(solution)/shard_map/ppermute | solution.py:328
  3.9 3.0 %collective-permute-start.2 = (f32[8,128]{1,0:T(8,128)S(1)}, f32[8,128]{1,0:T(8,128)S(1)}, u32[]{:S(2)}, u32[]{:S(2)}) collective-permute-start(f32[8,128]{1,0:T(8,128)S(1)} %shard_map.100), channel_id=1, source_target_pairs={{0,3},{3,0},{1,2},{2,1},{4,7},{7,4},{5,6},{6,5},{8,11},{11,8},{9,1... | collective-permute-start | bytes 12296 | tf_op jit(solution)/shard_map/ppermute | solution.py:329
  9.6 12.8 %collective-permute-start.3 = (bf16[272,640]{1,0:T(8,128)(2,1)}, bf16[272,640]{1,0:T(8,128)(2,1)S(1)}, u32[]{:S(2)}, u32[]{:S(2)}) collective-permute-start(bf16[272,640]{1,0:T(8,128)(2,1)} %get-tuple-element.16.own_ref.refs_0_), channel_id=1, source_target_pairs={{0,4},{4,8},{8,12},{12,16},{16,20},{20,24},{24,28},{28,0},{1,5},{5... | collective-permute-start | bytes 1044488 | tf_op jit(solution)/shard_map/ppermute | solution.py:308
  9.8 12.6 %collective-permute-start.4 = (bf16[272,640]{1,0:T(8,128)(2,1)}, bf16[272,640]{1,0:T(8,128)(2,1)S(1)}, u32[]{:S(2)}, u32[]{:S(2)}) collective-permute-start(bf16[272,640]{1,0:T(8,128)(2,1)} %get-tuple-element.16.own_ref.refs_0_), channel_id=1, source_target_pairs={{0,28},{4,0},{8,4},{12,8},{16,12},{20,16},{24,20},{28,24},{1,29},{... | collective-permute-start | bytes 1044488 | tf_op jit(solution)/shard_map/ppermute | solution.py:308
  13.7 31.5 %all-to-all-start = ((bf16[8,128,640]{2,1,0:T(8,128)(2,1)}), bf16[8,128,640]{2,1,0:T(8,128)(2,1)}, u32[]{:S(2)}, u32[]{:S(2)}) async-start(bf16[8,128,640]{2,1,0:T(8,128)(2,1)} %get-tuple-element.15), calls=%async_computation | async-start | bytes 2621440 | tf_op jit(solution)/shard_map/all_to_all | solution.py:342
  22.4 11.0 %copy-start.1 = (bf16[272,640]{1,0:T(8,128)(2,1)}, bf16[272,640]{1,0:T(8,128)(2,1)S(1)}, u32[]{:S(2)}) copy-start(bf16[272,640]{1,0:T(8,128)(2,1)S(1)} %get-tuple-element.17.near_up_ref.refs_1_) | copy-start | bytes 1044484
  22.4 11.0 %copy-start.2 = (bf16[272,640]{1,0:T(8,128)(2,1)}, bf16[272,640]{1,0:T(8,128)(2,1)S(1)}, u32[]{:S(2)}) copy-start(bf16[272,640]{1,0:T(8,128)(2,1)S(1)} %get-tuple-element.18.near_down_ref.refs_4_) | copy-start | bytes 1044484
  22.4 10.9 %collective-permute-start.5 = (bf16[272,640]{1,0:T(8,128)(2,1)S(1)}, bf16[272,640]{1,0:T(8,128)(2,1)S(1)}, u32[]{:S(2)}, u32[]{:S(2)}) collective-permute-start(bf16[272,640]{1,0:T(8,128)(2,1)S(1)} %get-tuple-element.17.near_up_ref.refs_1_), channel_id=1, source_target_pairs={{0,4},{4,8},{8,12},{12,16},{16,20},{20,24},{24,28},{28,0},{1,5},{5... | collective-permute-start | bytes 1044488 | tf_op jit(solution)/shard_map/ppermute | solution.py:308
  22.5 10.8 %collective-permute-start.6 = (bf16[272,640]{1,0:T(8,128)(2,1)S(1)}, bf16[272,640]{1,0:T(8,128)(2,1)S(1)}, u32[]{:S(2)}, u32[]{:S(2)}) collective-permute-start(bf16[272,640]{1,0:T(8,128)(2,1)S(1)} %get-tuple-element.18.near_down_ref.refs_4_), channel_id=1, source_target_pairs={{0,28},{4,0},{8,4},{12,8},{16,12},{20,16},{24,20},{28,24},{1,29},{... | collective-permute-start | bytes 1044488 | tf_op jit(solution)/shard_map/ppermute | solution.py:308
  33.3 3.3 %copy-start.3 = (bf16[272,640]{1,0:T(8,128)(2,1)}, bf16[272,640]{1,0:T(8,128)(2,1)S(1)}, u32[]{:S(2)}) copy-start(bf16[272,640]{1,0:T(8,128)(2,1)S(1)} %get-tuple-element.19.up_ref.refs_2_) | copy-start | bytes 1044484
  33.3 3.3 %copy-start.4 = (bf16[272,640]{1,0:T(8,128)(2,1)}, bf16[272,640]{1,0:T(8,128)(2,1)S(1)}, u32[]{:S(2)}) copy-start(bf16[272,640]{1,0:T(8,128)(2,1)S(1)} %get-tuple-element.20.down_ref.refs_5_) | copy-start | bytes 1044484
  33.3 11.9 %collective-permute-start.7 = (bf16[272,640]{1,0:T(8,128)(2,1)S(1)}, bf16[272,640]{1,0:T(8,128)(2,1)S(1)}, u32[]{:S(2)}, u32[]{:S(2)}) collective-permute-start(bf16[272,640]{1,0:T(8,128)(2,1)S(1)} %get-tuple-element.19.up_ref.refs_2_), channel_id=1, source_target_pairs={{0,4},{4,8},{8,12},{12,16},{16,20},{20,24},{24,28},{28,0},{1,5},{5... | collective-permute-start | bytes 1044488 | tf_op jit(solution)/shard_map/ppermute | solution.py:308
  35.1 10.1 %collective-permute-start.8 = (bf16[272,640]{1,0:T(8,128)(2,1)S(1)}, bf16[272,640]{1,0:T(8,128)(2,1)S(1)}, u32[]{:S(2)}, u32[]{:S(2)}) collective-permute-start(bf16[272,640]{1,0:T(8,128)(2,1)S(1)} %get-tuple-element.20.down_ref.refs_5_), channel_id=1, source_target_pairs={{0,28},{4,0},{8,4},{12,8},{16,12},{20,16},{24,20},{28,24},{1,29},{... | collective-permute-start | bytes 1044488 | tf_op jit(solution)/shard_map/ppermute | solution.py:308
  37.5 7.8 %collective-permute-start.9 = (bf16[16,640]{1,0:T(8,128)(2,1)S(1)}, bf16[16,640]{1,0:T(8,128)(2,1)S(1)}, u32[]{:S(2)}, u32[]{:S(2)}) collective-permute-start(bf16[16,640]{1,0:T(8,128)(2,1)S(1)} %get-tuple-element.21), channel_id=1, source_target_pairs={{0,8},{4,12},{8,16},{12,20},{16,24},{20,28},{24,0},{28,4},{1,9},{5... | collective-permute-start | bytes 61448 | tf_op jit(solution)/shard_map/ppermute | solution.py:308
  45.2 1.7 %copy-start.5 = (bf16[272,640]{1,0:T(8,128)(2,1)}, bf16[272,640]{1,0:T(8,128)(2,1)S(1)}, u32[]{:S(2)}) copy-start(bf16[272,640]{1,0:T(8,128)(2,1)S(1)} %get-tuple-element.22.refs_3_.up_ref) | copy-start | bytes 1044484
  45.3 1.7 %copy-start.6 = (bf16[272,640]{1,0:T(8,128)(2,1)}, bf16[272,640]{1,0:T(8,128)(2,1)S(1)}, u32[]{:S(2)}) copy-start(bf16[272,640]{1,0:T(8,128)(2,1)S(1)} %get-tuple-element.23.refs_6_.down_ref) | copy-start | bytes 1044484
  45.3 8.7 %collective-permute-start.10 = (bf16[272,640]{1,0:T(8,128)(2,1)S(1)}, bf16[272,640]{1,0:T(8,128)(2,1)}, u32[]{:S(2)}, u32[]{:S(2)}) collective-permute-start(bf16[272,640]{1,0:T(8,128)(2,1)S(1)} %get-tuple-element.22.refs_3_.up_ref), channel_id=1, source_target_pairs={{0,4},{4,8},{8,12},{12,16},{16,20},{20,24},{24,28},{28,0},{1,5},{5... | collective-permute-start | bytes 1044488 | tf_op jit(solution)/shard_map/ppermute | solution.py:308
  46.9 23.9 %all-to-all-start.2 = ((bf16[8,128,640]{2,1,0:T(8,128)(2,1)}), bf16[8,128,640]{2,1,0:T(8,128)(2,1)}, u32[]{:S(2)}, u32[]{:S(2)}) async-start(bf16[8,128,640]{2,1,0:T(8,128)(2,1)} %shard_map.108), calls=%async_computation.2 | async-start | bytes 2621440 | tf_op jit(solution)/shard_map/all_to_all | solution.py:360
  70.8 21.3 %all-to-all-start.1 = ((bf16[8,656,128]{2,1,0:T(8,128)(2,1)}), bf16[8,656,128]{2,1,0:T(8,128)(2,1)}, u32[]{:S(2)}, u32[]{:S(2)}) async-start(bf16[8,656,128]{2,1,0:T(8,128)(2,1)} %shard_map.107), calls=%async_computation.1 | async-start | bytes 2686976 | tf_op jit(solution)/shard_map/all_to_all | solution.py:364
